TPU v7x, 512 devices: a whole 4x8x8 slice. The times are simulated.
512 devices in a mesh: tm: 64 (over z_lo, y, x), tile: 8 (over z_hi, core).
Axes of the slice: x: 4, y: 8, z: 8 (z_hi: 4, z_lo: 2; z = z_hi * 2 + z_lo), core: 2. Of those that a mesh axis runs over, the one named last changes fastest.
Arguments:
- latent: bfloat16 [256, 32, 160, 128], P('tm', 'tile'), may hold values from -6 to 6
- cot_forward: bfloat16 [256, 32, 160, 128], P('tm', 'tile'), may hold values from -6 to 6
- cot_reverse: bfloat16 [256, 32, 160, 128], P('tm', 'tile'), may hold values from -6 to 6
- spatial_weight: bfloat16 [3, 3, 128, 128], replicated, may hold values from -0.1875 to 0.1875
- temporal_weight: bfloat16 [3, 128, 128], replicated, may hold values from -0.3125 to 0.3125
Outputs:
- out_forward: bfloat16 [256, 32, 160, 128], P('tm', 'tile')
- out_reverse: bfloat16 [256, 32, 160, 128], P('tm', 'tile')
- grad_input: bfloat16 [256, 32, 160, 128], P('tm', 'tile')
- grad_spatial: float32 [3, 3, 128, 128], replicated
- grad_temporal: float32 [3, 128, 128], replicated
All inputs are finite; a program needn't handle non-finite values.
Results may differ from a plain program's by a relative error of at most 0.0032.
Values may be sent and summed in bfloat16 or wider, within the bound.
No kernel may reach another device: no remote copies, remote signals or barrier semaphores. Data moves between devices by JAX's collectives and lax.ppermute only.
A program may use at most 64 MiB of HBM per device.

v0:
```python
import math

import jax
import jax.numpy as jnp
from jax import lax
from jax.sharding import PartitionSpec as P


def extended_2(cells, sides, width):
    for axis, dim in sides:
        count = lax.axis_size(axis)
        ends = count - 1
        head = lax.slice_in_dim(cells, 0, width, axis=dim)
        tail = lax.slice_in_dim(cells, cells.shape[dim] - width, cells.shape[dim], axis=dim)
        cells = jnp.concatenate(
            [
                lax.ppermute(tail, axis, [(i, (i + 1) % count) for i in range(ends)]),
                cells,
                lax.ppermute(head, axis, [((i + 1) % count, i) for i in range(ends)]),
            ],
            axis=dim,
        )
    return cells


def shifted(value, axis, steps):
    count = lax.axis_size(axis)
    initial, last = (max(0, -steps), min(count, count - steps))
    return lax.ppermute(value, axis, [(source, source + steps) for source in range(initial, last)])


def side_by_side(arrays, axis, dim, along):
    both = jnp.concatenate(arrays, axis=along)
    whole, at, outs = (lax.psum_scatter(both, axis, scatter_dimension=dim, tiled=True), 0, [])
    for a in arrays:
        outs.append(lax.slice_in_dim(whole, at, at + a.shape[along], axis=along))
        at += a.shape[along]
    return tuple(outs)


def sent_to_all(shard, axis):
    size = lax.axis_size(axis)
    return lax.all_to_all(
        jnp.broadcast_to(shard[None], (size, *shard.shape)), axis, 0, 0, tiled=True
    )


def over_copies(shard, axis):
    return sent_to_all(shard, axis).sum(axis=0)


def in_one(arrays, axis):
    ends = [0]
    for a in arrays:
        ends.append(ends[-1] + a.size)
    total = over_copies(jnp.concatenate([a.ravel() for a in arrays]), axis)
    return tuple((total[b:e].reshape(a.shape) for a, b, e in zip(arrays, ends, ends[1:])))


def in_order(pieces, dim):
    dims = list(pieces.shape[1:])
    dims[dim] *= pieces.shape[0]
    return jnp.moveaxis(pieces, 0, dim).reshape(dims)


def gather_directly(shard, axis, dim):
    return in_order(sent_to_all(shard, axis), dim)


def sent_together(arrays, axis, dim, along):
    both = jnp.concatenate(arrays, axis=along)
    whole, at, outs = (gather_directly(both, axis, dim), 0, [])
    for a in arrays:
        outs.append(lax.slice_in_dim(whole, at, at + a.shape[along], axis=along))
        at += a.shape[along]
    return tuple(outs)


def spatial_rows(padded, height, width_cells, flipped):
    pieces = []
    for row_step in range(3):
        for col_step in range(3):
            row_from = 2 - row_step if flipped else row_step
            col_from = 2 - col_step if flipped else col_step
            pieces.append(
                padded[:, row_from : row_from + height, col_from : col_from + width_cells, :]
            )
    joined = jnp.concatenate(pieces, axis=3)
    return joined.reshape(-1, joined.shape[3])


def widen(values):
    return jnp.pad(values, ((0, 0), (0, 0), (1, 1), (0, 0)))


def temporal_rows(extended, offsets, frame_count):
    joined = jnp.concatenate(
        [extended[offset : offset + frame_count] for offset in offsets], axis=2
    )
    return joined.reshape(-1, joined.shape[2])


def contract_rows(left, right):
    return lax.dot_general(
        left, right, (((0,), (0,)), ((), ())), preferred_element_type=jnp.float32
    )


def body(latent, cot_forward, cot_reverse, spatial_weight, temporal_weight):
    frame_count, height, width_cells, channels = latent.shape
    plane_cells = height * width_cells
    spatial_flat = spatial_weight.reshape(9 * channels, channels)
    flipped_flat = jnp.transpose(spatial_weight, (0, 1, 3, 2)).reshape(9 * channels, channels)
    forward_flat = temporal_weight.reshape(3 * channels, channels)
    backward_flat = jnp.transpose(temporal_weight, (0, 2, 1)).reshape(3 * channels, channels)
    latent_flat = latent.reshape(-1, channels)
    fwd_cot = cot_forward.reshape(frame_count, plane_cells, channels)
    rev_cot = cot_reverse.reshape(frame_count, plane_cells, channels)
    rimmed = extended_2(latent, (("tile", 1),), 1)
    patches = spatial_rows(widen(rimmed), height, width_cells, False)
    pre_act = jnp.dot(patches, spatial_flat, preferred_element_type=jnp.float32)
    act_frames = (
        jax.nn.silu(pre_act).astype(jnp.bfloat16).reshape(frame_count, plane_cells, channels)
    )
    rimmed_act = extended_2(act_frames, (("tm", 0),), 2)
    following = shifted(fwd_cot[:2], "tm", -1)
    earlier = shifted(rev_cot[-2:], "tm", 1)
    causal = temporal_rows(rimmed_act, (2, 1, 0), frame_count)
    anticausal = temporal_rows(rimmed_act, (2, 3, 4), frame_count)
    residual_in = latent_flat.astype(jnp.float32)
    out_forward = (
        (residual_in + jnp.dot(causal, forward_flat, preferred_element_type=jnp.float32))
        .astype(jnp.bfloat16)
        .reshape(latent.shape)
    )
    out_reverse = (
        (residual_in + jnp.dot(anticausal, forward_flat, preferred_element_type=jnp.float32))
        .astype(jnp.bfloat16)
        .reshape(latent.shape)
    )
    ahead_rows = temporal_rows(
        jnp.concatenate([fwd_cot, following], axis=0), (0, 1, 2), frame_count
    )
    behind = temporal_rows(jnp.concatenate([earlier, rev_cot], axis=0), (2, 1, 0), frame_count)
    grad_act = jnp.dot(ahead_rows, backward_flat, preferred_element_type=jnp.float32)
    grad_act = grad_act + jnp.dot(behind, backward_flat, preferred_element_type=jnp.float32)
    grad_temp = contract_rows(causal, cot_forward.reshape(-1, channels))
    grad_temp = grad_temp + contract_rows(anticausal, cot_reverse.reshape(-1, channels))
    sigmoid_pre = jax.nn.sigmoid(pre_act)
    grad_pre = (grad_act * sigmoid_pre * (1.0 + pre_act * (1.0 - sigmoid_pre))).astype(jnp.bfloat16)
    grad_rim = extended_2(grad_pre.reshape(latent.shape), (("tile", 1),), 1)
    grad_patches = spatial_rows(widen(grad_rim), height, width_cells, True)
    total_in = cot_forward.reshape(-1, channels).astype(jnp.float32) + cot_reverse.reshape(
        -1, channels
    ).astype(jnp.float32)
    total_in = total_in + jnp.dot(grad_patches, flipped_flat, preferred_element_type=jnp.float32)
    grad_input = total_in.astype(jnp.bfloat16).reshape(latent.shape)
    grad_space = contract_rows(patches, grad_pre)
    share_space, share_temp = side_by_side((grad_space, grad_temp), "tile", 1, 0)
    share_space, share_temp = in_one((share_space, share_temp), "tm")
    grad_space, grad_temp = sent_together((share_space, share_temp), "tile", 1, 0)
    positions = frame_count * height * width_cells * lax.axis_size("tm") * lax.axis_size("tile")
    grad_scale = 1.0 / math.sqrt(positions)
    grad_spatial = (grad_space * grad_scale).reshape(3, 3, channels, channels)
    grad_temporal = (grad_temp * grad_scale).reshape(3, channels, channels)
    return (out_forward, out_reverse, grad_input, grad_spatial, grad_temporal)


def solution(mesh):
    placed = (
        P("tm", "tile", None, None),
        P("tm", "tile", None, None),
        P("tm", "tile", None, None),
        P(),
        P(),
    )
    return jax.shard_map(
        body,
        mesh=mesh,
        in_specs=placed,
        out_specs=(
            P("tm", "tile", None, None),
            P("tm", "tile", None, None),
            P("tm", "tile", None, None),
            P(),
            P(),
        ),
        check_vma=False,
    )
```

profile of v0, /device:TPU:48, one launch (start us, length us, event | category | flops | bytes accessed | tf_op | source)
XLA Modules:
  0.0 303.8 jit_solution(18115949144913530407)
XLA Ops:
  7.2 1.1 fusion.41
  8.3 1.7 collective-permute-start
  10.1 1.3 collective-permute-start.1
  11.4 1.7 slice.186
  13.1 3.4 %collective-permute-start.5 = (bf16[2,640,128]{2,1,0:T(8,128)(2,1)}, bf16[2,640,128]{2,1,0:T(8,128)(2,1)S(1)}, u32[]{:S(2)}, u32[]{:S(2)}) collective-permute-start(bf16[2,640,128]{2,1,0:T(8,128)(2,1)} %bitcast.22), channel_id=1, source_target_pairs={{0,8},{8,16},{16,24},{24,32},{32,40},{40,48},{48,56},{56,64},{64,7... | collective-permute-start | bytes 983048 | tf_op jit(solution)/shard_map/ppermute | solution.py:29
  16.5 1.0 slice.182
  17.5 4.6 %collective-permute-start.4 = (bf16[2,640,128]{2,1,0:T(8,128)(2,1)S(1)}, bf16[2,640,128]{2,1,0:T(8,128)(2,1)S(1)}, u32[]{:S(2)}, u32[]{:S(2)}) collective-permute-start(bf16[2,640,128]{2,1,0:T(8,128)(2,1)S(1)} %bitcast.98), channel_id=1, source_target_pairs={{8,0},{16,8},{24,16},{32,24},{40,32},{48,40},{56,48},{64,56},{72,6... | collective-permute-start | bytes 983048 | tf_op jit(solution)/shard_map/ppermute | solution.py:29
  22.0 1.0 copy.27
  23.1 1.4 select_maximum_fusion.2
  26.3 1.8 multiply_convert_fusion
  28.1 1.9 collective-permute-start.2
  30.0 6.0 %collective-permute-start.3 = (bf16[2,640,128]{2,1,0:T(8,128)(2,1)S(1)}, bf16[2,640,128]{2,1,0:T(8,128)(2,1)S(1)}, u32[]{:S(2)}, u32[]{:S(2)}) collective-permute-start(bf16[2,640,128]{2,1,0:T(8,128)(2,1)S(1)} %bitcast.96), channel_id=1, source_target_pairs={{8,0},{16,8},{24,16},{32,24},{40,32},{48,40},{56,48},{64,56},{72,6... | collective-permute-start | bytes 983048 | tf_op jit(solution)/shard_map/ppermute | solution.py:19
  36.2 0.7 fusion.9
  37.3 0.9 fusion.5
  38.2 1.7 fusion.42
  40.0 0.9 collective-permute-done.3
  41.1 0.7 fusion.21
  41.8 0.7 convolution_add_fusion.4
  42.7 1.2 copy.34
  43.9 53.9 %reduce-scatter.4.cloned.1.call-done = f32[16,1536]{1,0:T(8,128)} async-done(((f32[128,1536]{1,0:T(8,128)}), f32[16,1536]{1,0:T(8,128)}) %reduce-scatter.4.cloned.1.call-update) | async-done | bytes 98320
  97.8 0.7 slice.233
  98.5 0.9 slice.232
  100.2 4.3 %broadcast_in_dim.4 = f32[64,1,24576]{2,1,0:T(1,128)} broadcast(f32[24576]{0:T(1024)S(1)} %pad_maximum_fusion.11), dimensions={2} | broadcast | bytes 6389760 | tf_op jit(solution)/shard_map/broadcast_in_dim | solution.py:44
  104.4 10.5 %all-to-all-start = ((f32[64,1,24576]{2,1,0:T(1,128)}), f32[64,1,24576]{2,1,0:T(1,128)}, u32[]{:S(2)}, u32[]{:S(2)}) async-start(f32[64,1,24576]{2,1,0:T(1,128)} %broadcast_in_dim.4), calls=%async_computation | async-start | bytes 12582912 | tf_op jit(solution)/shard_map/all_to_all | solution.py:43
  114.9 1.3 collective-permute-start.6
  116.2 1.5 collective-permute-start.7
  117.7 0.9 copy.28
  118.6 0.9 collective-permute-done.7
  119.9 2.8 fusion.3
  122.7 0.6 fusion.38
  123.4 0.9 constant_dynamic-update-slice_fusion.9
  124.3 0.9 constant_dynamic-update-slice_fusion.8
  125.2 1.0 constant_dynamic-update-slice_fusion.7
  126.3 0.9 constant_dynamic-update-slice_fusion.6
  127.2 1.0 constant_dynamic-update-slice_fusion.5
  128.1 1.0 constant_dynamic-update-slice_fusion.4
  129.1 1.0 constant_dynamic-update-slice_fusion.3
  130.1 121.1 %all-to-all-done = f32[64,1,24576]{2,1,0:T(1,128)} async-done(((f32[64,1,24576]{2,1,0:T(1,128)}), f32[64,1,24576]{2,1,0:T(1,128)}, u32[]{:S(2)}, u32[]{:S(2)}) %all-to-all-start) | async-done | bytes 6291488 | tf_op jit(solution)/shard_map/all_to_all | solution.py:43
  251.2 8.6 %reduce_sum.9 = f32[24576]{0:T(1024)S(1)} reduce(f32[64,1,24576]{2,1,0:T(1,128)} %all-to-all-done, f32[]{:T(128)} %constant.2.clone.1), dimensions={0,1}, to_apply=%region_1.2 | reduce | flops 1548288 | bytes 6389764 | tf_op jit(solution)/shard_map/reduce_sum | solution.py:49
  260.4 1.0 broadcast_in_dim.5
  261.4 10.7 %all-to-all-start.1 = ((f32[8,1536,16]{1,2,0:T(8,128)}), f32[8,1536,16]{1,2,0:T(8,128)S(1)}, u32[]{:S(2)}, u32[]{:S(2)}) async-start(f32[8,1536,16]{1,2,0:T(8,128)} %broadcast_in_dim.5), calls=%async_computation.1 | async-start | bytes 1572864 | tf_op jit(solution)/shard_map/all_to_all | solution.py:43
  272.1 2.9 fusion.2
  275.0 0.9 constant_dynamic-update-slice_fusion.2
  275.9 0.9 constant_dynamic-update-slice_fusion.1
  276.9 5.2 %fusion.4 = bf16[2560,128]{1,0:T(8,128)(2,1)} fusion(bf16[2560,1152]{1,0:T(8,128)(2,1)} %constant_dynamic-update-slice_fusion.1, bf16[1152,128]{1,0:T(8,128)(2,1)S(1)} %bitcast.100, bf16[2560,128]{1,0:T(8,128)(2,1)S(1)} %bitcast.83, bf16[2560,128]{1,0:T(8,128)(2,1)S(1)} %bitcast.79), kind=kOutput, calls=%fused_computation.8 | convolution fusion | flops 756613120 | bytes 8159232 | tf_op jit(solution)/shard_map/dot_general | solution.py:156
  282.1 12.5 %all-to-all-done.1 = f32[8,1536,16]{1,2,0:T(8,128)S(1)} async-done(((f32[8,1536,16]{1,2,0:T(8,128)}), f32[8,1536,16]{1,2,0:T(8,128)S(1)}, u32[]{:S(2)}, u32[]{:S(2)}) %all-to-all-start.1) | async-done | bytes 786464 | tf_op jit(solution)/shard_map/all_to_all | solution.py:43
  294.8 0.8 copy.33
  295.8 1.1 copy.32
  (67 shorter events, 4.8 us)
Async XLA Ops:
  7.2 17.4 %copy-start = (bf16[4,4,160,128]{3,2,1,0:T(8,128)(2,1)S(1)}, bf16[4,4,160,128]{3,2,1,0:T(8,128)(2,1)}, u32[]{:S(2)}) copy-start(bf16[4,4,160,128]{3,2,1,0:T(8,128)(2,1)} %param.5) | copy-start | bytes 1966084
  7.2 90.6 %reduce-scatter.4.cloned.1.call-start = ((), (), s32[]{:S(2)}) async-start(), calls=%async_computation.3 | async-start | bytes 884736
  8.3 14.8 %collective-permute-start = (bf16[4,1,160,128]{3,2,1,0:T(8,128)(2,1)S(1)}, bf16[4,1,160,128]{3,2,1,0:T(8,128)(2,1)S(1)}, u32[]{:S(2)}, u32[]{:S(2)}) collective-permute-start(bf16[4,1,160,128]{3,2,1,0:T(8,128)(2,1)S(1)} %get-tuple-element.47), channel_id=1, source_target_pairs={{0,1},{1,2},{2,3},{3,4},{4,5},{5,6},{6,7},{8,9},{9,10},{10,11},{11... | collective-permute-start | bytes 491528 | tf_op jit(solution)/shard_map/ppermute | solution.py:17
  10.1 13.0 %collective-permute-start.1 = (bf16[4,1,160,128]{3,2,1,0:T(8,128)(2,1)S(1)}, bf16[4,1,160,128]{3,2,1,0:T(8,128)(2,1)S(1)}, u32[]{:S(2)}, u32[]{:S(2)}) collective-permute-start(bf16[4,1,160,128]{3,2,1,0:T(8,128)(2,1)S(1)} %get-tuple-element.48), channel_id=1, source_target_pairs={{1,0},{2,1},{3,2},{4,3},{5,4},{6,5},{7,6},{9,8},{10,9},{11,10},{12... | collective-permute-start | bytes 491528 | tf_op jit(solution)/shard_map/ppermute | solution.py:19
  13.1 23.8 %collective-permute-start.5 = (bf16[2,640,128]{2,1,0:T(8,128)(2,1)}, bf16[2,640,128]{2,1,0:T(8,128)(2,1)S(1)}, u32[]{:S(2)}, u32[]{:S(2)}) collective-permute-start(bf16[2,640,128]{2,1,0:T(8,128)(2,1)} %bitcast.22), channel_id=1, source_target_pairs={{0,8},{8,16},{16,24},{24,32},{32,40},{40,48},{48,56},{56,64},{64,7... | collective-permute-start | bytes 983048 | tf_op jit(solution)/shard_map/ppermute | solution.py:29
  17.5 18.6 %collective-permute-start.4 = (bf16[2,640,128]{2,1,0:T(8,128)(2,1)S(1)}, bf16[2,640,128]{2,1,0:T(8,128)(2,1)S(1)}, u32[]{:S(2)}, u32[]{:S(2)}) collective-permute-start(bf16[2,640,128]{2,1,0:T(8,128)(2,1)S(1)} %bitcast.98), channel_id=1, source_target_pairs={{8,0},{16,8},{24,16},{32,24},{40,32},{48,40},{56,48},{64,56},{72,6... | collective-permute-start | bytes 983048 | tf_op jit(solution)/shard_map/ppermute | solution.py:29
  25.0 1.2 copy-start.9
  26.3 9.8 %copy-start.1 = (bf16[4,4,160,128]{3,2,1,0:T(8,128)(2,1)S(1)}, bf16[4,4,160,128]{3,2,1,0:T(8,128)(2,1)}, u32[]{:S(2)}) copy-start(bf16[4,4,160,128]{3,2,1,0:T(8,128)(2,1)} %param.6) | copy-start | bytes 1966084
  28.1 11.8 %collective-permute-start.2 = (bf16[2,640,128]{2,1,0:T(8,128)(2,1)S(1)}, bf16[2,640,128]{2,1,0:T(8,128)(2,1)S(1)}, u32[]{:S(2)}, u32[]{:S(2)}) collective-permute-start(bf16[2,640,128]{2,1,0:T(8,128)(2,1)S(1)} %bitcast.97), channel_id=1, source_target_pairs={{0,8},{8,16},{16,24},{24,32},{32,40},{40,48},{48,56},{56,64},{64,7... | collective-permute-start | bytes 983048 | tf_op jit(solution)/shard_map/ppermute | solution.py:17
  30.0 10.8 %collective-permute-start.3 = (bf16[2,640,128]{2,1,0:T(8,128)(2,1)S(1)}, bf16[2,640,128]{2,1,0:T(8,128)(2,1)S(1)}, u32[]{:S(2)}, u32[]{:S(2)}) collective-permute-start(bf16[2,640,128]{2,1,0:T(8,128)(2,1)S(1)} %bitcast.96), channel_id=1, source_target_pairs={{8,0},{16,8},{24,16},{32,24},{40,32},{48,40},{56,48},{64,56},{72,6... | collective-permute-start | bytes 983048 | tf_op jit(solution)/shard_map/ppermute | solution.py:19
  36.1 1.1 copy-start.3
  41.1 1.5 copy-start.5
  41.1 1.5 copy-start.6
  41.1 1.5 copy-start.7
  41.1 1.5 copy-start.8
  104.4 13.3 %copy-start.10 = (bf16[3,3,128,128]{3,2,1,0:T(8,128)(2,1)S(1)}, bf16[3,3,128,128]{3,2,1,0:T(8,128)(2,1)}, u32[]{:S(2)}) copy-start(bf16[3,3,128,128]{3,2,1,0:T(8,128)(2,1)} %param.8) | copy-start | bytes 884740
  104.4 146.7 %all-to-all-start = ((f32[64,1,24576]{2,1,0:T(1,128)}), f32[64,1,24576]{2,1,0:T(1,128)}, u32[]{:S(2)}, u32[]{:S(2)}) async-start(f32[64,1,24576]{2,1,0:T(1,128)} %broadcast_in_dim.4), calls=%async_computation | async-start | bytes 12582912 | tf_op jit(solution)/shard_map/all_to_all | solution.py:43
  114.9 5.0 %copy-start.12 = (bf16[3,128,128]{2,1,0:T(8,128)(2,1)S(1)}, bf16[3,128,128]{2,1,0:T(8,128)(2,1)}, u32[]{:S(2)}) copy-start(bf16[3,128,128]{2,1,0:T(8,128)(2,1)} %param.9) | copy-start | bytes 294916
  114.9 3.7 %collective-permute-start.6 = (bf16[4,1,160,128]{3,2,1,0:T(8,128)(2,1)S(1)}, bf16[4,1,160,128]{3,2,1,0:T(8,128)(2,1)S(1)}, u32[]{:S(2)}, u32[]{:S(2)}) collective-permute-start(bf16[4,1,160,128]{3,2,1,0:T(8,128)(2,1)S(1)} %get-tuple-element.41), channel_id=1, source_target_pairs={{0,1},{1,2},{2,3},{3,4},{4,5},{5,6},{6,7},{8,9},{9,10},{10,11},{11... | collective-permute-start | bytes 491528 | tf_op jit(solution)/shard_map/ppermute | solution.py:17
  116.2 3.3 %collective-permute-start.7 = (bf16[4,1,160,128]{3,2,1,0:T(8,128)(2,1)S(1)}, bf16[4,1,160,128]{3,2,1,0:T(8,128)(2,1)S(1)}, u32[]{:S(2)}, u32[]{:S(2)}) collective-permute-start(bf16[4,1,160,128]{3,2,1,0:T(8,128)(2,1)S(1)} %get-tuple-element.42), channel_id=1, source_target_pairs={{1,0},{2,1},{3,2},{4,3},{5,4},{6,5},{7,6},{9,8},{10,9},{11,10},{12... | collective-permute-start | bytes 491528 | tf_op jit(solution)/shard_map/ppermute | solution.py:19
  261.4 33.2 %all-to-all-start.1 = ((f32[8,1536,16]{1,2,0:T(8,128)}), f32[8,1536,16]{1,2,0:T(8,128)S(1)}, u32[]{:S(2)}, u32[]{:S(2)}) async-start(f32[8,1536,16]{1,2,0:T(8,128)} %broadcast_in_dim.5), calls=%async_computation.1 | async-start | bytes 1572864 | tf_op jit(solution)/shard_map/all_to_all | solution.py:43
  272.0 4.8 %copy-start.2 = (bf16[4,4,160,128]{3,2,1,0:T(8,128)(2,1)S(1)}, bf16[4,4,160,128]{3,2,1,0:T(8,128)(2,1)}, u32[]{:S(2)}) copy-start(bf16[4,4,160,128]{3,2,1,0:T(8,128)(2,1)} %param.6) | copy-start | bytes 1966084
  272.0 4.8 %copy-start.4 = (bf16[4,4,160,128]{3,2,1,0:T(8,128)(2,1)S(1)}, bf16[4,4,160,128]{3,2,1,0:T(8,128)(2,1)}, u32[]{:S(2)}) copy-start(bf16[4,4,160,128]{3,2,1,0:T(8,128)(2,1)} %param.7) | copy-start | bytes 1966084
  272.1 4.8 %copy-start.11 = (bf16[3,3,128,128]{2,3,1,0:T(8,128)(2,1)S(1)}, bf16[3,3,128,128]{2,3,1,0:T(8,128)(2,1)}, u32[]{:S(2)}) copy-start(bf16[3,3,128,128]{2,3,1,0:T(8,128)(2,1)} %copy.28) | copy-start | bytes 884740
Sparse Core Ops, SparseCore 0:
  44.0 53.7 reduce-scatter.3
where the time goes:
time: 305 us; the launch traced here: 304 us
  waiting for transfers between devices  189 us (62%)
  starting transfers between devices  42.9 us (14%)
  local copies, waits for them, and re-layouts  28.3 us (9%)
  matrix products  17.5 us (6%)
  between operations  14.6 us (5%)
  other arithmetic  11.3 us (4%)
    all_to_all x2, waiting for transfers between devices, sent_to_all(): lax.all_to_all(jnp.broadcast_to(shard[None], (size, *shard.shape)), axis,...  134 us
    unnamed x2, waiting for transfers between devices  54 us
    all_to_all x2, starting transfers between devices, sent_to_all(): lax.all_to_all(jnp.broadcast_to(shard[None], (size, *shard.shape)), axis,...  21.1 us
    unnamed x47, local copies, waits for them, and re-layouts  14.5 us
    ppermute x3, starting transfers between devices, extended_2(): lax.ppermute(head, axis, [((i + 1) % count, i) for i in range(ends)])  8.8 us
    reduce_sum x1, other arithmetic, over_copies(): return sent_to_all(shard, axis).sum(axis=0)  8.58 us
    ppermute x2, starting transfers between devices, shifted(): lax.ppermute(value, axis, [(source, source + steps) for source in range(i...  7.94 us
  transfers between devices with their start and end apart: 11, of which 5 were waited for; matrix products, arithmetic and copies ran while one was open for 11% of the time, Pallas kernels for 0%

commit v1 on v0

v1 whole, which is shorter than its diff:
```python
import math

import jax
import jax.numpy as jnp
from jax import lax
from jax.sharding import PartitionSpec as P

BOTH = ("tm", "tile")


def groups(bits):
    rest = [b for b in range(9) if b not in bits]
    out = []
    for r in range(1 << len(rest)):
        base = sum(((r >> i) & 1) << b for i, b in enumerate(rest))
        members = []
        for k in range(1 << len(bits)):
            members.append(base + sum(((k >> i) & 1) << b for i, b in enumerate(reversed(bits))))
        out.append(members)
    return out


NEAR = groups([8, 5, 4, 3, 0])
FAR = groups([7, 6, 2, 1])


def exchange(pieces, members):
    return lax.all_to_all(pieces, BOTH, 0, 0, tiled=True, axis_index_groups=members)


def to_all(shard, members):
    return exchange(jnp.broadcast_to(shard[None], (len(members[0]), *shard.shape)), members)


def total_over_mesh(partial):
    rows, channels = partial.shape
    near = len(NEAR[0])
    pieces = partial.astype(jnp.bfloat16).reshape(near, rows // near, channels)
    share = exchange(pieces, NEAR).astype(jnp.float32).sum(axis=0)
    share = to_all(share.astype(jnp.bfloat16), FAR).astype(jnp.float32).sum(axis=0)
    whole = to_all(share.astype(jnp.bfloat16), NEAR)
    return whole.reshape(rows, channels).astype(jnp.float32)


def shifted(value, axis, steps):
    count = lax.axis_size(axis)
    initial, last = (max(0, -steps), min(count, count - steps))
    return lax.ppermute(value, axis, [(source, source + steps) for source in range(initial, last)])


def rim(cells, axis, dim, width):
    head = lax.slice_in_dim(cells, 0, width, axis=dim)
    tail = lax.slice_in_dim(cells, cells.shape[dim] - width, cells.shape[dim], axis=dim)
    return jnp.concatenate([shifted(tail, axis, 1), cells, shifted(head, axis, -1)], axis=dim)


def spatial_rows(padded, height, width_cells, flipped):
    pieces = []
    for row_step in range(3):
        for col_step in range(3):
            row_from = 2 - row_step if flipped else row_step
            col_from = 2 - col_step if flipped else col_step
            pieces.append(
                padded[:, row_from : row_from + height, col_from : col_from + width_cells, :]
            )
    joined = jnp.concatenate(pieces, axis=3)
    return joined.reshape(-1, joined.shape[3])


def widen(values):
    return jnp.pad(values, ((0, 0), (0, 0), (1, 1), (0, 0)))


def temporal_rows(extended, offsets, frame_count):
    joined = jnp.concatenate(
        [extended[offset : offset + frame_count] for offset in offsets], axis=2
    )
    return joined.reshape(-1, joined.shape[2])


def contract_rows(left, right):
    return lax.dot_general(
        left, right, (((0,), (0,)), ((), ())), preferred_element_type=jnp.float32
    )


def body(latent, cot_forward, cot_reverse, spatial_weight, temporal_weight):
    frame_count, height, width_cells, channels = latent.shape
    plane_cells = height * width_cells
    spatial_flat = spatial_weight.reshape(9 * channels, channels)
    flipped_flat = jnp.transpose(spatial_weight, (0, 1, 3, 2)).reshape(9 * channels, channels)
    forward_flat = temporal_weight.reshape(3 * channels, channels)
    backward_flat = jnp.transpose(temporal_weight, (0, 2, 1)).reshape(3 * channels, channels)
    latent_flat = latent.reshape(-1, channels)
    fwd_cot = cot_forward.reshape(frame_count, plane_cells, channels)
    rev_cot = cot_reverse.reshape(frame_count, plane_cells, channels)
    following = shifted(fwd_cot[:2], "tm", -1)
    earlier = shifted(rev_cot[-2:], "tm", 1)
    rimmed = rim(latent, "tile", 1, 1)
    patches = spatial_rows(widen(rimmed), height, width_cells, False)
    pre_act = jnp.dot(patches, spatial_flat, preferred_element_type=jnp.float32)
    act_flat = jax.nn.silu(pre_act).astype(jnp.bfloat16)
    act_frames = act_flat.reshape(frame_count, plane_cells, channels)
    ahead = temporal_rows(jnp.concatenate([fwd_cot, following], axis=0), (0, 1, 2), frame_count)
    behind = temporal_rows(jnp.concatenate([earlier, rev_cot], axis=0), (2, 1, 0), frame_count)
    grad_act = jnp.dot(ahead, backward_flat, preferred_element_type=jnp.float32)
    grad_act = grad_act + jnp.dot(behind, backward_flat, preferred_element_type=jnp.float32)
    grad_temp = contract_rows(ahead, act_flat) + contract_rows(behind, act_flat)
    grad_temp = jnp.transpose(grad_temp.reshape(3, channels, channels), (0, 2, 1))
    sigmoid_pre = jax.nn.sigmoid(pre_act)
    grad_pre = (grad_act * sigmoid_pre * (1.0 + pre_act * (1.0 - sigmoid_pre))).astype(jnp.bfloat16)
    grad_space = contract_rows(patches, grad_pre)
    partial = jnp.concatenate([grad_space, grad_temp.reshape(3 * channels, channels)], axis=0)
    whole = total_over_mesh(partial)

    rimmed_act = rim(act_frames, "tm", 0, 2)
    causal = temporal_rows(rimmed_act, (2, 1, 0), frame_count)
    anticausal = temporal_rows(rimmed_act, (2, 3, 4), frame_count)
    residual_in = latent_flat.astype(jnp.float32)
    out_forward = (
        (residual_in + jnp.dot(causal, forward_flat, preferred_element_type=jnp.float32))
        .astype(jnp.bfloat16)
        .reshape(latent.shape)
    )
    out_reverse = (
        (residual_in + jnp.dot(anticausal, forward_flat, preferred_element_type=jnp.float32))
        .astype(jnp.bfloat16)
        .reshape(latent.shape)
    )
    grad_rim = rim(grad_pre.reshape(latent.shape), "tile", 1, 1)
    grad_patches = spatial_rows(widen(grad_rim), height, width_cells, True)
    total_in = cot_forward.reshape(-1, channels).astype(jnp.float32) + cot_reverse.reshape(
        -1, channels
    ).astype(jnp.float32)
    total_in = total_in + jnp.dot(grad_patches, flipped_flat, preferred_element_type=jnp.float32)
    grad_input = total_in.astype(jnp.bfloat16).reshape(latent.shape)
    positions = frame_count * height * width_cells * lax.axis_size("tm") * lax.axis_size("tile")
    whole = whole * (1.0 / math.sqrt(positions))
    grad_spatial = whole[: 9 * channels].reshape(3, 3, channels, channels)
    grad_temporal = whole[9 * channels :].reshape(3, channels, channels)
    return (out_forward, out_reverse, grad_input, grad_spatial, grad_temporal)


def solution(mesh):
    cells = P("tm", "tile", None, None)
    return jax.shard_map(
        body,
        mesh=mesh,
        in_specs=(cells, cells, cells, P(), P()),
        out_specs=(cells, cells, cells, P(), P()),
        check_vma=False,
    )
```

time: 305 us -> 131 us (0.43)
  the two profiles are of different devices: /device:TPU:48 before, /device:TPU:1 now
where the time goes in v1:
time: 131 us; the launch traced here: 130 us
  starting transfers between devices  62.6 us (48%)
  local copies, waits for them, and re-layouts  24.6 us (19%)
  matrix products  21.8 us (17%)
  waiting for transfers between devices  10.4 us (8%)
  other arithmetic  9.24 us (7%)
    all_to_all x3, starting transfers between devices, exchange(): lax.all_to_all(pieces, BOTH, 0, 0, tiled=True, axis_index_groups=members)  35.8 us
    ppermute x8, starting transfers between devices, shifted(): lax.ppermute(value, axis, [(source, source + steps) for source in range(i...  26.8 us
    unnamed x44, local copies, waits for them, and re-layouts  14 us
    all_to_all x3, waiting for transfers between devices, exchange(): lax.all_to_all(pieces, BOTH, 0, 0, tiled=True, axis_index_groups=members)  10.4 us
    dot_general x1, matrix products, body(): jnp.dot(grad_patches, flipped_flat, preferred_element_type=jnp.float32)  5.22 us
    dot_general x3, matrix products, contract_rows(): lax.dot_general(left, right, (((0,), (0,)), ((), ())), preferred_element_...  5.1 us
    concatenate x4, other arithmetic, rim(): jnp.concatenate([shifted(tail, axis, 1), cells, shifted(head, axis, -1)],...  4.55 us
    dot_general x1, matrix products, body(): pre_act = jnp.dot(patches, spatial_flat, preferred_element_type=jnp.float32)  2.86 us
  transfers between devices with their start and end apart: 11, of which 2 were waited for; matrix products, arithmetic and copies ran while one was open for 38% of the time, Pallas kernels for 0%

profile of v1, /device:TPU:1, one launch (start us, length us, event | category | flops | bytes accessed | tf_op | source)
XLA Modules:
  0.0 129.8 jit_solution(11936321890226635868)
XLA Ops:
  0.6 1.1 fusion.34
  1.7 7.2 %collective-permute-start = (bf16[4,1,160,128]{3,2,1,0:T(8,128)(2,1)S(1)}, bf16[4,1,160,128]{3,2,1,0:T(8,128)(2,1)S(1)}, u32[]{:S(2)}, u32[]{:S(2)}) collective-permute-start(bf16[4,1,160,128]{3,2,1,0:T(8,128)(2,1)S(1)} %get-tuple-element.27), channel_id=1, source_target_pairs={{0,1},{1,2},{2,3},{3,4},{4,5},{5,6},{6,7},{8,9},{9,10},{10,11},{11... | collective-permute-start | bytes 491528 | tf_op jit(solution)/shard_map/ppermute | solution.py:48
  8.9 2.9 %collective-permute-start.1 = (bf16[4,1,160,128]{3,2,1,0:T(8,128)(2,1)S(1)}, bf16[4,1,160,128]{3,2,1,0:T(8,128)(2,1)S(1)}, u32[]{:S(2)}, u32[]{:S(2)}) collective-permute-start(bf16[4,1,160,128]{3,2,1,0:T(8,128)(2,1)S(1)} %get-tuple-element.28), channel_id=1, source_target_pairs={{1,0},{2,1},{3,2},{4,3},{5,4},{6,5},{7,6},{9,8},{10,9},{11,10},{12... | collective-permute-start | bytes 491528 | tf_op jit(solution)/shard_map/ppermute | solution.py:48
  11.8 1.0 slice.154
  12.8 2.2 %collective-permute-start.5 = (bf16[2,640,128]{2,1,0:T(8,128)(2,1)S(1)}, bf16[2,640,128]{2,1,0:T(8,128)(2,1)S(1)}, u32[]{:S(2)}, u32[]{:S(2)}) collective-permute-start(bf16[2,640,128]{2,1,0:T(8,128)(2,1)S(1)} %bitcast.91), channel_id=1, source_target_pairs={{0,8},{8,16},{16,24},{24,32},{32,40},{40,48},{48,56},{56,64},{64,7... | collective-permute-start | bytes 983048 | tf_op jit(solution)/shard_map/ppermute | solution.py:48
  15.0 1.7 %slice.150 = bf16[2,4,160,128]{3,2,1,0:T(8,128)(2,1)} slice(bf16[4,4,160,128]{3,2,1,0:T(8,128)(2,1)} %param.6), slice={[0:2], [0:4], [0:160], [0:128]} | slice | bytes 655360 | tf_op jit(solution)/shard_map/slice | solution.py:97
  16.7 1.3 collective-permute-start.4
  18.0 1.0 copy.14
  19.0 1.9 %copy.15 = bf16[3,3,128,128]{2,3,1,0:T(8,128)(2,1)} copy(bf16[3,3,128,128]{3,2,1,0:T(8,128)(2,1)} %param.8) | data formatting | bytes 589824 | tf_op args[3]
  20.9 1.4 %select_maximum_fusion.2 = bf16[4,6,162,128]{3,2,1,0:T(8,128)(2,1)S(1)} fusion(bf16[4,1,160,128]{3,2,1,0:T(8,128)(2,1)S(1)} %collective-permute-done.1, bf16[4,4,160,128]{3,2,1,0:T(8,128)(2,1)} %param.5, bf16[4,1,160,128]{3,2,1,0:T(8,128)(2,1)S(1)} %collective-permute-done), kind=kLoop, calls=%fused_computation.30 | loop fusion | flops 5971968 | bytes 1978368 | tf_op jit(solution)/shard_map/concatenate | solution.py:54
  24.1 2.9 %multiply_convert_fusion = (bf16[2560,128]{1,0:T(8,128)(2,1)S(1)}, f32[2560,128]{1,0:T(8,128)}) fusion(bf16[2560,1152]{1,0:T(8,128)(2,1)S(1)} %bitcast.100, bf16[1152,128]{1,0:T(8,128)(2,1)S(1)} %bitcast.92), kind=kOutput, calls=%fused_computation.24 | convolution fusion | flops 756613120 | bytes 8159232 | tf_op jit(solution)/shard_map/dot_general | solution.py:101
  27.0 0.9 fusion.33
  27.9 4.7 %collective-permute-start.2 = (bf16[2,640,128]{2,1,0:T(8,128)(2,1)}, bf16[2,640,128]{2,1,0:T(8,128)(2,1)}, u32[]{:S(2)}, u32[]{:S(2)}) collective-permute-start(bf16[2,640,128]{2,1,0:T(8,128)(2,1)} %bitcast.3), channel_id=1, source_target_pairs={{0,8},{8,16},{16,24},{24,32},{32,40},{40,48},{48,56},{56,64},{64,7... | collective-permute-start | bytes 983048 | tf_op jit(solution)/shard_map/ppermute | solution.py:48
  32.6 1.3 collective-permute-start.3
  33.9 0.7 copy-done.7
  34.7 1.2 fusion.19
  35.9 0.8 copy-done.5
  36.7 0.7 fusion.17
  37.4 2.2 %fusion.20 = (bf16[4,640,128]{2,1,0:T(8,128)(2,1)}, bf16[4,640,128]{2,1,0:T(8,128)(2,1)}) fusion(bf16[4,640,128]{2,1,0:T(8,128)(2,1)S(1)} %bitcast.73, bf16[2,640,128]{2,1,0:T(8,128)(2,1)} %collective-permute-done.4), kind=kLoop, calls=%fused_computation.45 | loop fusion | flops 655360 | bytes 2293760 | tf_op jit(solution)/shard_map/concatenate | solution.py:104
  39.7 2.6 %fusion.15 = bf16[384,128]{1,0:T(8,128)(2,1)} fusion(f32[384,128]{1,0:T(8,128)S(1)} %fusion.17, bf16[2560,128]{1,0:T(8,128)(2,1)S(1)} %get-tuple-element.29, bf16[2560,128]{1,0:T(8,128)(2,1)} %bitcast.19, bf16[2560,128]{1,0:T(8,128)(2,1)} %bitcast.18, bf16[2560,128]{1,0:T(8,128)(2,1)S(1)} %bitcast.74), kind=kOutput, calls=%fused_computation.27 | convolution fusion | flops 257654784 | bytes 2916352 | tf_op jit(solution)/shard_map/dot_general | solution.py:82
  42.3 1.0 copy.16
  43.3 2.1 %fusion.18 = f32[2560,128]{1,0:T(8,128)S(1)} fusion(bf16[384,128]{1,0:T(8,128)(2,1)S(1)} %bitcast.97, bf16[2560,128]{1,0:T(8,128)(2,1)} %bitcast.19, bf16[2560,128]{1,0:T(8,128)(2,1)} %bitcast.18, bf16[2560,128]{1,0:T(8,128)(2,1)S(1)} %bitcast.75), kind=kOutput, calls=%fused_computation.42 | convolution fusion | flops 257556480 | bytes 3375104 | tf_op jit(solution)/shard_map/dot_general | solution.py:106
  45.5 0.9 fusion.5
  47.2 1.8 %convolution_convert_fusion = bf16[1152,128]{1,0:T(8,128)(2,1)S(1)} fusion(bf16[2560,1152]{1,0:T(8,128)(2,1)S(1)} %bitcast.103, bf16[2560,128]{1,0:T(8,128)(2,1)S(1)} %fusion.5), kind=kOutput, calls=%fused_computation.12 | convolution fusion | flops 755122176 | bytes 6848512 | tf_op jit(solution)/shard_map/dot_general | solution.py:82
  49.0 5.4 %collective-permute-start.6 = (bf16[4,1,160,128]{3,2,1,0:T(8,128)(2,1)S(1)}, bf16[4,1,160,128]{3,2,1,0:T(8,128)(2,1)S(1)}, u32[]{:S(2)}, u32[]{:S(2)}) collective-permute-start(bf16[4,1,160,128]{3,2,1,0:T(8,128)(2,1)S(1)} %get-tuple-element.21), channel_id=1, source_target_pairs={{0,1},{1,2},{2,3},{3,4},{4,5},{5,6},{6,7},{8,9},{9,10},{10,11},{11... | collective-permute-start | bytes 491528 | tf_op jit(solution)/shard_map/ppermute | solution.py:48
  54.4 1.9 %collective-permute-start.7 = (bf16[4,1,160,128]{3,2,1,0:T(8,128)(2,1)S(1)}, bf16[4,1,160,128]{3,2,1,0:T(8,128)(2,1)S(1)}, u32[]{:S(2)}, u32[]{:S(2)}) collective-permute-start(bf16[4,1,160,128]{3,2,1,0:T(8,128)(2,1)S(1)} %get-tuple-element.22), channel_id=1, source_target_pairs={{1,0},{2,1},{3,2},{4,3},{5,4},{6,5},{7,6},{9,8},{10,9},{11,10},{12... | collective-permute-start | bytes 491528 | tf_op jit(solution)/shard_map/ppermute | solution.py:48
  56.3 0.8 pad_maximum_fusion.16
  57.1 12.8 %all-to-all-start = ((bf16[32,48,128]{2,1,0:T(8,128)(2,1)}), bf16[32,48,128]{2,1,0:T(8,128)(2,1)S(1)}, u32[]{:S(2)}, u32[]{:S(2)}) async-start(bf16[32,48,128]{2,1,0:T(8,128)(2,1)} %bitcast.42), calls=%async_computation | async-start | bytes 786432 | tf_op jit(solution)/shard_map/all_to_all | solution.py:28
  70.8 0.9 constant_dynamic-update-slice_fusion.9
  71.9 0.9 constant_dynamic-update-slice_fusion.8
  72.8 1.0 constant_dynamic-update-slice_fusion.7
  73.8 0.9 constant_dynamic-update-slice_fusion.6
  74.7 0.9 constant_dynamic-update-slice_fusion.5
  75.7 1.0 constant_dynamic-update-slice_fusion.4
  76.7 2.8 %fusion.21 = (bf16[4,640,128]{2,1,0:T(8,128)(2,1)}, bf16[4,640,128]{2,1,0:T(8,128)(2,1)}, bf16[4,640,128]{2,1,0:T(8,128)(2,1)}, bf16[4,640,128]{2,1,0:T(8,128)(2,1)}) fusion(bf16[4,640,128]{2,1,0:T(8,128)(2,1)S(1)} %bitcast.66, bf16[2,640,128]{2,1,0:T(8,128)(2,1)} %collective-permute-done.3, bf16[2,640,128]{2,1,0:T(8,128)(2,1)} %collective-permute-done.2), kind=kLoop, calls=%fused_computation.46 | loop fusion | flops 1310720 | bytes 3932160 | tf_op jit(solution)/shard_map/concatenate | solution.py:54
  79.4 0.9 constant_dynamic-update-slice_fusion.3
  80.4 0.9 constant_dynamic-update-slice_fusion.2
  81.4 0.7 broadcast_in_dim.4
  82.1 15.3 %all-to-all-start.1 = ((bf16[16,48,128]{2,1,0:T(8,128)(2,1)}), bf16[16,48,128]{2,1,0:T(8,128)(2,1)S(1)}, u32[]{:S(2)}, u32[]{:S(2)}) async-start(bf16[16,48,128]{2,1,0:T(8,128)(2,1)} %broadcast_in_dim.4), calls=%async_computation.1 | async-start | bytes 393216 | tf_op jit(solution)/shard_map/all_to_all | solution.py:28
  97.4 2.8 %fusion.3 = bf16[2560,128]{1,0:T(8,128)(2,1)} fusion(bf16[384,128]{1,0:T(8,128)(2,1)S(1)} %bitcast.95, bf16[2560,128]{1,0:T(8,128)(2,1)S(1)} %get-tuple-element.29, bf16[2560,128]{1,0:T(8,128)(2,1)} %bitcast.88, bf16[2560,128]{1,0:T(8,128)(2,1)} %bitcast.87, bf16[2560,128]{1,0:T(8,128)(2,1)S(1)} %bitcast.59), kind=kOutput, calls=%fused_computation.7 | convolution fusion | flops 258539520 | bytes 3375104 | tf_op jit(solution)/shard_map/dot_general | solution.py:126
  100.2 0.9 constant_dynamic-update-slice_fusion.1
  101.1 8.6 %all-to-all-done.1 = bf16[16,48,128]{2,1,0:T(8,128)(2,1)S(1)} async-done(((bf16[16,48,128]{2,1,0:T(8,128)(2,1)}), bf16[16,48,128]{2,1,0:T(8,128)(2,1)S(1)}, u32[]{:S(2)}, u32[]{:S(2)}) %all-to-all-start.1) | async-done | bytes 196640 | tf_op jit(solution)/shard_map/all_to_all | solution.py:28
  109.8 0.8 broadcast_in_dim.5
  110.6 7.7 %all-to-all-start.2 = ((bf16[32,48,128]{2,1,0:T(8,128)(2,1)}), bf16[32,48,128]{2,1,0:T(8,128)(2,1)S(1)}, u32[]{:S(2)}, u32[]{:S(2)}) async-start(bf16[32,48,128]{2,1,0:T(8,128)(2,1)} %broadcast_in_dim.5), calls=%async_computation.2 | async-start | bytes 786432 | tf_op jit(solution)/shard_map/all_to_all | solution.py:28
  118.3 2.8 %fusion.2 = bf16[2560,128]{1,0:T(8,128)(2,1)} fusion(bf16[384,128]{1,0:T(8,128)(2,1)S(1)} %bitcast.96, bf16[2560,128]{1,0:T(8,128)(2,1)S(1)} %get-tuple-element.29, bf16[2560,128]{1,0:T(8,128)(2,1)} %bitcast.85, bf16[2560,128]{1,0:T(8,128)(2,1)} %bitcast.86, bf16[2560,128]{1,0:T(8,128)(2,1)S(1)} %bitcast.60), kind=kOutput, calls=%fused_computation.6 | convolution fusion | flops 258539520 | bytes 3375104 | tf_op jit(solution)/shard_map/dot_general | solution.py:121
  121.1 5.2 %fusion.4 = bf16[2560,128]{1,0:T(8,128)(2,1)} fusion(bf16[2560,1152]{1,0:T(8,128)(2,1)} %constant_dynamic-update-slice_fusion.1, bf16[1152,128]{1,0:T(8,128)(2,1)} %bitcast.93, bf16[2560,128]{1,0:T(8,128)(2,1)S(1)} %bitcast.80, bf16[2560,128]{1,0:T(8,128)(2,1)S(1)} %bitcast.76), kind=kOutput, calls=%fused_computation.8 | convolution fusion | flops 756613120 | bytes 8159232 | tf_op jit(solution)/shard_map/dot_general | solution.py:135
  126.3 1.8 %all-to-all-done.2 = bf16[32,48,128]{2,1,0:T(8,128)(2,1)S(1)} async-done(((bf16[32,48,128]{2,1,0:T(8,128)(2,1)}), bf16[32,48,128]{2,1,0:T(8,128)(2,1)S(1)}, u32[]{:S(2)}, u32[]{:S(2)}) %all-to-all-start.2) | async-done | bytes 393248 | tf_op jit(solution)/shard_map/all_to_all | solution.py:28
  128.2 0.9 slice.194
  (53 shorter events, 4.5 us)
Async XLA Ops:
  0.6 21.8 %copy-start = (bf16[4,4,160,128]{3,2,1,0:T(8,128)(2,1)S(1)}, bf16[4,4,160,128]{3,2,1,0:T(8,128)(2,1)}, u32[]{:S(2)}) copy-start(bf16[4,4,160,128]{3,2,1,0:T(8,128)(2,1)} %param.5) | copy-start | bytes 1966084
  1.7 19.2 %collective-permute-start = (bf16[4,1,160,128]{3,2,1,0:T(8,128)(2,1)S(1)}, bf16[4,1,160,128]{3,2,1,0:T(8,128)(2,1)S(1)}, u32[]{:S(2)}, u32[]{:S(2)}) collective-permute-start(bf16[4,1,160,128]{3,2,1,0:T(8,128)(2,1)S(1)} %get-tuple-element.27), channel_id=1, source_target_pairs={{0,1},{1,2},{2,3},{3,4},{4,5},{5,6},{6,7},{8,9},{9,10},{10,11},{11... | collective-permute-start | bytes 491528 | tf_op jit(solution)/shard_map/ppermute | solution.py:48
  8.9 12.0 %collective-permute-start.1 = (bf16[4,1,160,128]{3,2,1,0:T(8,128)(2,1)S(1)}, bf16[4,1,160,128]{3,2,1,0:T(8,128)(2,1)S(1)}, u32[]{:S(2)}, u32[]{:S(2)}) collective-permute-start(bf16[4,1,160,128]{3,2,1,0:T(8,128)(2,1)S(1)} %get-tuple-element.28), channel_id=1, source_target_pairs={{1,0},{2,1},{3,2},{4,3},{5,4},{6,5},{7,6},{9,8},{10,9},{11,10},{12... | collective-permute-start | bytes 491528 | tf_op jit(solution)/shard_map/ppermute | solution.py:48
  12.8 21.1 %collective-permute-start.5 = (bf16[2,640,128]{2,1,0:T(8,128)(2,1)S(1)}, bf16[2,640,128]{2,1,0:T(8,128)(2,1)S(1)}, u32[]{:S(2)}, u32[]{:S(2)}) collective-permute-start(bf16[2,640,128]{2,1,0:T(8,128)(2,1)S(1)} %bitcast.91), channel_id=1, source_target_pairs={{0,8},{8,16},{16,24},{24,32},{32,40},{40,48},{48,56},{56,64},{64,7... | collective-permute-start | bytes 983048 | tf_op jit(solution)/shard_map/ppermute | solution.py:48
  16.7 20.7 %collective-permute-start.4 = (bf16[2,640,128]{2,1,0:T(8,128)(2,1)}, bf16[2,640,128]{2,1,0:T(8,128)(2,1)}, u32[]{:S(2)}, u32[]{:S(2)}) collective-permute-start(bf16[2,640,128]{2,1,0:T(8,128)(2,1)} %bitcast.17), channel_id=1, source_target_pairs={{8,0},{16,8},{24,16},{32,24},{40,32},{48,40},{56,48},{64,56},{72,6... | collective-permute-start | bytes 983048 | tf_op jit(solution)/shard_map/ppermute | solution.py:48
  22.9 1.2 copy-start.8
  24.1 2.9 %copy-start.10 = (bf16[4,4,160,1152]{3,2,1,0:T(8,128)(2,1)}, bf16[4,4,160,1152]{3,2,1,0:T(8,128)(2,1)S(1)}, u32[]{:S(2)}) copy-start(bf16[4,4,160,1152]{3,2,1,0:T(8,128)(2,1)S(1)} %slice_dynamic-update-slice_fusion) | copy-start | bytes 17694724
  24.1 10.6 %copy-start.3 = (bf16[4,4,160,128]{3,2,1,0:T(8,128)(2,1)S(1)}, bf16[4,4,160,128]{3,2,1,0:T(8,128)(2,1)}, u32[]{:S(2)}) copy-start(bf16[4,4,160,128]{3,2,1,0:T(8,128)(2,1)} %param.7) | copy-start | bytes 1966084
  27.9 48.7 %collective-permute-start.2 = (bf16[2,640,128]{2,1,0:T(8,128)(2,1)}, bf16[2,640,128]{2,1,0:T(8,128)(2,1)}, u32[]{:S(2)}, u32[]{:S(2)}) collective-permute-start(bf16[2,640,128]{2,1,0:T(8,128)(2,1)} %bitcast.3), channel_id=1, source_target_pairs={{0,8},{8,16},{16,24},{24,32},{32,40},{40,48},{48,56},{56,64},{64,7... | collective-permute-start | bytes 983048 | tf_op jit(solution)/shard_map/ppermute | solution.py:48
  32.6 44.0 %collective-permute-start.3 = (bf16[2,640,128]{2,1,0:T(8,128)(2,1)}, bf16[2,640,128]{2,1,0:T(8,128)(2,1)}, u32[]{:S(2)}, u32[]{:S(2)}) collective-permute-start(bf16[2,640,128]{2,1,0:T(8,128)(2,1)} %bitcast.10), channel_id=1, source_target_pairs={{8,0},{16,8},{24,16},{32,24},{40,32},{48,40},{56,48},{64,56},{72,6... | collective-permute-start | bytes 983048 | tf_op jit(solution)/shard_map/ppermute | solution.py:48
  33.9 0.7 copy-start.7
  34.7 2.8 %copy-start.1 = (bf16[4,4,160,128]{3,2,1,0:T(8,128)(2,1)S(1)}, bf16[4,4,160,128]{3,2,1,0:T(8,128)(2,1)}, u32[]{:S(2)}) copy-start(bf16[4,4,160,128]{3,2,1,0:T(8,128)(2,1)} %param.6) | copy-start | bytes 1966084
  35.9 0.8 copy-start.5
  43.3 2.1 %copy-start.6 = (bf16[4,640,128]{2,1,0:T(8,128)(2,1)S(1)}, bf16[4,640,128]{2,1,0:T(8,128)(2,1)}, u32[]{:S(2)}) copy-start(bf16[4,640,128]{2,1,0:T(8,128)(2,1)} %copy-done.5) | copy-start | bytes 1966084
  43.3 2.1 %copy-start.11 = (f32[2560,128]{1,0:T(8,128)S(1)}, f32[2560,128]{1,0:T(8,128)}, u32[]{:S(2)}) copy-start(f32[2560,128]{1,0:T(8,128)} %get-tuple-element.30) | copy-start | bytes 3932164
  43.3 3.2 %slice-start = ((s8[5898240]{0:T(1024)(128)(4,1)}), s8[4194304]{0:T(1024)(128)(4,1)S(1)}, s32[]{:S(2)}) async-start(s8[5898240]{0:T(1024)(128)(4,1)} %bitcast.101), calls=%async_computation.3 | async-start | bytes 8388608
  45.5 1.7 %slice-start.1 = ((s8[5898240]{0:T(1024)(128)(4,1)}), s8[1703936]{0:T(1024)(128)(4,1)S(1)}, s32[]{:S(2)}) async-start(s8[5898240]{0:T(1024)(128)(4,1)} %bitcast.101), calls=%async_computation.4 | async-start | bytes 3407872
  49.0 20.9 %collective-permute-start.6 = (bf16[4,1,160,128]{3,2,1,0:T(8,128)(2,1)S(1)}, bf16[4,1,160,128]{3,2,1,0:T(8,128)(2,1)S(1)}, u32[]{:S(2)}, u32[]{:S(2)}) collective-permute-start(bf16[4,1,160,128]{3,2,1,0:T(8,128)(2,1)S(1)} %get-tuple-element.21), channel_id=1, source_target_pairs={{0,1},{1,2},{2,3},{3,4},{4,5},{5,6},{6,7},{8,9},{9,10},{10,11},{11... | collective-permute-start | bytes 491528 | tf_op jit(solution)/shard_map/ppermute | solution.py:48
  54.4 15.5 %collective-permute-start.7 = (bf16[4,1,160,128]{3,2,1,0:T(8,128)(2,1)S(1)}, bf16[4,1,160,128]{3,2,1,0:T(8,128)(2,1)S(1)}, u32[]{:S(2)}, u32[]{:S(2)}) collective-permute-start(bf16[4,1,160,128]{3,2,1,0:T(8,128)(2,1)S(1)} %get-tuple-element.22), channel_id=1, source_target_pairs={{1,0},{2,1},{3,2},{4,3},{5,4},{6,5},{7,6},{9,8},{10,9},{11,10},{12... | collective-permute-start | bytes 491528 | tf_op jit(solution)/shard_map/ppermute | solution.py:48
  57.1 24.2 %all-to-all-start = ((bf16[32,48,128]{2,1,0:T(8,128)(2,1)}), bf16[32,48,128]{2,1,0:T(8,128)(2,1)S(1)}, u32[]{:S(2)}, u32[]{:S(2)}) async-start(bf16[32,48,128]{2,1,0:T(8,128)(2,1)} %bitcast.42), calls=%async_computation | async-start | bytes 786432 | tf_op jit(solution)/shard_map/all_to_all | solution.py:28
  76.6 20.7 %copy-start.9 = (bf16[3,128,128]{2,1,0:T(8,128)(2,1)S(1)}, bf16[3,128,128]{2,1,0:T(8,128)(2,1)}, u32[]{:S(2)}) copy-start(bf16[3,128,128]{2,1,0:T(8,128)(2,1)} %param.9) | copy-start | bytes 294916
  82.1 27.6 %all-to-all-start.1 = ((bf16[16,48,128]{2,1,0:T(8,128)(2,1)}), bf16[16,48,128]{2,1,0:T(8,128)(2,1)S(1)}, u32[]{:S(2)}, u32[]{:S(2)}) async-start(bf16[16,48,128]{2,1,0:T(8,128)(2,1)} %broadcast_in_dim.4), calls=%async_computation.1 | async-start | bytes 393216 | tf_op jit(solution)/shard_map/all_to_all | solution.py:28
  109.8 11.4 %copy-start.2 = (bf16[4,4,160,128]{3,2,1,0:T(8,128)(2,1)S(1)}, bf16[4,4,160,128]{3,2,1,0:T(8,128)(2,1)}, u32[]{:S(2)}) copy-start(bf16[4,4,160,128]{3,2,1,0:T(8,128)(2,1)} %param.6) | copy-start | bytes 1966084
  109.8 11.4 %copy-start.4 = (bf16[4,4,160,128]{3,2,1,0:T(8,128)(2,1)S(1)}, bf16[4,4,160,128]{3,2,1,0:T(8,128)(2,1)}, u32[]{:S(2)}) copy-start(bf16[4,4,160,128]{3,2,1,0:T(8,128)(2,1)} %param.7) | copy-start | bytes 1966084
  110.6 17.6 %all-to-all-start.2 = ((bf16[32,48,128]{2,1,0:T(8,128)(2,1)}), bf16[32,48,128]{2,1,0:T(8,128)(2,1)S(1)}, u32[]{:S(2)}, u32[]{:S(2)}) async-start(bf16[32,48,128]{2,1,0:T(8,128)(2,1)} %broadcast_in_dim.5), calls=%async_computation.2 | async-start | bytes 786432 | tf_op jit(solution)/shard_map/all_to_all | solution.py:28

commit v2 on v1

v2 whole, which is shorter than its diff:
```python
import functools
import math

import jax
import jax.numpy as jnp
from jax import lax
from jax.experimental import pallas as pl
from jax.experimental.pallas import tpu as pltpu
from jax.sharding import PartitionSpec as P

BOTH = ("tm", "tile")
F32 = jnp.float32
BF16 = jnp.bfloat16


def groups(bits):
    rest = [b for b in range(9) if b not in bits]
    out = []
    for r in range(1 << len(rest)):
        base = sum(((r >> i) & 1) << b for i, b in enumerate(rest))
        members = []
        for k in range(1 << len(bits)):
            members.append(base + sum(((k >> i) & 1) << b for i, b in enumerate(reversed(bits))))
        out.append(members)
    return out


NEAR = groups([8, 5, 4, 3, 0])
FAR = groups([7, 6, 2, 1])


def exchange(pieces, members):
    return lax.all_to_all(pieces, BOTH, 0, 0, tiled=True, axis_index_groups=members)


def swapped(value, axis, phase):
    count = lax.axis_size(axis)
    pairs = []
    for i in range(phase, count - 1, 2):
        pairs += [(i, i + 1), (i + 1, i)]
    return lax.ppermute(value, axis, pairs)


def is_even(axis):
    return lax.rem(lax.axis_index(axis), 2) == 0


def vmem_call(kernel, outs, scratch=(), name=None, anywhere=0):
    space = pl.BlockSpec(memory_space=pltpu.VMEM)

    def call(*args):
        return pl.pallas_call(
            kernel,
            out_shape=tuple(jax.ShapeDtypeStruct(s, t) for s, t in outs),
            in_specs=[space] * (len(args) - anywhere)
            + [pl.BlockSpec(memory_space=pl.ANY)] * anywhere,
            out_specs=tuple(space for _ in outs),
            scratch_shapes=list(scratch),
            compiler_params=pltpu.CompilerParams(vmem_limit_bytes=48 << 20),
            name=name,
        )(*args)

    return call


def edges_kernel(lat, fwd, rev, cots_a, cots_b, row_a, row_b, sems):
    even = is_even("tm")
    head, tail = fwd.at[pl.ds(0, 2)], rev.at[pl.ds(2, 2)]
    at = jnp.where(is_even("tile"), 3, 0)

    @pl.when(even)
    def _():
        pltpu.make_async_copy(tail, cots_a, sems.at[0]).start()
        pltpu.make_async_copy(head, cots_b, sems.at[1]).start()

    @pl.when(jnp.logical_not(even))
    def _():
        pltpu.make_async_copy(head, cots_a, sems.at[0]).start()
        pltpu.make_async_copy(tail, cots_b, sems.at[1]).start()

    pltpu.make_async_copy(lat.at[:, at], row_a, sems.at[2]).start()
    pltpu.make_async_copy(lat.at[:, 3 - at], row_b, sems.at[3]).start()
    pltpu.make_async_copy(head, cots_a, sems.at[0]).wait()
    pltpu.make_async_copy(tail, cots_b, sems.at[1]).wait()
    pltpu.make_async_copy(lat.at[:, at], row_a, sems.at[2]).wait()
    pltpu.make_async_copy(lat.at[:, 3 - at], row_b, sems.at[3]).wait()


def edges(lat, fwd, rev):
    frames, rows, width, channels = lat.shape
    line = (frames, width, channels)
    pair = (2, rows, width, channels)
    return vmem_call(
        edges_kernel,
        [(pair, BF16), (pair, BF16), (line, BF16), (line, BF16)],
        [pltpu.SemaphoreType.DMA((4,))],
        "edges",
        anywhere=3,
    )(lat, fwd, rev)


def spread_columns(row, out, frame, at):
    width = row.shape[0]
    wide = row.astype(F32)
    place = lax.broadcasted_iota(jnp.int32, wide.shape, 0)
    left = jnp.where(place == 0, 0.0, pltpu.roll(wide, 1, 0))
    right = jnp.where(place == width - 1, 0.0, pltpu.roll(wide, width - 1, 0))
    out[frame, at, :, 0:128] = left.astype(BF16)
    out[frame, at, :, 128:256] = row
    out[frame, at, :, 256:384] = right.astype(BF16)


def spread_frame(own, got_a, got_b, even, out, frame):
    one, two = got_a[frame], got_b[frame]
    spread_columns(jnp.where(even, two, one), out, frame, 0)
    for r in range(4):
        spread_columns(own[frame, r], out, frame, r + 1)
    spread_columns(jnp.where(even, one, two), out, frame, 5)


def patch_rows(spread, frame):
    return jnp.concatenate(
        [spread[frame, i : i + 4].reshape(640, 384) for i in range(3)], axis=1
    )


def transposed(block):
    return jnp.transpose(block.astype(F32))


def front_kernel(
    lat, row_a, row_b, fwd, rev, cots_a, cots_b, w_space_at, w_time_at,
    act_out, act_a, act_b, gp, gp_a, gp_b, partial,
    spread, w_space, w_time, back, acc_space, acc_time, sems,
):
    loads = [
        pltpu.make_async_copy(w_time_at, w_time, sems.at[0]),
        pltpu.make_async_copy(w_space_at, w_space, sems.at[1]),
    ]
    for c in loads:
        c.start()
    even_tm, even_tile = is_even("tm"), is_even("tile")
    spread_frame(lat, row_a, row_b, even_tile, spread, 0)
    for c in loads:
        c.wait()
    for k in range(3):
        turned = transposed(w_time[k * 128 : (k + 1) * 128, :]).astype(BF16)
        back[k * 128 : (k + 1) * 128, :] = turned
        back[384 + k * 128 : 384 + (k + 1) * 128, :] = turned
    for f in range(4):
        if f > 0:
            spread_frame(lat, row_a, row_b, even_tile, spread, f)
        patches = patch_rows(spread, f)
        pre = jnp.dot(patches, w_space[...], preferred_element_type=F32)
        sig = 0.5 + 0.5 * jnp.tanh(0.5 * pre)
        act32 = pre * sig
        act = act32.astype(BF16)
        act_out[f] = act.reshape(4, 160, 128)
        cots = []
        for k in range(3):
            if f + k < 4:
                cots.append(fwd[f + k])
            else:
                cots.append(jnp.where(even_tm, cots_a[f + k - 4], cots_b[f + k - 4]))
        for k in range(3):
            if f >= k:
                cots.append(rev[f - k])
            else:
                cots.append(jnp.where(even_tm, cots_b[f - k + 2], cots_a[f - k + 2]))
        cots = jnp.concatenate([c.reshape(640, 128) for c in cots], axis=1)
        grad_act = jnp.dot(cots, back[...], preferred_element_type=F32)
        grad = (grad_act * (sig + act32 * (1.0 - sig))).astype(BF16)
        gp[f] = grad.reshape(4, 160, 128)
        gp_a[f] = jnp.where(even_tile, grad[480:640], grad[0:160])
        gp_b[f] = jnp.where(even_tile, grad[0:160], grad[480:640])
        turn = transposed(grad).astype(BF16)
        more = jnp.dot(turn, patches, preferred_element_type=F32)
        turn = transposed(act).astype(BF16)
        more_time = jnp.dot(turn, cots, preferred_element_type=F32)
        more_time = more_time[:, :384] + more_time[:, 384:]
        if f == 0:
            acc_space[...] = more
            acc_time[...] = more_time
        else:
            acc_space[...] += more
            acc_time[...] += more_time
    for f in range(2):
        act_a[f] = jnp.where(even_tm, act_out[f + 2], act_out[f])
        act_b[f] = jnp.where(even_tm, act_out[f], act_out[f + 2])
    for k in range(9):
        partial[k * 128 : (k + 1) * 128, :] = jnp.transpose(
            acc_space[:, k * 128 : (k + 1) * 128]
        ).astype(BF16)
    for k in range(3):
        partial[(9 + k) * 128 : (10 + k) * 128, :] = acc_time[
            :, k * 128 : (k + 1) * 128
        ].astype(BF16)


def sum_kernel(scale, pieces, out):
    total = pieces[0].astype(F32)
    for k in range(1, pieces.shape[0]):
        total += pieces[k].astype(F32)
    total = (total * scale).astype(BF16)
    for k in range(out.shape[0]):
        out[k] = total


def sum_to_all(pieces, count, scale=1.0):
    (copies,) = vmem_call(
        functools.partial(sum_kernel, scale), [((count, *pieces.shape[1:]), BF16)], (), "share"
    )(pieces)
    return copies


def widen_kernel(pieces, space, time):
    rows = pieces.shape[1]
    for k in range(pieces.shape[0]):
        at = k * rows
        if at < space.shape[0]:
            space[at : at + rows, :] = pieces[k].astype(F32)
        else:
            at -= space.shape[0]
            time[at : at + rows, :] = pieces[k].astype(F32)


def outs_kernel(lat, act, got_a, got_b, w_time, out_f, out_r):
    even = is_even("tm")

    def frame(t):
        if t < 0:
            return jnp.where(even, got_b[t + 2], got_a[t + 2])
        if t < 4:
            return act[t]
        return jnp.where(even, got_a[t - 4], got_b[t - 4])

    for t in range(4):
        residual = lat[t].reshape(640, 128).astype(F32)
        for sign, out in ((-1, out_f), (1, out_r)):
            rows = jnp.concatenate([frame(t + sign * k).reshape(640, 128) for k in range(3)], axis=1)
            total = residual + jnp.dot(rows, w_time[...], preferred_element_type=F32)
            out[t] = total.astype(BF16).reshape(4, 160, 128)


def input_kernel(gp, got_a, got_b, fwd, rev, w_space, out, spread, back):
    even = is_even("tile")
    for i in range(3):
        for j in range(3):
            at = (i * 3 + j) * 128
            back[at : at + 128, :] = transposed(
                w_space[((2 - i) * 3 + 2 - j) * 128 : ((2 - i) * 3 + 3 - j) * 128, :]
            ).astype(BF16)
    for f in range(4):
        spread_frame(gp, got_a, got_b, even, spread, f)
        patches = patch_rows(spread, f)
        total = fwd[f].astype(F32) + rev[f].astype(F32)
        total = total.reshape(640, 128) + jnp.dot(patches, back[...], preferred_element_type=F32)
        out[f] = total.astype(BF16).reshape(4, 160, 128)


def body(latent, cot_forward, cot_reverse, spatial_weight, temporal_weight):
    frame_count, height, width_cells, channels = latent.shape
    cells = latent.shape
    line = (frame_count, width_cells, channels)
    pair = (2, height, width_cells, channels)
    w_space = spatial_weight.reshape(9 * channels, channels)
    w_time = temporal_weight.reshape(3 * channels, channels)
    spread = pltpu.VMEM((frame_count, height + 2, width_cells, 3 * channels), BF16)

    cots_a, cots_b, row_a, row_b = edges(latent, cot_forward, cot_reverse)
    cots_b = swapped(cots_b, "tm", 1)
    cots_a = swapped(cots_a, "tm", 0)
    row_b = swapped(row_b, "tile", 1)
    row_a = swapped(row_a, "tile", 0)
    act, act_a, act_b, gp, gp_a, gp_b, partial = vmem_call(
        front_kernel,
        [
            (cells, BF16), (pair, BF16), (pair, BF16),
            (cells, BF16), (line, BF16), (line, BF16),
            ((12 * channels, channels), BF16),
        ],
        [
            spread,
            pltpu.VMEM((9 * channels, channels), BF16),
            pltpu.VMEM((3 * channels, channels), BF16),
            pltpu.VMEM((6 * channels, channels), BF16),
            pltpu.VMEM((channels, 9 * channels), F32),
            pltpu.VMEM((channels, 3 * channels), F32),
            pltpu.SemaphoreType.DMA((2,)),
        ],
        "front",
        anywhere=2,
    )(latent, row_a, row_b, cot_forward, cot_reverse, cots_a, cots_b, w_space, w_time)

    near, far = len(NEAR[0]), len(FAR[0])
    positions = frame_count * height * width_cells * lax.axis_size("tm") * lax.axis_size("tile")
    shares = sum_to_all(exchange(partial.reshape(near, -1, channels), NEAR), far)
    shares, act_a, act_b, gp_a, gp_b = lax.optimization_barrier((shares, act_a, act_b, gp_a, gp_b))
    shares = exchange(shares, FAR)
    act_b = swapped(act_b, "tm", 1)
    act_a = swapped(act_a, "tm", 0)
    gp_b = swapped(gp_b, "tile", 1)
    gp_a = swapped(gp_a, "tile", 0)
    out_forward, out_reverse = vmem_call(outs_kernel, [(cells, BF16), (cells, BF16)], (), "outs")(
        latent, act, act_a, act_b, w_time
    )
    shares, out_forward, out_reverse, gp_a, gp_b = lax.optimization_barrier(
        (shares, out_forward, out_reverse, gp_a, gp_b)
    )
    whole = exchange(sum_to_all(shares, near, 1.0 / math.sqrt(positions)), NEAR)
    (grad_input,) = vmem_call(
        input_kernel, [(cells, BF16)], [spread, pltpu.VMEM((9 * channels, channels), BF16)], "grad_input"
    )(gp, gp_a, gp_b, cot_forward, cot_reverse, w_space)
    grad_spatial, grad_temporal = vmem_call(
        widen_kernel, [((9 * channels, channels), F32), ((3 * channels, channels), F32)], (), "widen"
    )(whole)
    grad_spatial = grad_spatial.reshape(3, 3, channels, channels)
    grad_temporal = grad_temporal.reshape(3, channels, channels)
    return (out_forward, out_reverse, grad_input, grad_spatial, grad_temporal)


def solution(mesh):
    cells = P("tm", "tile", None, None)
    return jax.shard_map(
        body,
        mesh=mesh,
        in_specs=(cells, cells, cells, P(), P()),
        out_specs=(cells, cells, cells, P(), P()),
        check_vma=False,
    )
```

time: 131 us -> 96.9 us (0.74)
  matrix products: 21.8 us -> 0 us
  local copies, waits for them, and re-layouts: 24.6 us -> 3.27 us
  blocking collectives: 0 us -> 16.9 us
  starting transfers between devices: 62.6 us -> 47.5 us
  Pallas kernels: 0 us -> 13.5 us
  other arithmetic: 9.24 us -> 0 us
  waiting for transfers between devices: 10.4 us -> 14.2 us
    dot_general x9 -> x0, matrix products: 21.8 us -> none  [the longest x1 5.22 us: body(): jnp.dot(grad_patches, flipped_flat, preferred_element_type=jnp.float32)]
    all_to_all x0 -> x1, blocking collectives: none -> 16.9 us  [exchange(): lax.all_to_all(pieces, BOTH, 0, 0, tiled=True, axis_index_groups=members)]
    pallas_call x0 -> x7, Pallas kernels: none -> 13.5 us  [call(): pl.pallas_call(kernel, out_shape=tuple((jax.ShapeDtypeStruct(s, t) for s,...]
    all_to_all x3 -> x2, starting transfers between devices: 35.8 us -> 24.1 us  [exchange(): lax.all_to_all(pieces, BOTH, 0, 0, tiled=True, axis_index_groups=members)]
    unnamed x44 -> x16, local copies, waits for them, and re-layouts: 14 us -> 3.27 us
    concatenate x7 -> x0, other arithmetic: 8.75 us -> none  [the longest x4 4.55 us: rim(): jnp.concatenate([shifted(tail, axis, 1), cells, shifted(head, axis, -1)],...]
    ppermute x8, waiting for transfers between devices: 0.02 us -> 7.14 us  [swapped(): return lax.ppermute(value, axis, pairs)]
    slice x8 -> x0, local copies, waits for them, and re-layouts: 6.94 us -> none  [the longest x1 1.72 us: body(): following = shifted(fwd_cot[:2], 'tm', -1)]
  transfers between devices with their start and end apart: 11 -> 10, of which waited for: 2 -> 4; matrix products, arithmetic and copies ran while one was open for 38% -> 0% of each run, Pallas kernels for 0% -> 5%
where the time goes in v2:
time: 96.9 us; the launch traced here: 96.2 us
  starting transfers between devices  47.5 us (49%)
  blocking collectives  16.9 us (17%)
  waiting for transfers between devices  14.2 us (15%)
  Pallas kernels  13.5 us (14%)
  local copies, waits for them, and re-layouts  3.27 us (3%)
    all_to_all x2, starting transfers between devices, exchange(): lax.all_to_all(pieces, BOTH, 0, 0, tiled=True, axis_index_groups=members)  24.1 us
    ppermute x8, starting transfers between devices, swapped(): return lax.ppermute(value, axis, pairs)  23.4 us
    all_to_all x1, blocking collectives, exchange(): lax.all_to_all(pieces, BOTH, 0, 0, tiled=True, axis_index_groups=members)  16.9 us
    pallas_call x7, Pallas kernels, call(): pl.pallas_call(kernel, out_shape=tuple((jax.ShapeDtypeStruct(s, t) for s,...  13.5 us
    ppermute x8, waiting for transfers between devices, swapped(): return lax.ppermute(value, axis, pairs)  7.14 us
    all_to_all x2, waiting for transfers between devices, exchange(): lax.all_to_all(pieces, BOTH, 0, 0, tiled=True, axis_index_groups=members)  7.07 us
    unnamed x16, local copies, waits for them, and re-layouts  3.27 us
  transfers between devices with their start and end apart: 10, of which 4 were waited for; matrix products, arithmetic and copies ran while one was open for 0% of the time, Pallas kernels for 5%

profile of v2, /device:TPU:1, one launch (start us, length us, event | category | flops | bytes accessed | tf_op | source)
XLA Modules:
  0.0 96.2 jit_solution(10517129865880069596)
XLA Ops:
  0.6 0.0 copy-start
  0.6 1.1 %copy-done = bf16[4,4,160,128]{3,2,1,0:T(8,128)(2,1)S(1)} copy-done((bf16[4,4,160,128]{3,2,1,0:T(8,128)(2,1)S(1)}, bf16[4,4,160,128]{3,2,1,0:T(8,128)(2,1)}, u32[]{:S(2)}) %copy-start) | copy-done | bytes 655384
  1.7 0.0 copy-start.2
  1.7 1.1 %copy-done.2 = bf16[4,4,160,128]{3,2,1,0:T(8,128)(2,1)S(1)} copy-done((bf16[4,4,160,128]{3,2,1,0:T(8,128)(2,1)S(1)}, bf16[4,4,160,128]{3,2,1,0:T(8,128)(2,1)}, u32[]{:S(2)}) %copy-start.2) | copy-done | bytes 655384
  2.8 0.0 copy-start.4
  2.8 1.1 %copy-done.4 = bf16[4,4,160,128]{3,2,1,0:T(8,128)(2,1)S(1)} copy-done((bf16[4,4,160,128]{3,2,1,0:T(8,128)(2,1)S(1)}, bf16[4,4,160,128]{3,2,1,0:T(8,128)(2,1)}, u32[]{:S(2)}) %copy-start.4) | copy-done | bytes 655384
  3.9 0.0 copy-start.6
  3.9 0.0 copy-start.7
  3.9 0.4 edges.1
  4.3 3.9 %collective-permute-start.2 = (bf16[2,4,160,128]{3,2,1,0:T(8,128)(2,1)S(1)}, bf16[2,4,160,128]{3,2,1,0:T(8,128)(2,1)S(1)}, u32[]{:S(2)}, u32[]{:S(2)}) collective-permute-start(bf16[2,4,160,128]{3,2,1,0:T(8,128)(2,1)S(1)} %get-tuple-element.32), channel_id=1, source_target_pairs={{0,8},{8,0},{16,24},{24,16},{32,40},{40,32},{48,56},{56,48},{64,72... | collective-permute-start | bytes 983048 | tf_op jit(solution)/shard_map/ppermute | solution.py:41
  8.2 0.7 collective-permute-start.3
  8.9 6.8 %collective-permute-start = (bf16[4,160,128]{2,1,0:T(8,128)(2,1)S(1)}, bf16[4,160,128]{2,1,0:T(8,128)(2,1)S(1)}, u32[]{:S(2)}, u32[]{:S(2)}) collective-permute-start(bf16[4,160,128]{2,1,0:T(8,128)(2,1)S(1)} %get-tuple-element.30), channel_id=1, source_target_pairs={{0,1},{1,0},{2,3},{3,2},{4,5},{5,4},{6,7},{7,6},{8,9},{9,8},{10,11... | collective-permute-start | bytes 491528 | tf_op jit(solution)/shard_map/ppermute | solution.py:41
  15.7 1.9 %collective-permute-start.1 = (bf16[4,160,128]{2,1,0:T(8,128)(2,1)S(1)}, bf16[4,160,128]{2,1,0:T(8,128)(2,1)S(1)}, u32[]{:S(2)}, u32[]{:S(2)}) collective-permute-start(bf16[4,160,128]{2,1,0:T(8,128)(2,1)S(1)} %get-tuple-element.31), channel_id=1, source_target_pairs={{1,2},{2,1},{3,4},{4,3},{5,6},{6,5},{9,10},{10,9},{11,12},{12,11},... | collective-permute-start | bytes 491528 | tf_op jit(solution)/shard_map/ppermute | solution.py:41
  17.6 0.0 collective-permute-done.row_a
  17.6 5.6 %collective-permute-done.1.row_b = bf16[4,160,128]{2,1,0:T(8,128)(2,1)S(1)} collective-permute-done((bf16[4,160,128]{2,1,0:T(8,128)(2,1)S(1)}, bf16[4,160,128]{2,1,0:T(8,128)(2,1)S(1)}, u32[]{:S(2)}, u32[]{:S(2)}) %collective-permute-start.1) | collective-permute-done | bytes 163872 | tf_op jit(solution)/shard_map/ppermute | solution.py:41
  23.2 0.0 collective-permute-done.2.cots_a
  23.2 0.0 collective-permute-done.3.cots_b
  23.2 0.0 copy-done.6
  23.2 0.0 copy-done.7
  23.2 5.8 %front.1 = (bf16[4,4,160,128]{3,2,1,0:T(8,128)(2,1)S(1)}, bf16[2,4,160,128]{3,2,1,0:T(8,128)(2,1)}, bf16[2,4,160,128]{3,2,1,0:T(8,128)(2,1)S(1)}, bf16[4,4,160,1...) custom-call(bf16[4,4,160,128]{3,2,1,0:T(8,128)(2,1)S(1)} %copy-done,, ...), custom_call_target="tpu_custom_call" | custom-call | tf_op jit(solution)/shard_map/front/pallas_call | solution.py:52
  29.0 16.9 %all_to_all.15.pieces = bf16[32,48,128]{2,1,0:T(8,128)(2,1)S(1)} all-to-all(bf16[32,48,128]{2,1,0:T(8,128)(2,1)S(1)} %bitcast.9), channel_id=1, replica_groups={{0,1,8,9,16,17,24,25,32,33,40,41,48,49,56,57,256,257,264,265,272,273,28..., dimensions={0} | all-to-all | bytes 786432 | tf_op jit(solution)/shard_map/all_to_all | solution.py:33
  46.0 0.0 copy-start.1
  46.0 0.7 share.2
  46.7 14.3 %all-to-all-start.1 = ((bf16[16,48,128]{2,1,0:T(8,128)(2,1)}), bf16[16,48,128]{2,1,0:T(8,128)(2,1)S(1)}, u32[]{:S(2)}, u32[]{:S(2)}) async-start(bf16[16,48,128]{2,1,0:T(8,128)(2,1)} %share.2), calls=%async_computation.1 | async-start | bytes 393216 | tf_op jit(solution)/shard_map/all_to_all | solution.py:33
  61.0 2.1 %collective-permute-start.4 = (bf16[2,4,160,128]{3,2,1,0:T(8,128)(2,1)}, bf16[2,4,160,128]{3,2,1,0:T(8,128)(2,1)S(1)}, u32[]{:S(2)}, u32[]{:S(2)}) collective-permute-start(bf16[2,4,160,128]{3,2,1,0:T(8,128)(2,1)} %get-tuple-element.41), channel_id=1, source_target_pairs={{0,8},{8,0},{16,24},{24,16},{32,40},{40,32},{48,56},{56,48},{64,72... | collective-permute-start | bytes 983048 | tf_op jit(solution)/shard_map/ppermute | solution.py:41
  63.1 0.7 collective-permute-start.5
  63.8 3.0 %collective-permute-start.6 = (bf16[4,160,128]{2,1,0:T(8,128)(2,1)}, bf16[4,160,128]{2,1,0:T(8,128)(2,1)S(1)}, u32[]{:S(2)}, u32[]{:S(2)}) collective-permute-start(bf16[4,160,128]{2,1,0:T(8,128)(2,1)} %get-tuple-element.45), channel_id=1, source_target_pairs={{0,1},{1,0},{2,3},{3,2},{4,5},{5,4},{6,7},{7,6},{8,9},{9,8},{10,11... | collective-permute-start | bytes 491528 | tf_op jit(solution)/shard_map/ppermute | solution.py:41
  66.8 4.3 %collective-permute-start.7 = (bf16[4,160,128]{2,1,0:T(8,128)(2,1)S(1)}, bf16[4,160,128]{2,1,0:T(8,128)(2,1)S(1)}, u32[]{:S(2)}, u32[]{:S(2)}) collective-permute-start(bf16[4,160,128]{2,1,0:T(8,128)(2,1)S(1)} %get-tuple-element.46), channel_id=1, source_target_pairs={{1,2},{2,1},{3,4},{4,3},{5,6},{6,5},{9,10},{10,9},{11,12},{12,11},... | collective-permute-start | bytes 491528 | tf_op jit(solution)/shard_map/ppermute | solution.py:41
  71.1 0.6 collective-permute-done.4.got_a
  71.7 0.0 collective-permute-done.5.got_b
  71.7 0.0 copy-done.1
  71.7 2.1 %outs.1 = (bf16[4,4,160,128]{3,2,1,0:T(8,128)(2,1)}, bf16[4,4,160,128]{3,2,1,0:T(8,128)(2,1)}) custom-call(bf16[4,4,160,128]{3,2,1,0:T(8,128)(2,1)S(1)} %copy-done.1, bf16[4,4,160,128]{3,2,1,0:T(8,128)(2,1)S(1)} %get-tuple-element.40.act, bf16[2,4,160,128]{3,2,1,0:T(8,128)(2,1)S(1)} %collective-permute-done.4.got_a, ...), custom_call_target="tpu_custom_call" | custom-call | tf_op jit(solution)/shard_map/outs/pallas_call | solution.py:52
  73.8 0.0 collective-permute-done.6.got_a
  73.8 1.0 %collective-permute-done.7.got_b = bf16[4,160,128]{2,1,0:T(8,128)(2,1)S(1)} collective-permute-done((bf16[4,160,128]{2,1,0:T(8,128)(2,1)S(1)}, bf16[4,160,128]{2,1,0:T(8,128)(2,1)S(1)}, u32[]{:S(2)}, u32[]{:S(2)}) %collective-permute-start.7) | collective-permute-done | bytes 163872 | tf_op jit(solution)/shard_map/ppermute | solution.py:41
  74.8 0.0 all-to-all-done.1.pieces
  74.8 0.0 copy-start.3
  74.8 0.0 copy-start.5
  74.8 0.8 share.3
  75.6 9.9 %all-to-all-start.2 = ((bf16[32,48,128]{2,1,0:T(8,128)(2,1)}), bf16[32,48,128]{2,1,0:T(8,128)(2,1)S(1)}, u32[]{:S(2)}, u32[]{:S(2)}) async-start(bf16[32,48,128]{2,1,0:T(8,128)(2,1)} %share.3), calls=%async_computation.2 | async-start | bytes 786432 | tf_op jit(solution)/shard_map/all_to_all | solution.py:33
  85.5 0.0 copy-done.3
  85.5 0.0 copy-done.5
  85.5 2.7 %grad_input.1 = bf16[4,4,160,128]{3,2,1,0:T(8,128)(2,1)} custom-call(bf16[4,4,160,128]{3,2,1,0:T(8,128)(2,1)S(1)} %get-tuple-element.49.gp, bf16[4,160,128]{2,1,0:T(8,128)(2,1)S(1)} %collective-permute-done.6.got_a, bf16[4,160,128]{2,1,0:T(8,128)(2,1)S(1)} %collective-permute-done.7.got_b, bf16[4,4,160,128]{3,2,1,0:T(8,128)(2,1)S(1)} %copy-done.3, ...), custom_call_target="tpu_custom_call" | custom-call | tf_op jit(solution)/shard_map/grad_input/pallas_call | solution.py:52
  88.2 7.1 %all-to-all-done.2.pieces = bf16[32,48,128]{2,1,0:T(8,128)(2,1)S(1)} async-done(((bf16[32,48,128]{2,1,0:T(8,128)(2,1)}), bf16[32,48,128]{2,1,0:T(8,128)(2,1)S(1)}, u32[]{:S(2)}, u32[]{:S(2)}) %all-to-all-start.2) | async-done | bytes 393248 | tf_op jit(solution)/shard_map/all_to_all | solution.py:33
  95.3 0.9 widen.1
Async XLA Ops:
  0.6 1.1 %copy-start = (bf16[4,4,160,128]{3,2,1,0:T(8,128)(2,1)S(1)}, bf16[4,4,160,128]{3,2,1,0:T(8,128)(2,1)}, u32[]{:S(2)}) copy-start(bf16[4,4,160,128]{3,2,1,0:T(8,128)(2,1)} %lat.5) | copy-start | bytes 1966084
  1.7 1.1 %copy-start.2 = (bf16[4,4,160,128]{3,2,1,0:T(8,128)(2,1)S(1)}, bf16[4,4,160,128]{3,2,1,0:T(8,128)(2,1)}, u32[]{:S(2)}) copy-start(bf16[4,4,160,128]{3,2,1,0:T(8,128)(2,1)} %fwd.5) | copy-start | bytes 1966084
  2.8 1.1 %copy-start.4 = (bf16[4,4,160,128]{3,2,1,0:T(8,128)(2,1)S(1)}, bf16[4,4,160,128]{3,2,1,0:T(8,128)(2,1)}, u32[]{:S(2)}) copy-start(bf16[4,4,160,128]{3,2,1,0:T(8,128)(2,1)} %rev.5) | copy-start | bytes 1966084
  3.9 19.3 %copy-start.6 = (bf16[3,3,128,128]{3,2,1,0:T(8,128)(2,1)S(1)}, bf16[3,3,128,128]{3,2,1,0:T(8,128)(2,1)}, u32[]{:S(2)}) copy-start(bf16[3,3,128,128]{3,2,1,0:T(8,128)(2,1)} %param.8) | copy-start | bytes 884740
  3.9 19.3 %copy-start.7 = (bf16[3,128,128]{2,1,0:T(8,128)(2,1)S(1)}, bf16[3,128,128]{2,1,0:T(8,128)(2,1)}, u32[]{:S(2)}) copy-start(bf16[3,128,128]{2,1,0:T(8,128)(2,1)} %param.9) | copy-start | bytes 294916
  4.3 19.0 %collective-permute-start.2 = (bf16[2,4,160,128]{3,2,1,0:T(8,128)(2,1)S(1)}, bf16[2,4,160,128]{3,2,1,0:T(8,128)(2,1)S(1)}, u32[]{:S(2)}, u32[]{:S(2)}) collective-permute-start(bf16[2,4,160,128]{3,2,1,0:T(8,128)(2,1)S(1)} %get-tuple-element.32), channel_id=1, source_target_pairs={{0,8},{8,0},{16,24},{24,16},{32,40},{40,32},{48,56},{56,48},{64,72... | collective-permute-start | bytes 983048 | tf_op jit(solution)/shard_map/ppermute | solution.py:41
  8.2 15.0 %collective-permute-start.3 = (bf16[2,4,160,128]{3,2,1,0:T(8,128)(2,1)S(1)}, bf16[2,4,160,128]{3,2,1,0:T(8,128)(2,1)S(1)}, u32[]{:S(2)}, u32[]{:S(2)}) collective-permute-start(bf16[2,4,160,128]{3,2,1,0:T(8,128)(2,1)S(1)} %get-tuple-element.33), channel_id=1, source_target_pairs={{8,16},{16,8},{24,32},{32,24},{40,48},{48,40},{56,64},{64,56},{72,... | collective-permute-start | bytes 983048 | tf_op jit(solution)/shard_map/ppermute | solution.py:41
  8.9 8.7 %collective-permute-start = (bf16[4,160,128]{2,1,0:T(8,128)(2,1)S(1)}, bf16[4,160,128]{2,1,0:T(8,128)(2,1)S(1)}, u32[]{:S(2)}, u32[]{:S(2)}) collective-permute-start(bf16[4,160,128]{2,1,0:T(8,128)(2,1)S(1)} %get-tuple-element.30), channel_id=1, source_target_pairs={{0,1},{1,0},{2,3},{3,2},{4,5},{5,4},{6,7},{7,6},{8,9},{9,8},{10,11... | collective-permute-start | bytes 491528 | tf_op jit(solution)/shard_map/ppermute | solution.py:41
  15.7 7.5 %collective-permute-start.1 = (bf16[4,160,128]{2,1,0:T(8,128)(2,1)S(1)}, bf16[4,160,128]{2,1,0:T(8,128)(2,1)S(1)}, u32[]{:S(2)}, u32[]{:S(2)}) collective-permute-start(bf16[4,160,128]{2,1,0:T(8,128)(2,1)S(1)} %get-tuple-element.31), channel_id=1, source_target_pairs={{1,2},{2,1},{3,4},{4,3},{5,6},{6,5},{9,10},{10,9},{11,12},{12,11},... | collective-permute-start | bytes 491528 | tf_op jit(solution)/shard_map/ppermute | solution.py:41
  46.0 25.7 %copy-start.1 = (bf16[4,4,160,128]{3,2,1,0:T(8,128)(2,1)S(1)}, bf16[4,4,160,128]{3,2,1,0:T(8,128)(2,1)}, u32[]{:S(2)}) copy-start(bf16[4,4,160,128]{3,2,1,0:T(8,128)(2,1)} %lat.5) | copy-start | bytes 1966084
  46.7 28.1 %all-to-all-start.1 = ((bf16[16,48,128]{2,1,0:T(8,128)(2,1)}), bf16[16,48,128]{2,1,0:T(8,128)(2,1)S(1)}, u32[]{:S(2)}, u32[]{:S(2)}) async-start(bf16[16,48,128]{2,1,0:T(8,128)(2,1)} %share.2), calls=%async_computation.1 | async-start | bytes 393216 | tf_op jit(solution)/shard_map/all_to_all | solution.py:33
  61.0 10.7 %collective-permute-start.4 = (bf16[2,4,160,128]{3,2,1,0:T(8,128)(2,1)}, bf16[2,4,160,128]{3,2,1,0:T(8,128)(2,1)S(1)}, u32[]{:S(2)}, u32[]{:S(2)}) collective-permute-start(bf16[2,4,160,128]{3,2,1,0:T(8,128)(2,1)} %get-tuple-element.41), channel_id=1, source_target_pairs={{0,8},{8,0},{16,24},{24,16},{32,40},{40,32},{48,56},{56,48},{64,72... | collective-permute-start | bytes 983048 | tf_op jit(solution)/shard_map/ppermute | solution.py:41
  63.1 8.6 %collective-permute-start.5 = (bf16[2,4,160,128]{3,2,1,0:T(8,128)(2,1)S(1)}, bf16[2,4,160,128]{3,2,1,0:T(8,128)(2,1)S(1)}, u32[]{:S(2)}, u32[]{:S(2)}) collective-permute-start(bf16[2,4,160,128]{3,2,1,0:T(8,128)(2,1)S(1)} %get-tuple-element.42), channel_id=1, source_target_pairs={{8,16},{16,8},{24,32},{32,24},{40,48},{48,40},{56,64},{64,56},{72,... | collective-permute-start | bytes 983048 | tf_op jit(solution)/shard_map/ppermute | solution.py:41
  63.8 10.0 %collective-permute-start.6 = (bf16[4,160,128]{2,1,0:T(8,128)(2,1)}, bf16[4,160,128]{2,1,0:T(8,128)(2,1)S(1)}, u32[]{:S(2)}, u32[]{:S(2)}) collective-permute-start(bf16[4,160,128]{2,1,0:T(8,128)(2,1)} %get-tuple-element.45), channel_id=1, source_target_pairs={{0,1},{1,0},{2,3},{3,2},{4,5},{5,4},{6,7},{7,6},{8,9},{9,8},{10,11... | collective-permute-start | bytes 491528 | tf_op jit(solution)/shard_map/ppermute | solution.py:41
  66.8 8.0 %collective-permute-start.7 = (bf16[4,160,128]{2,1,0:T(8,128)(2,1)S(1)}, bf16[4,160,128]{2,1,0:T(8,128)(2,1)S(1)}, u32[]{:S(2)}, u32[]{:S(2)}) collective-permute-start(bf16[4,160,128]{2,1,0:T(8,128)(2,1)S(1)} %get-tuple-element.46), channel_id=1, source_target_pairs={{1,2},{2,1},{3,4},{4,3},{5,6},{6,5},{9,10},{10,9},{11,12},{12,11},... | collective-permute-start | bytes 491528 | tf_op jit(solution)/shard_map/ppermute | solution.py:41
  74.8 10.7 %copy-start.3 = (bf16[4,4,160,128]{3,2,1,0:T(8,128)(2,1)S(1)}, bf16[4,4,160,128]{3,2,1,0:T(8,128)(2,1)}, u32[]{:S(2)}) copy-start(bf16[4,4,160,128]{3,2,1,0:T(8,128)(2,1)} %fwd.5) | copy-start | bytes 1966084
  74.8 10.7 %copy-start.5 = (bf16[4,4,160,128]{3,2,1,0:T(8,128)(2,1)S(1)}, bf16[4,4,160,128]{3,2,1,0:T(8,128)(2,1)}, u32[]{:S(2)}) copy-start(bf16[4,4,160,128]{3,2,1,0:T(8,128)(2,1)} %rev.5) | copy-start | bytes 1966084
  75.6 19.7 %all-to-all-start.2 = ((bf16[32,48,128]{2,1,0:T(8,128)(2,1)}), bf16[32,48,128]{2,1,0:T(8,128)(2,1)S(1)}, u32[]{:S(2)}, u32[]{:S(2)}) async-start(bf16[32,48,128]{2,1,0:T(8,128)(2,1)} %share.3), calls=%async_computation.2 | async-start | bytes 786432 | tf_op jit(solution)/shard_map/all_to_all | solution.py:33

commit v3 on v2

--- a/solution.py
+++ b/solution.py
@@ -45,22 +45,28 @@
     return lax.rem(lax.axis_index(axis), 2) == 0
 
 
-def vmem_call(kernel, outs, scratch=(), name=None, anywhere=0):
+def vmem_call(kernel, outs, scratch=(), name=None, in_hbm=0, outs_hbm=()):
     space = pl.BlockSpec(memory_space=pltpu.VMEM)
 
     def call(*args):
         return pl.pallas_call(
             kernel,
-            out_shape=tuple(jax.ShapeDtypeStruct(s, t) for s, t in outs),
-            in_specs=[space] * (len(args) - anywhere)
-            + [pl.BlockSpec(memory_space=pl.ANY)] * anywhere,
-            out_specs=tuple(space for _ in outs),
+            out_shape=tuple(jax.ShapeDtypeStruct(s, t) for s, t in outs)
+            + tuple(pltpu.HBM(s, t) for s, t in outs_hbm),
+            in_specs=[space] * (len(args) - in_hbm)
+            + [pl.BlockSpec(memory_space=pltpu.HBM)] * in_hbm,
+            out_specs=tuple(space for _ in outs)
+            + tuple(pl.BlockSpec(memory_space=pltpu.HBM) for _ in outs_hbm),
             scratch_shapes=list(scratch),
             compiler_params=pltpu.CompilerParams(vmem_limit_bytes=48 << 20),
             name=name,
-        )(*args)
+        )(*args[: len(args) - in_hbm], *(held(a) for a in args[len(args) - in_hbm :]))
 
     return call
+
+
+def held(value):
+    return pltpu.with_memory_space_constraint(value, pltpu.HBM)
 
 
 def edges_kernel(lat, fwd, rev, cots_a, cots_b, row_a, row_b, sems):
@@ -90,13 +96,15 @@
     frames, rows, width, channels = lat.shape
     line = (frames, width, channels)
     pair = (2, rows, width, channels)
-    return vmem_call(
+    anywhere = pl.BlockSpec(memory_space=pl.ANY)
+    return pl.pallas_call(
         edges_kernel,
-        [(pair, BF16), (pair, BF16), (line, BF16), (line, BF16)],
-        [pltpu.SemaphoreType.DMA((4,))],
-        "edges",
-        anywhere=3,
-    )(lat, fwd, rev)
+        out_shape=tuple(jax.ShapeDtypeStruct(s, BF16) for s in (pair, pair, line, line)),
+        in_specs=[anywhere] * 3,
+        out_specs=(pl.BlockSpec(memory_space=pltpu.VMEM),) * 4,
+        scratch_shapes=[pltpu.SemaphoreType.DMA((4,))],
+        name="edges",
+    )(held(lat), held(fwd), held(rev))
 
 
 def spread_columns(row, out, frame, at):
@@ -129,9 +137,9 @@
 
 
 def front_kernel(
-    lat, row_a, row_b, fwd, rev, cots_a, cots_b, w_space_at, w_time_at,
-    act_out, act_a, act_b, gp, gp_a, gp_b, partial,
-    spread, w_space, w_time, back, acc_space, acc_time, sems,
+    lat, row_b, row_a, fwd, rev, cots_b, cots_a, w_space_at, w_time_at,
+    act_out, gp_out, act_a, act_b, gp_a, gp_b, partial,
+    spread, gp, w_space, w_time, back, acc_space, acc_time, summed, sems,
 ):
     loads = [
         pltpu.make_async_copy(w_time_at, w_time, sems.at[0]),
@@ -147,6 +155,7 @@
         turned = transposed(w_time[k * 128 : (k + 1) * 128, :]).astype(BF16)
         back[k * 128 : (k + 1) * 128, :] = turned
         back[384 + k * 128 : 384 + (k + 1) * 128, :] = turned
+    stores = []
     for f in range(4):
         if f > 0:
             spread_frame(lat, row_a, row_b, even_tile, spread, f)
@@ -171,8 +180,9 @@
         grad_act = jnp.dot(cots, back[...], preferred_element_type=F32)
         grad = (grad_act * (sig + act32 * (1.0 - sig))).astype(BF16)
         gp[f] = grad.reshape(4, 160, 128)
-        gp_a[f] = jnp.where(even_tile, grad[480:640], grad[0:160])
-        gp_b[f] = jnp.where(even_tile, grad[0:160], grad[480:640])
+        gp_copy = pltpu.make_async_copy(gp.at[f], gp_out.at[f], sems.at[7 + f])
+        gp_copy.start()
+        stores.append(gp_copy)
         turn = transposed(grad).astype(BF16)
         more = jnp.dot(turn, patches, preferred_element_type=F32)
         turn = transposed(act).astype(BF16)
@@ -184,17 +194,28 @@
         else:
             acc_space[...] += more
             acc_time[...] += more_time
-    for f in range(2):
-        act_a[f] = jnp.where(even_tm, act_out[f + 2], act_out[f])
-        act_b[f] = jnp.where(even_tm, act_out[f], act_out[f + 2])
+    at_frame, at_row = jnp.where(even_tm, 2, 0), jnp.where(even_tile, 3, 0)
+    edge_stores = [
+        pltpu.make_async_copy(act_out.at[pl.ds(at_frame, 2)], act_a, sems.at[2]),
+        pltpu.make_async_copy(act_out.at[pl.ds(2 - at_frame, 2)], act_b, sems.at[3]),
+        pltpu.make_async_copy(gp.at[:, at_row], gp_a, sems.at[4]),
+        pltpu.make_async_copy(gp.at[:, 3 - at_row], gp_b, sems.at[5]),
+    ]
+    for c in edge_stores:
+        c.start()
+    stores += edge_stores
     for k in range(9):
-        partial[k * 128 : (k + 1) * 128, :] = jnp.transpose(
+        summed[k * 128 : (k + 1) * 128, :] = jnp.transpose(
             acc_space[:, k * 128 : (k + 1) * 128]
         ).astype(BF16)
     for k in range(3):
-        partial[(9 + k) * 128 : (10 + k) * 128, :] = acc_time[
+        summed[(9 + k) * 128 : (10 + k) * 128, :] = acc_time[
             :, k * 128 : (k + 1) * 128
         ].astype(BF16)
+    stores.append(pltpu.make_async_copy(summed, partial, sems.at[6]))
+    stores[-1].start()
+    for c in stores:
+        c.wait()
 
 
 def sum_kernel(scale, pieces, out):
@@ -224,7 +245,7 @@
             time[at : at + rows, :] = pieces[k].astype(F32)
 
 
-def outs_kernel(lat, act, got_a, got_b, w_time, out_f, out_r):
+def outs_kernel(lat, act, got_b, got_a, w_time, out_f, out_r):
     even = is_even("tm")
 
     def frame(t):
@@ -242,7 +263,7 @@
             out[t] = total.astype(BF16).reshape(4, 160, 128)
 
 
-def input_kernel(gp, got_a, got_b, fwd, rev, w_space, out, spread, back):
+def input_kernel(gp, got_b, got_a, fwd, rev, w_space, out, spread, back):
     even = is_even("tile")
     for i in range(3):
         for j in range(3):
@@ -272,45 +293,44 @@
     cots_a = swapped(cots_a, "tm", 0)
     row_b = swapped(row_b, "tile", 1)
     row_a = swapped(row_a, "tile", 0)
-    act, act_a, act_b, gp, gp_a, gp_b, partial = vmem_call(
+    act, gp, act_a, act_b, gp_a, gp_b, partial = vmem_call(
         front_kernel,
-        [
-            (cells, BF16), (pair, BF16), (pair, BF16),
-            (cells, BF16), (line, BF16), (line, BF16),
-            ((12 * channels, channels), BF16),
-        ],
+        [(cells, BF16)],
         [
             spread,
+            pltpu.VMEM(cells, BF16),
             pltpu.VMEM((9 * channels, channels), BF16),
             pltpu.VMEM((3 * channels, channels), BF16),
             pltpu.VMEM((6 * channels, channels), BF16),
             pltpu.VMEM((channels, 9 * channels), F32),
             pltpu.VMEM((channels, 3 * channels), F32),
-            pltpu.SemaphoreType.DMA((2,)),
+            pltpu.VMEM((12 * channels, channels), BF16),
+            pltpu.SemaphoreType.DMA((11,)),
         ],
         "front",
-        anywhere=2,
-    )(latent, row_a, row_b, cot_forward, cot_reverse, cots_a, cots_b, w_space, w_time)
+        in_hbm=2,
+        outs_hbm=[(cells, BF16)] + [(pair, BF16)] * 2 + [(line, BF16)] * 2 + [((12 * channels, channels), BF16)],
+    )(latent, row_b, row_a, cot_forward, cot_reverse, cots_b, cots_a, w_space, w_time)
 
     near, far = len(NEAR[0]), len(FAR[0])
     positions = frame_count * height * width_cells * lax.axis_size("tm") * lax.axis_size("tile")
     shares = sum_to_all(exchange(partial.reshape(near, -1, channels), NEAR), far)
-    shares, act_a, act_b, gp_a, gp_b = lax.optimization_barrier((shares, act_a, act_b, gp_a, gp_b))
-    shares = exchange(shares, FAR)
     act_b = swapped(act_b, "tm", 1)
     act_a = swapped(act_a, "tm", 0)
+    shares, gp_b, gp_a, act_b, act_a = lax.optimization_barrier((shares, gp_b, gp_a, act_b, act_a))
+    shares = exchange(shares, FAR)
     gp_b = swapped(gp_b, "tile", 1)
     gp_a = swapped(gp_a, "tile", 0)
     out_forward, out_reverse = vmem_call(outs_kernel, [(cells, BF16), (cells, BF16)], (), "outs")(
-        latent, act, act_a, act_b, w_time
+        latent, act, act_b, act_a, w_time
     )
-    shares, out_forward, out_reverse, gp_a, gp_b = lax.optimization_barrier(
-        (shares, out_forward, out_reverse, gp_a, gp_b)
+    shares, out_forward, out_reverse, gp_b, gp_a = lax.optimization_barrier(
+        (shares, out_forward, out_reverse, gp_b, gp_a)
     )
     whole = exchange(sum_to_all(shares, near, 1.0 / math.sqrt(positions)), NEAR)
     (grad_input,) = vmem_call(
         input_kernel, [(cells, BF16)], [spread, pltpu.VMEM((9 * channels, channels), BF16)], "grad_input"
-    )(gp, gp_a, gp_b, cot_forward, cot_reverse, w_space)
+    )(gp, gp_b, gp_a, cot_forward, cot_reverse, w_space)
     grad_spatial, grad_temporal = vmem_call(
         widen_kernel, [((9 * channels, channels), F32), ((3 * channels, channels), F32)], (), "widen"
     )(whole)

time: 96.9 us -> 97.6 us (level)
  blocking collectives: 16.9 us -> 0 us
  starting transfers between devices: 47.5 us -> 59.1 us
  waiting for transfers between devices: 14.2 us -> 18.7 us
  Pallas kernels: 13.5 us -> 17.6 us
  local copies, waits for them, and re-layouts: 3.27 us -> 0.69 us
    all_to_all x1 -> x0, blocking collectives: 16.9 us -> none  [exchange(): lax.all_to_all(pieces, BOTH, 0, 0, tiled=True, axis_index_groups=members)]
    ppermute x8, starting transfers between devices: 23.4 us -> 30.3 us  [swapped(): return lax.ppermute(value, axis, pairs)]
    all_to_all x2 -> x3, starting transfers between devices: 24.1 us -> 28.8 us  [exchange(): lax.all_to_all(pieces, BOTH, 0, 0, tiled=True, axis_index_groups=members)]
    all_to_all x2 -> x3, waiting for transfers between devices: 7.07 us -> 10.5 us  [exchange(): lax.all_to_all(pieces, BOTH, 0, 0, tiled=True, axis_index_groups=members)]
    unnamed x16, local copies, waits for them, and re-layouts: 3.27 us -> 0.69 us
    pallas_call x0 -> x1, Pallas kernels: none -> 2.28 us  [edges(): pl.pallas_call(edges_kernel, out_shape=tuple((jax.ShapeDtypeStruct(s, BF1...]
    pallas_call x7 -> x6, Pallas kernels: 13.5 us -> 15.3 us  [call(): pl.pallas_call(kernel, out_shape=tuple((jax.ShapeDtypeStruct(s, t) for s,...]
    ppermute x8, waiting for transfers between devices: 7.14 us -> 8.21 us  [swapped(): return lax.ppermute(value, axis, pairs)]
  transfers between devices with their start and end apart: 10 -> 11, of which waited for: 4 -> 6; matrix products, arithmetic and copies ran while one was open for 0% -> 0% of each run, Pallas kernels for 5% -> 7%
where the time goes in v3:
time: 97.6 us; the launch traced here: 96.9 us
  starting transfers between devices  59.1 us (61%)
  waiting for transfers between devices  18.7 us (19%)
  Pallas kernels  17.6 us (18%)
    ppermute x8, starting transfers between devices, swapped(): return lax.ppermute(value, axis, pairs)  30.3 us
    all_to_all x3, starting transfers between devices, exchange(): lax.all_to_all(pieces, BOTH, 0, 0, tiled=True, axis_index_groups=members)  28.8 us
    pallas_call x6, Pallas kernels, call(): pl.pallas_call(kernel, out_shape=tuple((jax.ShapeDtypeStruct(s, t) for s,...  15.3 us
    all_to_all x3, waiting for transfers between devices, exchange(): lax.all_to_all(pieces, BOTH, 0, 0, tiled=True, axis_index_groups=members)  10.5 us
    ppermute x8, waiting for transfers between devices, swapped(): return lax.ppermute(value, axis, pairs)  8.21 us
    pallas_call x1, Pallas kernels, edges(): pl.pallas_call(edges_kernel, out_shape=tuple((jax.ShapeDtypeStruct(s, BF1...  2.28 us
  transfers between devices with their start and end apart: 11, of which 6 were waited for; matrix products, arithmetic and copies ran while one was open for 0% of the time, Pallas kernels for 7%

profile of v3, /device:TPU:1, one launch (start us, length us, event | category | flops | bytes accessed | tf_op | source)
XLA Modules:
  0.0 96.9 jit_solution(1831841887304083158)
XLA Ops:
  0.6 0.0 copy-start.2
  0.6 0.0 copy-start.1
  0.7 0.0 copy-start
  0.7 2.3 %edges.1 = (bf16[2,4,160,128]{3,2,1,0:T(8,128)(2,1)}, bf16[2,4,160,128]{3,2,1,0:T(8,128)(2,1)}, bf16[4,160,128]{2,1,0:T(8,128)(2,1)}, bf16[4,160,128]{2,1,0:T(8,128)(2,1)}) custom-call(bf16[4,4,160,128]{3,2,1,0:T(8,128)(2,1)} %lat.5, bf16[4,4,160,128]{3,2,1,0:T(8,128)(2,1)} %fwd.5, bf16[4,4,160,128]{3,2,1,0:T(8,128)(2,1)} %rev.5), custom_call_target="tpu_custom_call" | custom-call | tf_op jit(solution)/shard_map/edges/pallas_call | solution.py:100
  2.9 0.7 collective-permute-start.2
  3.6 6.4 %collective-permute-start.3 = (bf16[2,4,160,128]{3,2,1,0:T(8,128)(2,1)}, bf16[2,4,160,128]{3,2,1,0:T(8,128)(2,1)S(1)}, u32[]{:S(2)}, u32[]{:S(2)}) collective-permute-start(bf16[2,4,160,128]{3,2,1,0:T(8,128)(2,1)} %get-tuple-element.33), channel_id=1, source_target_pairs={{0,8},{8,0},{16,24},{24,16},{32,40},{40,32},{48,56},{56,48},{64,72... | collective-permute-start | bytes 983048 | tf_op jit(solution)/shard_map/ppermute | solution.py:41
  10.0 6.9 %collective-permute-start = (bf16[4,160,128]{2,1,0:T(8,128)(2,1)}, bf16[4,160,128]{2,1,0:T(8,128)(2,1)S(1)}, u32[]{:S(2)}, u32[]{:S(2)}) collective-permute-start(bf16[4,160,128]{2,1,0:T(8,128)(2,1)} %get-tuple-element.30), channel_id=1, source_target_pairs={{1,2},{2,1},{3,4},{4,3},{5,6},{6,5},{9,10},{10,9},{11,12},{12,11},... | collective-permute-start | bytes 491528 | tf_op jit(solution)/shard_map/ppermute | solution.py:41
  17.0 1.9 %collective-permute-start.1 = (bf16[4,160,128]{2,1,0:T(8,128)(2,1)}, bf16[4,160,128]{2,1,0:T(8,128)(2,1)S(1)}, u32[]{:S(2)}, u32[]{:S(2)}) collective-permute-start(bf16[4,160,128]{2,1,0:T(8,128)(2,1)} %get-tuple-element.31), channel_id=1, source_target_pairs={{0,1},{1,0},{2,3},{3,2},{4,5},{5,4},{6,7},{7,6},{8,9},{9,8},{10,11... | collective-permute-start | bytes 491528 | tf_op jit(solution)/shard_map/ppermute | solution.py:41
  18.9 1.3 %collective-permute-done.row_b = bf16[4,160,128]{2,1,0:T(8,128)(2,1)S(1)} collective-permute-done((bf16[4,160,128]{2,1,0:T(8,128)(2,1)}, bf16[4,160,128]{2,1,0:T(8,128)(2,1)S(1)}, u32[]{:S(2)}, u32[]{:S(2)}) %collective-permute-start) | collective-permute-done | bytes 163872 | tf_op jit(solution)/shard_map/ppermute | solution.py:41
  20.2 0.3 collective-permute-done.1.row_a
  20.5 0.0 collective-permute-done.2.cots_b
  20.5 0.0 collective-permute-done.3.cots_a
  20.5 0.0 copy-done.2
  20.5 0.0 copy-done.1
  20.5 0.0 copy-done
  20.5 7.0 %front.1 = (bf16[4,4,160,128]{3,2,1,0:T(8,128)(2,1)S(1)}, bf16[4,4,160,128]{3,2,1,0:T(8,128)(2,1)}, bf16[2,4,160,128]{3,2,1,0:T(8,128)(2,1)}, bf16[2,4,160,128]{...) custom-call(bf16[4,4,160,128]{3,2,1,0:T(8,128)(2,1)S(1)} %copy-done, ...), custom_call_target="tpu_custom_call" | custom-call | tf_op jit(solution)/shard_map/front/pallas_call | solution.py:52
  27.5 7.9 %all-to-all-start = ((bf16[32,48,128]{2,1,0:T(8,128)(2,1)}), bf16[32,48,128]{2,1,0:T(8,128)(2,1)S(1)}, u32[]{:S(2)}, u32[]{:S(2)}) async-start(bf16[32,48,128]{2,1,0:T(8,128)(2,1)} %bitcast.9), calls=%async_computation | async-start | bytes 786432 | tf_op jit(solution)/shard_map/all_to_all | solution.py:33
  35.4 0.7 collective-permute-start.4
  36.1 5.7 %collective-permute-start.5 = (bf16[2,4,160,128]{3,2,1,0:T(8,128)(2,1)}, bf16[2,4,160,128]{3,2,1,0:T(8,128)(2,1)}, u32[]{:S(2)}, u32[]{:S(2)}) collective-permute-start(bf16[2,4,160,128]{3,2,1,0:T(8,128)(2,1)} %get-tuple-element.38), channel_id=1, source_target_pairs={{0,8},{8,0},{16,24},{24,16},{32,40},{40,32},{48,56},{56,48},{64,72... | collective-permute-start | bytes 983048 | tf_op jit(solution)/shard_map/ppermute | solution.py:41
  41.8 3.4 %all-to-all-done.pieces = bf16[32,48,128]{2,1,0:T(8,128)(2,1)S(1)} async-done(((bf16[32,48,128]{2,1,0:T(8,128)(2,1)}), bf16[32,48,128]{2,1,0:T(8,128)(2,1)S(1)}, u32[]{:S(2)}, u32[]{:S(2)}) %all-to-all-start) | async-done | bytes 393248 | tf_op jit(solution)/shard_map/all_to_all | solution.py:33
  45.2 0.7 share.2
  46.0 0.0 collective-permute-done.4.got_b
  46.0 3.9 %collective-permute-done.5.got_a = bf16[2,4,160,128]{3,2,1,0:T(8,128)(2,1)} collective-permute-done((bf16[2,4,160,128]{3,2,1,0:T(8,128)(2,1)}, bf16[2,4,160,128]{3,2,1,0:T(8,128)(2,1)}, u32[]{:S(2)}, u32[]{:S(2)}) %collective-permute-start.5) | collective-permute-done | bytes 327712 | tf_op jit(solution)/shard_map/ppermute | solution.py:41
  49.8 0.0 copy-start.5
  49.8 17.1 %all-to-all-start.1 = ((bf16[16,48,128]{2,1,0:T(8,128)(2,1)}), bf16[16,48,128]{2,1,0:T(8,128)(2,1)S(1)}, u32[]{:S(2)}, u32[]{:S(2)}) async-start(bf16[16,48,128]{2,1,0:T(8,128)(2,1)} %share.2), calls=%async_computation.1 | async-start | bytes 393216 | tf_op jit(solution)/shard_map/all_to_all | solution.py:33
  67.0 6.1 %collective-permute-start.6 = (bf16[4,160,128]{2,1,0:T(8,128)(2,1)}, bf16[4,160,128]{2,1,0:T(8,128)(2,1)S(1)}, u32[]{:S(2)}, u32[]{:S(2)}) collective-permute-start(bf16[4,160,128]{2,1,0:T(8,128)(2,1)} %get-tuple-element.45), channel_id=1, source_target_pairs={{1,2},{2,1},{3,4},{4,3},{5,6},{6,5},{9,10},{10,9},{11,12},{12,11},... | collective-permute-start | bytes 491528 | tf_op jit(solution)/shard_map/ppermute | solution.py:41
  73.1 1.9 %collective-permute-start.7 = (bf16[4,160,128]{2,1,0:T(8,128)(2,1)}, bf16[4,160,128]{2,1,0:T(8,128)(2,1)S(1)}, u32[]{:S(2)}, u32[]{:S(2)}) collective-permute-start(bf16[4,160,128]{2,1,0:T(8,128)(2,1)} %get-tuple-element.46), channel_id=1, source_target_pairs={{0,1},{1,0},{2,3},{3,2},{4,5},{5,4},{6,7},{7,6},{8,9},{9,8},{10,11... | collective-permute-start | bytes 491528 | tf_op jit(solution)/shard_map/ppermute | solution.py:41
  75.0 0.0 copy-done.5
  75.1 3.1 %outs.1 = (bf16[4,4,160,128]{3,2,1,0:T(8,128)(2,1)}, bf16[4,4,160,128]{3,2,1,0:T(8,128)(2,1)}) custom-call(bf16[4,4,160,128]{3,2,1,0:T(8,128)(2,1)S(1)} %copy-done, bf16[4,4,160,128]{3,2,1,0:T(8,128)(2,1)S(1)} %get-tuple-element.40.act, bf16[2,4,160,128]{3,2,1,0:T(8,128)(2,1)S(1)} %collective-permute-done.4.got_b, ...), custom_call_target="tpu_custom_call" | custom-call | tf_op jit(solution)/shard_map/outs/pallas_call | solution.py:52
  78.2 2.8 %collective-permute-done.6.got_b = bf16[4,160,128]{2,1,0:T(8,128)(2,1)S(1)} collective-permute-done((bf16[4,160,128]{2,1,0:T(8,128)(2,1)}, bf16[4,160,128]{2,1,0:T(8,128)(2,1)S(1)}, u32[]{:S(2)}, u32[]{:S(2)}) %collective-permute-start.6) | collective-permute-done | bytes 163872 | tf_op jit(solution)/shard_map/ppermute | solution.py:41
  80.9 0.0 collective-permute-done.7.got_a
  80.9 0.0 copy-start.6
  80.9 0.7 copy-done.6
  81.6 0.0 all-to-all-done.1.pieces
  81.6 0.0 copy-start.4
  81.6 0.8 share.3
  82.4 0.0 copy-start.3
  82.4 0.0 copy-start.7
  82.4 3.8 %all-to-all-start.2 = ((bf16[32,48,128]{2,1,0:T(8,128)(2,1)}), bf16[32,48,128]{2,1,0:T(8,128)(2,1)S(1)}, u32[]{:S(2)}, u32[]{:S(2)}) async-start(bf16[32,48,128]{2,1,0:T(8,128)(2,1)} %share.3), calls=%async_computation.2 | async-start | bytes 786432 | tf_op jit(solution)/shard_map/all_to_all | solution.py:33
  86.2 0.0 copy-done.4
  86.2 0.0 copy-done.3
  86.2 0.0 copy-done.7
  86.2 2.7 %grad_input.1 = bf16[4,4,160,128]{3,2,1,0:T(8,128)(2,1)} custom-call(bf16[4,4,160,128]{3,2,1,0:T(8,128)(2,1)S(1)} %copy-done.4, bf16[4,160,128]{2,1,0:T(8,128)(2,1)S(1)} %collective-permute-done.6.got_b, bf16[4,160,128]{2,1,0:T(8,128)(2,1)S(1)} %copy-done.7, bf16[4,4,160,128]{3,2,1,0:T(8,128)(2,1)S(1)} %copy-done.1, bf16[4,4,160,128]{3,2,1,0:T(8,128)(2,1)S(1)} %copy-done.2, ...), custom_call_target="tpu_custom_call" | custom-call | tf_op jit(solution)/shard_map/grad_input/pallas_call | solution.py:52
  89.0 7.1 %all-to-all-done.2.pieces = bf16[32,48,128]{2,1,0:T(8,128)(2,1)S(1)} async-done(((bf16[32,48,128]{2,1,0:T(8,128)(2,1)}), bf16[32,48,128]{2,1,0:T(8,128)(2,1)S(1)}, u32[]{:S(2)}, u32[]{:S(2)}) %all-to-all-start.2) | async-done | bytes 393248 | tf_op jit(solution)/shard_map/all_to_all | solution.py:33
  96.0 0.9 widen.1
Async XLA Ops:
  0.6 19.8 %copy-start.2 = (bf16[4,4,160,128]{3,2,1,0:T(8,128)(2,1)S(1)}, bf16[4,4,160,128]{3,2,1,0:T(8,128)(2,1)}, u32[]{:S(2)}) copy-start(bf16[4,4,160,128]{3,2,1,0:T(8,128)(2,1)} %rev.5) | copy-start | bytes 1966084
  0.6 19.8 %copy-start.1 = (bf16[4,4,160,128]{3,2,1,0:T(8,128)(2,1)S(1)}, bf16[4,4,160,128]{3,2,1,0:T(8,128)(2,1)}, u32[]{:S(2)}) copy-start(bf16[4,4,160,128]{3,2,1,0:T(8,128)(2,1)} %fwd.5) | copy-start | bytes 1966084
  0.7 19.8 %copy-start = (bf16[4,4,160,128]{3,2,1,0:T(8,128)(2,1)S(1)}, bf16[4,4,160,128]{3,2,1,0:T(8,128)(2,1)}, u32[]{:S(2)}) copy-start(bf16[4,4,160,128]{3,2,1,0:T(8,128)(2,1)} %lat.5) | copy-start | bytes 1966084
  2.9 17.5 %collective-permute-start.2 = (bf16[2,4,160,128]{3,2,1,0:T(8,128)(2,1)}, bf16[2,4,160,128]{3,2,1,0:T(8,128)(2,1)S(1)}, u32[]{:S(2)}, u32[]{:S(2)}) collective-permute-start(bf16[2,4,160,128]{3,2,1,0:T(8,128)(2,1)} %get-tuple-element.32), channel_id=1, source_target_pairs={{8,16},{16,8},{24,32},{32,24},{40,48},{48,40},{56,64},{64,56},{72,... | collective-permute-start | bytes 983048 | tf_op jit(solution)/shard_map/ppermute | solution.py:41
  3.6 16.8 %collective-permute-start.3 = (bf16[2,4,160,128]{3,2,1,0:T(8,128)(2,1)}, bf16[2,4,160,128]{3,2,1,0:T(8,128)(2,1)S(1)}, u32[]{:S(2)}, u32[]{:S(2)}) collective-permute-start(bf16[2,4,160,128]{3,2,1,0:T(8,128)(2,1)} %get-tuple-element.33), channel_id=1, source_target_pairs={{0,8},{8,0},{16,24},{24,16},{32,40},{40,32},{48,56},{56,48},{64,72... | collective-permute-start | bytes 983048 | tf_op jit(solution)/shard_map/ppermute | solution.py:41
  10.0 10.1 %collective-permute-start = (bf16[4,160,128]{2,1,0:T(8,128)(2,1)}, bf16[4,160,128]{2,1,0:T(8,128)(2,1)S(1)}, u32[]{:S(2)}, u32[]{:S(2)}) collective-permute-start(bf16[4,160,128]{2,1,0:T(8,128)(2,1)} %get-tuple-element.30), channel_id=1, source_target_pairs={{1,2},{2,1},{3,4},{4,3},{5,6},{6,5},{9,10},{10,9},{11,12},{12,11},... | collective-permute-start | bytes 491528 | tf_op jit(solution)/shard_map/ppermute | solution.py:41
  17.0 3.5 %collective-permute-start.1 = (bf16[4,160,128]{2,1,0:T(8,128)(2,1)}, bf16[4,160,128]{2,1,0:T(8,128)(2,1)S(1)}, u32[]{:S(2)}, u32[]{:S(2)}) collective-permute-start(bf16[4,160,128]{2,1,0:T(8,128)(2,1)} %get-tuple-element.31), channel_id=1, source_target_pairs={{0,1},{1,0},{2,3},{3,2},{4,5},{5,4},{6,7},{7,6},{8,9},{9,8},{10,11... | collective-permute-start | bytes 491528 | tf_op jit(solution)/shard_map/ppermute | solution.py:41
  27.5 17.7 %all-to-all-start = ((bf16[32,48,128]{2,1,0:T(8,128)(2,1)}), bf16[32,48,128]{2,1,0:T(8,128)(2,1)S(1)}, u32[]{:S(2)}, u32[]{:S(2)}) async-start(bf16[32,48,128]{2,1,0:T(8,128)(2,1)} %bitcast.9), calls=%async_computation | async-start | bytes 786432 | tf_op jit(solution)/shard_map/all_to_all | solution.py:33
  35.4 10.6 %collective-permute-start.4 = (bf16[2,4,160,128]{3,2,1,0:T(8,128)(2,1)}, bf16[2,4,160,128]{3,2,1,0:T(8,128)(2,1)S(1)}, u32[]{:S(2)}, u32[]{:S(2)}) collective-permute-start(bf16[2,4,160,128]{3,2,1,0:T(8,128)(2,1)} %get-tuple-element.37), channel_id=1, source_target_pairs={{8,16},{16,8},{24,32},{32,24},{40,48},{48,40},{56,64},{64,56},{72,... | collective-permute-start | bytes 983048 | tf_op jit(solution)/shard_map/ppermute | solution.py:41
  36.1 13.8 %collective-permute-start.5 = (bf16[2,4,160,128]{3,2,1,0:T(8,128)(2,1)}, bf16[2,4,160,128]{3,2,1,0:T(8,128)(2,1)}, u32[]{:S(2)}, u32[]{:S(2)}) collective-permute-start(bf16[2,4,160,128]{3,2,1,0:T(8,128)(2,1)} %get-tuple-element.38), channel_id=1, source_target_pairs={{0,8},{8,0},{16,24},{24,16},{32,40},{40,32},{48,56},{56,48},{64,72... | collective-permute-start | bytes 983048 | tf_op jit(solution)/shard_map/ppermute | solution.py:41
  49.8 25.2 %copy-start.5 = (bf16[3,128,128]{2,1,0:T(8,128)(2,1)S(1)}, bf16[3,128,128]{2,1,0:T(8,128)(2,1)}, u32[]{:S(2)}) copy-start(bf16[3,128,128]{2,1,0:T(8,128)(2,1)} %param.9) | copy-start | bytes 294916
  49.8 31.8 %all-to-all-start.1 = ((bf16[16,48,128]{2,1,0:T(8,128)(2,1)}), bf16[16,48,128]{2,1,0:T(8,128)(2,1)S(1)}, u32[]{:S(2)}, u32[]{:S(2)}) async-start(bf16[16,48,128]{2,1,0:T(8,128)(2,1)} %share.2), calls=%async_computation.1 | async-start | bytes 393216 | tf_op jit(solution)/shard_map/all_to_all | solution.py:33
  67.0 13.9 %collective-permute-start.6 = (bf16[4,160,128]{2,1,0:T(8,128)(2,1)}, bf16[4,160,128]{2,1,0:T(8,128)(2,1)S(1)}, u32[]{:S(2)}, u32[]{:S(2)}) collective-permute-start(bf16[4,160,128]{2,1,0:T(8,128)(2,1)} %get-tuple-element.45), channel_id=1, source_target_pairs={{1,2},{2,1},{3,4},{4,3},{5,6},{6,5},{9,10},{10,9},{11,12},{12,11},... | collective-permute-start | bytes 491528 | tf_op jit(solution)/shard_map/ppermute | solution.py:41
  73.1 7.8 %collective-permute-start.7 = (bf16[4,160,128]{2,1,0:T(8,128)(2,1)}, bf16[4,160,128]{2,1,0:T(8,128)(2,1)S(1)}, u32[]{:S(2)}, u32[]{:S(2)}) collective-permute-start(bf16[4,160,128]{2,1,0:T(8,128)(2,1)} %get-tuple-element.46), channel_id=1, source_target_pairs={{0,1},{1,0},{2,3},{3,2},{4,5},{5,4},{6,7},{7,6},{8,9},{9,8},{10,11... | collective-permute-start | bytes 491528 | tf_op jit(solution)/shard_map/ppermute | solution.py:41
  80.9 0.7 copy-start.6
  81.6 4.6 %copy-start.4 = (bf16[4,4,160,128]{3,2,1,0:T(8,128)(2,1)S(1)}, bf16[4,4,160,128]{3,2,1,0:T(8,128)(2,1)}, u32[]{:S(2)}) copy-start(bf16[4,4,160,128]{3,2,1,0:T(8,128)(2,1)} %get-tuple-element.49.gp) | copy-start | bytes 1966084
  82.4 3.8 %copy-start.3 = (bf16[3,3,128,128]{3,2,1,0:T(8,128)(2,1)S(1)}, bf16[3,3,128,128]{3,2,1,0:T(8,128)(2,1)}, u32[]{:S(2)}) copy-start(bf16[3,3,128,128]{3,2,1,0:T(8,128)(2,1)} %param.8) | copy-start | bytes 884740
  82.4 3.8 %copy-start.7 = (bf16[4,160,128]{2,1,0:T(8,128)(2,1)S(1)}, bf16[4,160,128]{2,1,0:T(8,128)(2,1)}, u32[]{:S(2)}) copy-start(bf16[4,160,128]{2,1,0:T(8,128)(2,1)} %copy-done.6) | copy-start | bytes 491524
  82.4 13.6 %all-to-all-start.2 = ((bf16[32,48,128]{2,1,0:T(8,128)(2,1)}), bf16[32,48,128]{2,1,0:T(8,128)(2,1)S(1)}, u32[]{:S(2)}, u32[]{:S(2)}) async-start(bf16[32,48,128]{2,1,0:T(8,128)(2,1)} %share.3), calls=%async_computation.2 | async-start | bytes 786432 | tf_op jit(solution)/shard_map/all_to_all | solution.py:33

commit v4 on v3

--- a/solution.py
+++ b/solution.py
@@ -204,16 +204,17 @@
     for c in edge_stores:
         c.start()
     stores += edge_stores
-    for k in range(9):
-        summed[k * 128 : (k + 1) * 128, :] = jnp.transpose(
-            acc_space[:, k * 128 : (k + 1) * 128]
-        ).astype(BF16)
     for k in range(3):
-        summed[(9 + k) * 128 : (10 + k) * 128, :] = acc_time[
-            :, k * 128 : (k + 1) * 128
-        ].astype(BF16)
-    stores.append(pltpu.make_async_copy(summed, partial, sems.at[6]))
-    stores[-1].start()
+        summed[(9 + k) * 128 : (10 + k) * 128, :] = acc_time[:, k * 128 : (k + 1) * 128].astype(BF16)
+    for part in (3, 0, 1, 2):
+        if part < 3:
+            for k in range(part * 3, part * 3 + 3):
+                summed[k * 128 : (k + 1) * 128, :] = jnp.transpose(
+                    acc_space[:, k * 128 : (k + 1) * 128]
+                ).astype(BF16)
+        rows = pl.ds(part * 384, 384)
+        stores.append(pltpu.make_async_copy(summed.at[rows], partial.at[rows], sems.at[11 + part]))
+        stores[-1].start()
     for c in stores:
         c.wait()
 
@@ -305,7 +306,7 @@
             pltpu.VMEM((channels, 9 * channels), F32),
             pltpu.VMEM((channels, 3 * channels), F32),
             pltpu.VMEM((12 * channels, channels), BF16),
-            pltpu.SemaphoreType.DMA((11,)),
+            pltpu.SemaphoreType.DMA((15,)),
         ],
         "front",
         in_hbm=2,
@@ -317,17 +318,16 @@
     shares = sum_to_all(exchange(partial.reshape(near, -1, channels), NEAR), far)
     act_b = swapped(act_b, "tm", 1)
     act_a = swapped(act_a, "tm", 0)
-    shares, gp_b, gp_a, act_b, act_a = lax.optimization_barrier((shares, gp_b, gp_a, act_b, act_a))
-    shares = exchange(shares, FAR)
-    gp_b = swapped(gp_b, "tile", 1)
-    gp_a = swapped(gp_a, "tile", 0)
     out_forward, out_reverse = vmem_call(outs_kernel, [(cells, BF16), (cells, BF16)], (), "outs")(
         latent, act, act_b, act_a, w_time
     )
-    shares, out_forward, out_reverse, gp_b, gp_a = lax.optimization_barrier(
-        (shares, out_forward, out_reverse, gp_b, gp_a)
-    )
-    whole = exchange(sum_to_all(shares, near, 1.0 / math.sqrt(positions)), NEAR)
+    gp_b, gp_a, out_forward, out_reverse = lax.optimization_barrier((gp_b, gp_a, out_forward, out_reverse))
+    gp_b = swapped(gp_b, "tile", 1)
+    gp_a = swapped(gp_a, "tile", 0)
+    shares = exchange(shares, FAR)
+    shares, gp_b, gp_a = lax.optimization_barrier((shares, gp_b, gp_a))
+    shares = sum_to_all(shares, near, 1.0 / math.sqrt(positions))
+    whole = exchange(shares, NEAR)
     (grad_input,) = vmem_call(
         input_kernel, [(cells, BF16)], [spread, pltpu.VMEM((9 * channels, channels), BF16)], "grad_input"
     )(gp, gp_b, gp_a, cot_forward, cot_reverse, w_space)

time: 97.6 us -> 91.3 us (0.935)
  starting transfers between devices: 59.1 us -> 56.1 us
  waiting for transfers between devices: 18.7 us -> 16.1 us
    ppermute x8, waiting for transfers between devices: 8.21 us -> 5.55 us  [swapped(): return lax.ppermute(value, axis, pairs)]
    all_to_all x3, starting transfers between devices: 28.8 us -> 26.8 us  [exchange(): lax.all_to_all(pieces, BOTH, 0, 0, tiled=True, axis_index_groups=members)]
    ppermute x8, starting transfers between devices: 30.3 us -> 29.2 us  [swapped(): return lax.ppermute(value, axis, pairs)]
  transfers between devices with their start and end apart: 11 -> 11, of which waited for: 6 -> 5; matrix products, arithmetic and copies ran while one was open for 0% -> 0% of each run, Pallas kernels for 7% -> 7%
where the time goes in v4:
time: 91.3 us; the launch traced here: 90.7 us
  starting transfers between devices  56.1 us (61%)
  Pallas kernels  17.7 us (19%)
  waiting for transfers between devices  16.1 us (18%)
    ppermute x8, starting transfers between devices, swapped(): return lax.ppermute(value, axis, pairs)  29.2 us
    all_to_all x3, starting transfers between devices, exchange(): lax.all_to_all(pieces, BOTH, 0, 0, tiled=True, axis_index_groups=members)  26.8 us
    pallas_call x6, Pallas kernels, call(): pl.pallas_call(kernel, out_shape=tuple((jax.ShapeDtypeStruct(s, t) for s,...  15.4 us
    all_to_all x3, waiting for transfers between devices, exchange(): lax.all_to_all(pieces, BOTH, 0, 0, tiled=True, axis_index_groups=members)  10.5 us
    ppermute x8, waiting for transfers between devices, swapped(): return lax.ppermute(value, axis, pairs)  5.55 us
    pallas_call x1, Pallas kernels, edges(): pl.pallas_call(edges_kernel, out_shape=tuple((jax.ShapeDtypeStruct(s, BF1...  2.28 us
  transfers between devices with their start and end apart: 11, of which 5 were waited for; matrix products, arithmetic and copies ran while one was open for 0% of the time, Pallas kernels for 7%

profile of v4, /device:TPU:1, one launch (start us, length us, event | category | flops | bytes accessed | tf_op | source)
XLA Modules:
  0.0 90.7 jit_solution(15926556514218437980)
XLA Ops:
  0.6 0.0 copy-start.2
  0.6 0.0 copy-start.1
  0.7 0.0 copy-start
  0.7 2.3 %edges.1 = (bf16[2,4,160,128]{3,2,1,0:T(8,128)(2,1)}, bf16[2,4,160,128]{3,2,1,0:T(8,128)(2,1)}, bf16[4,160,128]{2,1,0:T(8,128)(2,1)}, bf16[4,160,128]{2,1,0:T(8,128)(2,1)}) custom-call(bf16[4,4,160,128]{3,2,1,0:T(8,128)(2,1)} %lat.5, bf16[4,4,160,128]{3,2,1,0:T(8,128)(2,1)} %fwd.5, bf16[4,4,160,128]{3,2,1,0:T(8,128)(2,1)} %rev.5), custom_call_target="tpu_custom_call" | custom-call | tf_op jit(solution)/shard_map/edges/pallas_call | solution.py:100
  2.9 0.7 collective-permute-start.2
  3.6 6.4 %collective-permute-start.3 = (bf16[2,4,160,128]{3,2,1,0:T(8,128)(2,1)}, bf16[2,4,160,128]{3,2,1,0:T(8,128)(2,1)S(1)}, u32[]{:S(2)}, u32[]{:S(2)}) collective-permute-start(bf16[2,4,160,128]{3,2,1,0:T(8,128)(2,1)} %get-tuple-element.30), channel_id=1, source_target_pairs={{0,8},{8,0},{16,24},{24,16},{32,40},{40,32},{48,56},{56,48},{64,72... | collective-permute-start | bytes 983048 | tf_op jit(solution)/shard_map/ppermute | solution.py:41
  10.0 6.9 %collective-permute-start = (bf16[4,160,128]{2,1,0:T(8,128)(2,1)}, bf16[4,160,128]{2,1,0:T(8,128)(2,1)S(1)}, u32[]{:S(2)}, u32[]{:S(2)}) collective-permute-start(bf16[4,160,128]{2,1,0:T(8,128)(2,1)} %get-tuple-element.27), channel_id=1, source_target_pairs={{1,2},{2,1},{3,4},{4,3},{5,6},{6,5},{9,10},{10,9},{11,12},{12,11},... | collective-permute-start | bytes 491528 | tf_op jit(solution)/shard_map/ppermute | solution.py:41
  17.0 1.9 %collective-permute-start.1 = (bf16[4,160,128]{2,1,0:T(8,128)(2,1)}, bf16[4,160,128]{2,1,0:T(8,128)(2,1)S(1)}, u32[]{:S(2)}, u32[]{:S(2)}) collective-permute-start(bf16[4,160,128]{2,1,0:T(8,128)(2,1)} %get-tuple-element.28), channel_id=1, source_target_pairs={{0,1},{1,0},{2,3},{3,2},{4,5},{5,4},{6,7},{7,6},{8,9},{9,8},{10,11... | collective-permute-start | bytes 491528 | tf_op jit(solution)/shard_map/ppermute | solution.py:41
  18.9 1.3 %collective-permute-done.row_b = bf16[4,160,128]{2,1,0:T(8,128)(2,1)S(1)} collective-permute-done((bf16[4,160,128]{2,1,0:T(8,128)(2,1)}, bf16[4,160,128]{2,1,0:T(8,128)(2,1)S(1)}, u32[]{:S(2)}, u32[]{:S(2)}) %collective-permute-start) | collective-permute-done | bytes 163872 | tf_op jit(solution)/shard_map/ppermute | solution.py:41
  20.2 0.3 collective-permute-done.1.row_a
  20.5 0.0 collective-permute-done.2.cots_b
  20.5 0.0 collective-permute-done.3.cots_a
  20.5 0.0 copy-done.2
  20.5 0.0 copy-done.1
  20.5 0.0 copy-done
  20.5 7.0 %front.1 = (bf16[4,4,160,128]{3,2,1,0:T(8,128)(2,1)S(1)}, bf16[4,4,160,128]{3,2,1,0:T(8,128)(2,1)}, bf16[2,4,160,128]{3,2,1,0:T(8,128)(2,1)}, bf16[2,4,160,128]{...) custom-call(bf16[4,4,160,128]{3,2,1,0:T(8,128)(2,1)S(1)} %copy-done, ...), custom_call_target="tpu_custom_call" | custom-call | tf_op jit(solution)/shard_map/front/pallas_call | solution.py:52
  27.6 7.9 %all-to-all-start = ((bf16[32,48,128]{2,1,0:T(8,128)(2,1)}), bf16[32,48,128]{2,1,0:T(8,128)(2,1)S(1)}, u32[]{:S(2)}, u32[]{:S(2)}) async-start(bf16[32,48,128]{2,1,0:T(8,128)(2,1)} %bitcast.9), calls=%async_computation | async-start | bytes 786432 | tf_op jit(solution)/shard_map/all_to_all | solution.py:33
  35.4 0.7 collective-permute-start.4
  36.1 5.7 %collective-permute-start.5 = (bf16[2,4,160,128]{3,2,1,0:T(8,128)(2,1)}, bf16[2,4,160,128]{3,2,1,0:T(8,128)(2,1)}, u32[]{:S(2)}, u32[]{:S(2)}) collective-permute-start(bf16[2,4,160,128]{3,2,1,0:T(8,128)(2,1)} %get-tuple-element.35), channel_id=1, source_target_pairs={{0,8},{8,0},{16,24},{24,16},{32,40},{40,32},{48,56},{56,48},{64,72... | collective-permute-start | bytes 983048 | tf_op jit(solution)/shard_map/ppermute | solution.py:41
  41.8 3.4 %all-to-all-done.pieces = bf16[32,48,128]{2,1,0:T(8,128)(2,1)S(1)} async-done(((bf16[32,48,128]{2,1,0:T(8,128)(2,1)}), bf16[32,48,128]{2,1,0:T(8,128)(2,1)S(1)}, u32[]{:S(2)}, u32[]{:S(2)}) %all-to-all-start) | async-done | bytes 393248 | tf_op jit(solution)/shard_map/all_to_all | solution.py:33
  45.3 0.7 share.2
  46.0 0.0 copy-start.5
  46.0 15.2 %all-to-all-start.1 = ((bf16[16,48,128]{2,1,0:T(8,128)(2,1)}), bf16[16,48,128]{2,1,0:T(8,128)(2,1)S(1)}, u32[]{:S(2)}, u32[]{:S(2)}) async-start(bf16[16,48,128]{2,1,0:T(8,128)(2,1)} %share.2), calls=%async_computation.1 | async-start | bytes 393216 | tf_op jit(solution)/shard_map/all_to_all | solution.py:33
  61.2 0.0 collective-permute-done.4.got_b
  61.2 0.0 collective-permute-done.5.got_a
  61.2 0.0 copy-done.5
  61.2 0.0 copy-start.7
  61.2 0.0 copy-start.6
  61.2 3.2 %outs.1 = (bf16[4,4,160,128]{3,2,1,0:T(8,128)(2,1)}, bf16[4,4,160,128]{3,2,1,0:T(8,128)(2,1)}) custom-call(bf16[4,4,160,128]{3,2,1,0:T(8,128)(2,1)S(1)} %copy-done, bf16[4,4,160,128]{3,2,1,0:T(8,128)(2,1)S(1)} %get-tuple-element.33.act, bf16[2,4,160,128]{3,2,1,0:T(8,128)(2,1)S(1)} %collective-permute-done.4.got_b, ...), custom_call_target="tpu_custom_call" | custom-call | tf_op jit(solution)/shard_map/outs/pallas_call | solution.py:52
  64.4 0.0 copy-done.7
  64.4 0.0 copy-start.4
  64.4 5.0 %collective-permute-start.6 = (bf16[4,160,128]{2,1,0:T(8,128)(2,1)S(1)}, bf16[4,160,128]{2,1,0:T(8,128)(2,1)S(1)}, u32[]{:S(2)}, u32[]{:S(2)}) collective-permute-start(bf16[4,160,128]{2,1,0:T(8,128)(2,1)S(1)} %copy-done.7), channel_id=1, source_target_pairs={{1,2},{2,1},{3,4},{4,3},{5,6},{6,5},{9,10},{10,9},{11,12},{12,11},... | collective-permute-start | bytes 491528 | tf_op jit(solution)/shard_map/ppermute | solution.py:41
  69.4 0.0 copy-done.6
  69.4 1.9 %collective-permute-start.7 = (bf16[4,160,128]{2,1,0:T(8,128)(2,1)S(1)}, bf16[4,160,128]{2,1,0:T(8,128)(2,1)S(1)}, u32[]{:S(2)}, u32[]{:S(2)}) collective-permute-start(bf16[4,160,128]{2,1,0:T(8,128)(2,1)S(1)} %copy-done.6), channel_id=1, source_target_pairs={{0,1},{1,0},{2,3},{3,2},{4,5},{5,4},{6,7},{7,6},{8,9},{9,8},{10,11... | collective-permute-start | bytes 491528 | tf_op jit(solution)/shard_map/ppermute | solution.py:41
  71.4 4.0 %collective-permute-done.6.got_b = bf16[4,160,128]{2,1,0:T(8,128)(2,1)S(1)} collective-permute-done((bf16[4,160,128]{2,1,0:T(8,128)(2,1)S(1)}, bf16[4,160,128]{2,1,0:T(8,128)(2,1)S(1)}, u32[]{:S(2)}, u32[]{:S(2)}) %collective-permute-start.6) | collective-permute-done | bytes 163872 | tf_op jit(solution)/shard_map/ppermute | solution.py:41
  75.3 0.0 collective-permute-done.7.got_a
  75.3 0.0 all-to-all-done.1.pieces
  75.3 0.8 share.3
  76.1 0.0 copy-start.3
  76.1 3.8 %all-to-all-start.2 = ((bf16[32,48,128]{2,1,0:T(8,128)(2,1)}), bf16[32,48,128]{2,1,0:T(8,128)(2,1)S(1)}, u32[]{:S(2)}, u32[]{:S(2)}) async-start(bf16[32,48,128]{2,1,0:T(8,128)(2,1)} %share.3), calls=%async_computation.2 | async-start | bytes 786432 | tf_op jit(solution)/shard_map/all_to_all | solution.py:33
  79.9 0.0 copy-done.4
  79.9 0.0 copy-done.3
  79.9 2.7 %grad_input.1 = bf16[4,4,160,128]{3,2,1,0:T(8,128)(2,1)} custom-call(bf16[4,4,160,128]{3,2,1,0:T(8,128)(2,1)S(1)} %copy-done.4, bf16[4,160,128]{2,1,0:T(8,128)(2,1)S(1)} %collective-permute-done.6.got_b, bf16[4,160,128]{2,1,0:T(8,128)(2,1)S(1)} %collective-permute-done.7.got_a, bf16[4,4,160,128]{3,2,1,0:T(8,128)(2,1)S(1)} %copy-done.1, ...), custom_call_target="tpu_custom_call" | custom-call | tf_op jit(solution)/shard_map/grad_input/pallas_call | solution.py:52
  82.7 7.1 %all-to-all-done.2.pieces = bf16[32,48,128]{2,1,0:T(8,128)(2,1)S(1)} async-done(((bf16[32,48,128]{2,1,0:T(8,128)(2,1)}), bf16[32,48,128]{2,1,0:T(8,128)(2,1)S(1)}, u32[]{:S(2)}, u32[]{:S(2)}) %all-to-all-start.2) | async-done | bytes 393248 | tf_op jit(solution)/shard_map/all_to_all | solution.py:33
  89.8 0.9 %widen.1 = (f32[1152,128]{1,0:T(8,128)}, f32[384,128]{1,0:T(8,128)}) custom-call(bf16[32,48,128]{2,1,0:T(8,128)(2,1)S(1)} %all-to-all-done.2.pieces), custom_call_target="tpu_custom_call" | custom-call | tf_op jit(solution)/shard_map/widen/pallas_call | solution.py:52
Async XLA Ops:
  0.6 19.8 %copy-start.2 = (bf16[4,4,160,128]{3,2,1,0:T(8,128)(2,1)S(1)}, bf16[4,4,160,128]{3,2,1,0:T(8,128)(2,1)}, u32[]{:S(2)}) copy-start(bf16[4,4,160,128]{3,2,1,0:T(8,128)(2,1)} %rev.5) | copy-start | bytes 1966084
  0.6 19.8 %copy-start.1 = (bf16[4,4,160,128]{3,2,1,0:T(8,128)(2,1)S(1)}, bf16[4,4,160,128]{3,2,1,0:T(8,128)(2,1)}, u32[]{:S(2)}) copy-start(bf16[4,4,160,128]{3,2,1,0:T(8,128)(2,1)} %fwd.5) | copy-start | bytes 1966084
  0.7 19.8 %copy-start = (bf16[4,4,160,128]{3,2,1,0:T(8,128)(2,1)S(1)}, bf16[4,4,160,128]{3,2,1,0:T(8,128)(2,1)}, u32[]{:S(2)}) copy-start(bf16[4,4,160,128]{3,2,1,0:T(8,128)(2,1)} %lat.5) | copy-start | bytes 1966084
  2.9 17.5 %collective-permute-start.2 = (bf16[2,4,160,128]{3,2,1,0:T(8,128)(2,1)}, bf16[2,4,160,128]{3,2,1,0:T(8,128)(2,1)S(1)}, u32[]{:S(2)}, u32[]{:S(2)}) collective-permute-start(bf16[2,4,160,128]{3,2,1,0:T(8,128)(2,1)} %get-tuple-element.29), channel_id=1, source_target_pairs={{8,16},{16,8},{24,32},{32,24},{40,48},{48,40},{56,64},{64,56},{72,... | collective-permute-start | bytes 983048 | tf_op jit(solution)/shard_map/ppermute | solution.py:41
  3.6 16.8 %collective-permute-start.3 = (bf16[2,4,160,128]{3,2,1,0:T(8,128)(2,1)}, bf16[2,4,160,128]{3,2,1,0:T(8,128)(2,1)S(1)}, u32[]{:S(2)}, u32[]{:S(2)}) collective-permute-start(bf16[2,4,160,128]{3,2,1,0:T(8,128)(2,1)} %get-tuple-element.30), channel_id=1, source_target_pairs={{0,8},{8,0},{16,24},{24,16},{32,40},{40,32},{48,56},{56,48},{64,72... | collective-permute-start | bytes 983048 | tf_op jit(solution)/shard_map/ppermute | solution.py:41
  10.0 10.1 %collective-permute-start = (bf16[4,160,128]{2,1,0:T(8,128)(2,1)}, bf16[4,160,128]{2,1,0:T(8,128)(2,1)S(1)}, u32[]{:S(2)}, u32[]{:S(2)}) collective-permute-start(bf16[4,160,128]{2,1,0:T(8,128)(2,1)} %get-tuple-element.27), channel_id=1, source_target_pairs={{1,2},{2,1},{3,4},{4,3},{5,6},{6,5},{9,10},{10,9},{11,12},{12,11},... | collective-permute-start | bytes 491528 | tf_op jit(solution)/shard_map/ppermute | solution.py:41
  17.0 3.5 %collective-permute-start.1 = (bf16[4,160,128]{2,1,0:T(8,128)(2,1)}, bf16[4,160,128]{2,1,0:T(8,128)(2,1)S(1)}, u32[]{:S(2)}, u32[]{:S(2)}) collective-permute-start(bf16[4,160,128]{2,1,0:T(8,128)(2,1)} %get-tuple-element.28), channel_id=1, source_target_pairs={{0,1},{1,0},{2,3},{3,2},{4,5},{5,4},{6,7},{7,6},{8,9},{9,8},{10,11... | collective-permute-start | bytes 491528 | tf_op jit(solution)/shard_map/ppermute | solution.py:41
  27.6 17.7 %all-to-all-start = ((bf16[32,48,128]{2,1,0:T(8,128)(2,1)}), bf16[32,48,128]{2,1,0:T(8,128)(2,1)S(1)}, u32[]{:S(2)}, u32[]{:S(2)}) async-start(bf16[32,48,128]{2,1,0:T(8,128)(2,1)} %bitcast.9), calls=%async_computation | async-start | bytes 786432 | tf_op jit(solution)/shard_map/all_to_all | solution.py:33
  35.4 25.8 %collective-permute-start.4 = (bf16[2,4,160,128]{3,2,1,0:T(8,128)(2,1)}, bf16[2,4,160,128]{3,2,1,0:T(8,128)(2,1)S(1)}, u32[]{:S(2)}, u32[]{:S(2)}) collective-permute-start(bf16[2,4,160,128]{3,2,1,0:T(8,128)(2,1)} %get-tuple-element.34), channel_id=1, source_target_pairs={{8,16},{16,8},{24,32},{32,24},{40,48},{48,40},{56,64},{64,56},{72,... | collective-permute-start | bytes 983048 | tf_op jit(solution)/shard_map/ppermute | solution.py:41
  36.1 25.1 %collective-permute-start.5 = (bf16[2,4,160,128]{3,2,1,0:T(8,128)(2,1)}, bf16[2,4,160,128]{3,2,1,0:T(8,128)(2,1)}, u32[]{:S(2)}, u32[]{:S(2)}) collective-permute-start(bf16[2,4,160,128]{3,2,1,0:T(8,128)(2,1)} %get-tuple-element.35), channel_id=1, source_target_pairs={{0,8},{8,0},{16,24},{24,16},{32,40},{40,32},{48,56},{56,48},{64,72... | collective-permute-start | bytes 983048 | tf_op jit(solution)/shard_map/ppermute | solution.py:41
  46.0 15.2 %copy-start.5 = (bf16[3,128,128]{2,1,0:T(8,128)(2,1)S(1)}, bf16[3,128,128]{2,1,0:T(8,128)(2,1)}, u32[]{:S(2)}) copy-start(bf16[3,128,128]{2,1,0:T(8,128)(2,1)} %param.9) | copy-start | bytes 294916
  46.0 29.3 %all-to-all-start.1 = ((bf16[16,48,128]{2,1,0:T(8,128)(2,1)}), bf16[16,48,128]{2,1,0:T(8,128)(2,1)S(1)}, u32[]{:S(2)}, u32[]{:S(2)}) async-start(bf16[16,48,128]{2,1,0:T(8,128)(2,1)} %share.2), calls=%async_computation.1 | async-start | bytes 393216 | tf_op jit(solution)/shard_map/all_to_all | solution.py:33
  61.2 3.2 %copy-start.7 = (bf16[4,160,128]{2,1,0:T(8,128)(2,1)S(1)}, bf16[4,160,128]{2,1,0:T(8,128)(2,1)}, u32[]{:S(2)}) copy-start(bf16[4,160,128]{2,1,0:T(8,128)(2,1)} %get-tuple-element.42) | copy-start | bytes 491524
  61.2 8.2 %copy-start.6 = (bf16[4,160,128]{2,1,0:T(8,128)(2,1)S(1)}, bf16[4,160,128]{2,1,0:T(8,128)(2,1)}, u32[]{:S(2)}) copy-start(bf16[4,160,128]{2,1,0:T(8,128)(2,1)} %get-tuple-element.43) | copy-start | bytes 491524
  64.4 15.5 %copy-start.4 = (bf16[4,4,160,128]{3,2,1,0:T(8,128)(2,1)S(1)}, bf16[4,4,160,128]{3,2,1,0:T(8,128)(2,1)}, u32[]{:S(2)}) copy-start(bf16[4,4,160,128]{3,2,1,0:T(8,128)(2,1)} %get-tuple-element.40.gp) | copy-start | bytes 1966084
  64.4 10.9 %collective-permute-start.6 = (bf16[4,160,128]{2,1,0:T(8,128)(2,1)S(1)}, bf16[4,160,128]{2,1,0:T(8,128)(2,1)S(1)}, u32[]{:S(2)}, u32[]{:S(2)}) collective-permute-start(bf16[4,160,128]{2,1,0:T(8,128)(2,1)S(1)} %copy-done.7), channel_id=1, source_target_pairs={{1,2},{2,1},{3,4},{4,3},{5,6},{6,5},{9,10},{10,9},{11,12},{12,11},... | collective-permute-start | bytes 491528 | tf_op jit(solution)/shard_map/ppermute | solution.py:41
  69.4 5.9 %collective-permute-start.7 = (bf16[4,160,128]{2,1,0:T(8,128)(2,1)S(1)}, bf16[4,160,128]{2,1,0:T(8,128)(2,1)S(1)}, u32[]{:S(2)}, u32[]{:S(2)}) collective-permute-start(bf16[4,160,128]{2,1,0:T(8,128)(2,1)S(1)} %copy-done.6), channel_id=1, source_target_pairs={{0,1},{1,0},{2,3},{3,2},{4,5},{5,4},{6,7},{7,6},{8,9},{9,8},{10,11... | collective-permute-start | bytes 491528 | tf_op jit(solution)/shard_map/ppermute | solution.py:41
  76.1 3.8 %copy-start.3 = (bf16[3,3,128,128]{3,2,1,0:T(8,128)(2,1)S(1)}, bf16[3,3,128,128]{3,2,1,0:T(8,128)(2,1)}, u32[]{:S(2)}) copy-start(bf16[3,3,128,128]{3,2,1,0:T(8,128)(2,1)} %param.8) | copy-start | bytes 884740
  76.1 13.6 %all-to-all-start.2 = ((bf16[32,48,128]{2,1,0:T(8,128)(2,1)}), bf16[32,48,128]{2,1,0:T(8,128)(2,1)S(1)}, u32[]{:S(2)}, u32[]{:S(2)}) async-start(bf16[32,48,128]{2,1,0:T(8,128)(2,1)} %share.3), calls=%async_computation.2 | async-start | bytes 786432 | tf_op jit(solution)/shard_map/all_to_all | solution.py:33

commit v5 on v4

--- a/solution.py
+++ b/solution.py
@@ -45,7 +45,7 @@
     return lax.rem(lax.axis_index(axis), 2) == 0
 
 
-def vmem_call(kernel, outs, scratch=(), name=None, in_hbm=0, outs_hbm=()):
+def vmem_call(kernel, outs, scratch=(), name=None, in_hbm=0, outs_hbm=(), cost=None):
     space = pl.BlockSpec(memory_space=pltpu.VMEM)
 
     def call(*args):
@@ -60,6 +60,7 @@
             scratch_shapes=list(scratch),
             compiler_params=pltpu.CompilerParams(vmem_limit_bytes=48 << 20),
             name=name,
+            cost_estimate=cost,
         )(*args[: len(args) - in_hbm], *(held(a) for a in args[len(args) - in_hbm :]))
 
     return call
@@ -318,16 +319,16 @@
     shares = sum_to_all(exchange(partial.reshape(near, -1, channels), NEAR), far)
     act_b = swapped(act_b, "tm", 1)
     act_a = swapped(act_a, "tm", 0)
-    out_forward, out_reverse = vmem_call(outs_kernel, [(cells, BF16), (cells, BF16)], (), "outs")(
+    shares = exchange(shares, FAR)
+    out_forward, out_reverse = vmem_call(outs_kernel, [(cells, BF16), (cells, BF16)], (), "outs", cost=pl.CostEstimate(flops=8000000000, bytes_accessed=6 << 20, transcendentals=0))(
         latent, act, act_b, act_a, w_time
     )
-    gp_b, gp_a, out_forward, out_reverse = lax.optimization_barrier((gp_b, gp_a, out_forward, out_reverse))
+    shares, out_forward, out_reverse = lax.optimization_barrier((shares, out_forward, out_reverse))
+    shares = sum_to_all(shares, near, 1.0 / math.sqrt(positions))
+    shares, gp_b, gp_a = lax.optimization_barrier((shares, gp_b, gp_a))
+    whole = exchange(shares, NEAR)
     gp_b = swapped(gp_b, "tile", 1)
     gp_a = swapped(gp_a, "tile", 0)
-    shares = exchange(shares, FAR)
-    shares, gp_b, gp_a = lax.optimization_barrier((shares, gp_b, gp_a))
-    shares = sum_to_all(shares, near, 1.0 / math.sqrt(positions))
-    whole = exchange(shares, NEAR)
     (grad_input,) = vmem_call(
         input_kernel, [(cells, BF16)], [spread, pltpu.VMEM((9 * channels, channels), BF16)], "grad_input"
     )(gp, gp_b, gp_a, cot_forward, cot_reverse, w_space)

time: 91.3 us -> 92.8 us (1.016)
  waiting for transfers between devices: 16.1 us -> 18 us
    all_to_all x3, waiting for transfers between devices: 10.5 us -> 12.7 us  [exchange(): lax.all_to_all(pieces, BOTH, 0, 0, tiled=True, axis_index_groups=members)]
    ppermute x8, starting transfers between devices: 29.2 us -> 27.1 us  [swapped(): return lax.ppermute(value, axis, pairs)]
    all_to_all x3, starting transfers between devices: 26.8 us -> 28.5 us  [exchange(): lax.all_to_all(pieces, BOTH, 0, 0, tiled=True, axis_index_groups=members)]
where the time goes in v5:
time: 92.8 us; the launch traced here: 92.1 us
  starting transfers between devices  55.6 us (60%)
  waiting for transfers between devices  18 us (19%)
  Pallas kernels  17.6 us (19%)
    all_to_all x3, starting transfers between devices, exchange(): lax.all_to_all(pieces, BOTH, 0, 0, tiled=True, axis_index_groups=members)  28.5 us
    ppermute x8, starting transfers between devices, swapped(): return lax.ppermute(value, axis, pairs)  27.1 us
    pallas_call x6, Pallas kernels, call(): pl.pallas_call(kernel, out_shape=tuple((jax.ShapeDtypeStruct(s, t) for s,...  15.3 us
    all_to_all x3, waiting for transfers between devices, exchange(): lax.all_to_all(pieces, BOTH, 0, 0, tiled=True, axis_index_groups=members)  12.7 us
    ppermute x8, waiting for transfers between devices, swapped(): return lax.ppermute(value, axis, pairs)  5.35 us
    pallas_call x1, Pallas kernels, edges(): pl.pallas_call(edges_kernel, out_shape=tuple((jax.ShapeDtypeStruct(s, BF1...  2.28 us
  transfers between devices with their start and end apart: 11, of which 5 were waited for; matrix products, arithmetic and copies ran while one was open for 0% of the time, Pallas kernels for 7%

profile of v5, /device:TPU:1, one launch (start us, length us, event | category | flops | bytes accessed | tf_op | source)
XLA Modules:
  0.0 92.1 jit_solution(15758045814468374631)
XLA Ops:
  0.6 0.0 copy-start.1
  0.6 0.0 copy-start
  0.7 0.0 copy-start.2
  0.7 2.3 %edges.1 = (bf16[2,4,160,128]{3,2,1,0:T(8,128)(2,1)}, bf16[2,4,160,128]{3,2,1,0:T(8,128)(2,1)}, bf16[4,160,128]{2,1,0:T(8,128)(2,1)}, bf16[4,160,128]{2,1,0:T(8,128)(2,1)}) custom-call(bf16[4,4,160,128]{3,2,1,0:T(8,128)(2,1)} %lat.5, bf16[4,4,160,128]{3,2,1,0:T(8,128)(2,1)} %fwd.5, bf16[4,4,160,128]{3,2,1,0:T(8,128)(2,1)} %rev.5), custom_call_target="tpu_custom_call" | custom-call | tf_op jit(solution)/shard_map/edges/pallas_call | solution.py:101
  2.9 0.7 collective-permute-start.2
  3.6 6.4 %collective-permute-start.3 = (bf16[2,4,160,128]{3,2,1,0:T(8,128)(2,1)}, bf16[2,4,160,128]{3,2,1,0:T(8,128)(2,1)S(1)}, u32[]{:S(2)}, u32[]{:S(2)}) collective-permute-start(bf16[2,4,160,128]{3,2,1,0:T(8,128)(2,1)} %get-tuple-element.29), channel_id=1, source_target_pairs={{0,8},{8,0},{16,24},{24,16},{32,40},{40,32},{48,56},{56,48},{64,72... | collective-permute-start | bytes 983048 | tf_op jit(solution)/shard_map/ppermute | solution.py:41
  10.0 6.9 %collective-permute-start = (bf16[4,160,128]{2,1,0:T(8,128)(2,1)}, bf16[4,160,128]{2,1,0:T(8,128)(2,1)S(1)}, u32[]{:S(2)}, u32[]{:S(2)}) collective-permute-start(bf16[4,160,128]{2,1,0:T(8,128)(2,1)} %get-tuple-element.26), channel_id=1, source_target_pairs={{1,2},{2,1},{3,4},{4,3},{5,6},{6,5},{9,10},{10,9},{11,12},{12,11},... | collective-permute-start | bytes 491528 | tf_op jit(solution)/shard_map/ppermute | solution.py:41
  17.0 1.9 %collective-permute-start.1 = (bf16[4,160,128]{2,1,0:T(8,128)(2,1)}, bf16[4,160,128]{2,1,0:T(8,128)(2,1)S(1)}, u32[]{:S(2)}, u32[]{:S(2)}) collective-permute-start(bf16[4,160,128]{2,1,0:T(8,128)(2,1)} %get-tuple-element.27), channel_id=1, source_target_pairs={{0,1},{1,0},{2,3},{3,2},{4,5},{5,4},{6,7},{7,6},{8,9},{9,8},{10,11... | collective-permute-start | bytes 491528 | tf_op jit(solution)/shard_map/ppermute | solution.py:41
  18.9 1.3 %collective-permute-done.row_b = bf16[4,160,128]{2,1,0:T(8,128)(2,1)S(1)} collective-permute-done((bf16[4,160,128]{2,1,0:T(8,128)(2,1)}, bf16[4,160,128]{2,1,0:T(8,128)(2,1)S(1)}, u32[]{:S(2)}, u32[]{:S(2)}) %collective-permute-start) | collective-permute-done | bytes 163872 | tf_op jit(solution)/shard_map/ppermute | solution.py:41
  20.2 0.3 collective-permute-done.1.row_a
  20.5 0.0 collective-permute-done.2.cots_b
  20.5 0.0 collective-permute-done.3.cots_a
  20.5 0.0 copy-done.1
  20.5 0.0 copy-done
  20.5 0.0 copy-done.2
  20.5 7.0 %front.1 = (bf16[4,4,160,128]{3,2,1,0:T(8,128)(2,1)S(1)}, bf16[4,4,160,128]{3,2,1,0:T(8,128)(2,1)}, bf16[2,4,160,128]{3,2,1,0:T(8,128)(2,1)}, bf16[2,4,160,128]{...) custom-call(bf16[4,4,160,128]{3,2,1,0:T(8,128)(2,1)S(1)} %copy-done.2, ...), custom_call_target="tpu_custom_call" | custom-call | tf_op jit(solution)/shard_map/front/pallas_call | solution.py:52
  27.6 7.9 %all-to-all-start = ((bf16[32,48,128]{2,1,0:T(8,128)(2,1)}), bf16[32,48,128]{2,1,0:T(8,128)(2,1)S(1)}, u32[]{:S(2)}, u32[]{:S(2)}) async-start(bf16[32,48,128]{2,1,0:T(8,128)(2,1)} %bitcast.9), calls=%async_computation | async-start | bytes 786432 | tf_op jit(solution)/shard_map/all_to_all | solution.py:33
  35.4 0.7 collective-permute-start.4
  36.1 5.7 %collective-permute-start.5 = (bf16[2,4,160,128]{3,2,1,0:T(8,128)(2,1)}, bf16[2,4,160,128]{3,2,1,0:T(8,128)(2,1)}, u32[]{:S(2)}, u32[]{:S(2)}) collective-permute-start(bf16[2,4,160,128]{3,2,1,0:T(8,128)(2,1)} %get-tuple-element.33), channel_id=1, source_target_pairs={{0,8},{8,0},{16,24},{24,16},{32,40},{40,32},{48,56},{56,48},{64,72... | collective-permute-start | bytes 983048 | tf_op jit(solution)/shard_map/ppermute | solution.py:41
  41.8 3.4 %all-to-all-done.pieces = bf16[32,48,128]{2,1,0:T(8,128)(2,1)S(1)} async-done(((bf16[32,48,128]{2,1,0:T(8,128)(2,1)}), bf16[32,48,128]{2,1,0:T(8,128)(2,1)S(1)}, u32[]{:S(2)}, u32[]{:S(2)}) %all-to-all-start) | async-done | bytes 393248 | tf_op jit(solution)/shard_map/all_to_all | solution.py:33
  45.3 0.7 share.2
  46.0 0.0 copy-start.5
  46.0 15.2 %all-to-all-start.1 = ((bf16[16,48,128]{2,1,0:T(8,128)(2,1)}), bf16[16,48,128]{2,1,0:T(8,128)(2,1)S(1)}, u32[]{:S(2)}, u32[]{:S(2)}) async-start(bf16[16,48,128]{2,1,0:T(8,128)(2,1)} %share.2), calls=%async_computation.1 | async-start | bytes 393216 | tf_op jit(solution)/shard_map/all_to_all | solution.py:33
  61.2 0.0 collective-permute-done.4.got_b
  61.2 0.0 collective-permute-done.5.got_a
  61.2 0.0 copy-done.5
  61.2 3.1 %outs.1 = (bf16[4,4,160,128]{3,2,1,0:T(8,128)(2,1)}, bf16[4,4,160,128]{3,2,1,0:T(8,128)(2,1)}) custom-call(bf16[4,4,160,128]{3,2,1,0:T(8,128)(2,1)S(1)} %copy-done.2, bf16[4,4,160,128]{3,2,1,0:T(8,128)(2,1)S(1)} %get-tuple-element.31.act, bf16[2,4,160,128]{3,2,1,0:T(8,128)(2,1)S(1)} %collective-permute-done.4.got_b, ...), custom_call_target="tpu_custom_call" | custom-call | flops 8000000000 | bytes 6291456 | tf_op jit(solution)/shard_map/outs/pallas_call | solution.py:52
  64.3 9.2 %all-to-all-done.1.pieces = bf16[16,48,128]{2,1,0:T(8,128)(2,1)S(1)} async-done(((bf16[16,48,128]{2,1,0:T(8,128)(2,1)}), bf16[16,48,128]{2,1,0:T(8,128)(2,1)S(1)}, u32[]{:S(2)}, u32[]{:S(2)}) %all-to-all-start.1) | async-done | bytes 196640 | tf_op jit(solution)/shard_map/all_to_all | solution.py:33
  73.6 0.0 copy-start.4
  73.6 0.8 share.3
  74.4 0.0 copy-start.7
  74.4 0.0 copy-start.6
  74.4 0.0 copy-start.3
  74.4 5.5 %all-to-all-start.2 = ((bf16[32,48,128]{2,1,0:T(8,128)(2,1)}), bf16[32,48,128]{2,1,0:T(8,128)(2,1)S(1)}, u32[]{:S(2)}, u32[]{:S(2)}) async-start(bf16[32,48,128]{2,1,0:T(8,128)(2,1)} %share.3), calls=%async_computation.2 | async-start | bytes 786432 | tf_op jit(solution)/shard_map/all_to_all | solution.py:33
  79.8 0.0 copy-done.7
  79.9 2.9 %collective-permute-start.6 = (bf16[4,160,128]{2,1,0:T(8,128)(2,1)S(1)}, bf16[4,160,128]{2,1,0:T(8,128)(2,1)S(1)}, u32[]{:S(2)}, u32[]{:S(2)}) collective-permute-start(bf16[4,160,128]{2,1,0:T(8,128)(2,1)S(1)} %copy-done.7), channel_id=1, source_target_pairs={{1,2},{2,1},{3,4},{4,3},{5,6},{6,5},{9,10},{10,9},{11,12},{12,11},... | collective-permute-start | bytes 491528 | tf_op jit(solution)/shard_map/ppermute | solution.py:41
  82.7 0.0 copy-done.6
  82.7 1.9 %collective-permute-start.7 = (bf16[4,160,128]{2,1,0:T(8,128)(2,1)S(1)}, bf16[4,160,128]{2,1,0:T(8,128)(2,1)S(1)}, u32[]{:S(2)}, u32[]{:S(2)}) collective-permute-start(bf16[4,160,128]{2,1,0:T(8,128)(2,1)S(1)} %copy-done.6), channel_id=1, source_target_pairs={{0,1},{1,0},{2,3},{3,2},{4,5},{5,4},{6,7},{7,6},{8,9},{9,8},{10,11... | collective-permute-start | bytes 491528 | tf_op jit(solution)/shard_map/ppermute | solution.py:41
  84.7 3.8 %collective-permute-done.6.got_b = bf16[4,160,128]{2,1,0:T(8,128)(2,1)S(1)} collective-permute-done((bf16[4,160,128]{2,1,0:T(8,128)(2,1)S(1)}, bf16[4,160,128]{2,1,0:T(8,128)(2,1)S(1)}, u32[]{:S(2)}, u32[]{:S(2)}) %collective-permute-start.6) | collective-permute-done | bytes 163872 | tf_op jit(solution)/shard_map/ppermute | solution.py:41
  88.4 0.0 collective-permute-done.7.got_a
  88.5 0.0 copy-done.4
  88.5 0.0 copy-done.3
  88.5 2.7 %grad_input.1 = bf16[4,4,160,128]{3,2,1,0:T(8,128)(2,1)} custom-call(bf16[4,4,160,128]{3,2,1,0:T(8,128)(2,1)S(1)} %copy-done.4, bf16[4,160,128]{2,1,0:T(8,128)(2,1)S(1)} %collective-permute-done.6.got_b, bf16[4,160,128]{2,1,0:T(8,128)(2,1)S(1)} %collective-permute-done.7.got_a, bf16[4,4,160,128]{3,2,1,0:T(8,128)(2,1)S(1)} %copy-done, ...), custom_call_target="tpu_custom_call" | custom-call | tf_op jit(solution)/shard_map/grad_input/pallas_call | solution.py:52
  91.2 0.0 all-to-all-done.2.pieces
  91.2 0.9 widen.1
Async XLA Ops:
  0.6 19.8 %copy-start.1 = (bf16[4,4,160,128]{3,2,1,0:T(8,128)(2,1)S(1)}, bf16[4,4,160,128]{3,2,1,0:T(8,128)(2,1)}, u32[]{:S(2)}) copy-start(bf16[4,4,160,128]{3,2,1,0:T(8,128)(2,1)} %rev.5) | copy-start | bytes 1966084
  0.6 19.8 %copy-start = (bf16[4,4,160,128]{3,2,1,0:T(8,128)(2,1)S(1)}, bf16[4,4,160,128]{3,2,1,0:T(8,128)(2,1)}, u32[]{:S(2)}) copy-start(bf16[4,4,160,128]{3,2,1,0:T(8,128)(2,1)} %fwd.5) | copy-start | bytes 1966084
  0.7 19.8 %copy-start.2 = (bf16[4,4,160,128]{3,2,1,0:T(8,128)(2,1)S(1)}, bf16[4,4,160,128]{3,2,1,0:T(8,128)(2,1)}, u32[]{:S(2)}) copy-start(bf16[4,4,160,128]{3,2,1,0:T(8,128)(2,1)} %lat.5) | copy-start | bytes 1966084
  2.9 17.5 %collective-permute-start.2 = (bf16[2,4,160,128]{3,2,1,0:T(8,128)(2,1)}, bf16[2,4,160,128]{3,2,1,0:T(8,128)(2,1)S(1)}, u32[]{:S(2)}, u32[]{:S(2)}) collective-permute-start(bf16[2,4,160,128]{3,2,1,0:T(8,128)(2,1)} %get-tuple-element.28), channel_id=1, source_target_pairs={{8,16},{16,8},{24,32},{32,24},{40,48},{48,40},{56,64},{64,56},{72,... | collective-permute-start | bytes 983048 | tf_op jit(solution)/shard_map/ppermute | solution.py:41
  3.6 16.8 %collective-permute-start.3 = (bf16[2,4,160,128]{3,2,1,0:T(8,128)(2,1)}, bf16[2,4,160,128]{3,2,1,0:T(8,128)(2,1)S(1)}, u32[]{:S(2)}, u32[]{:S(2)}) collective-permute-start(bf16[2,4,160,128]{3,2,1,0:T(8,128)(2,1)} %get-tuple-element.29), channel_id=1, source_target_pairs={{0,8},{8,0},{16,24},{24,16},{32,40},{40,32},{48,56},{56,48},{64,72... | collective-permute-start | bytes 983048 | tf_op jit(solution)/shard_map/ppermute | solution.py:41
  10.0 10.1 %collective-permute-start = (bf16[4,160,128]{2,1,0:T(8,128)(2,1)}, bf16[4,160,128]{2,1,0:T(8,128)(2,1)S(1)}, u32[]{:S(2)}, u32[]{:S(2)}) collective-permute-start(bf16[4,160,128]{2,1,0:T(8,128)(2,1)} %get-tuple-element.26), channel_id=1, source_target_pairs={{1,2},{2,1},{3,4},{4,3},{5,6},{6,5},{9,10},{10,9},{11,12},{12,11},... | collective-permute-start | bytes 491528 | tf_op jit(solution)/shard_map/ppermute | solution.py:41
  17.0 3.5 %collective-permute-start.1 = (bf16[4,160,128]{2,1,0:T(8,128)(2,1)}, bf16[4,160,128]{2,1,0:T(8,128)(2,1)S(1)}, u32[]{:S(2)}, u32[]{:S(2)}) collective-permute-start(bf16[4,160,128]{2,1,0:T(8,128)(2,1)} %get-tuple-element.27), channel_id=1, source_target_pairs={{0,1},{1,0},{2,3},{3,2},{4,5},{5,4},{6,7},{7,6},{8,9},{9,8},{10,11... | collective-permute-start | bytes 491528 | tf_op jit(solution)/shard_map/ppermute | solution.py:41
  27.6 17.7 %all-to-all-start = ((bf16[32,48,128]{2,1,0:T(8,128)(2,1)}), bf16[32,48,128]{2,1,0:T(8,128)(2,1)S(1)}, u32[]{:S(2)}, u32[]{:S(2)}) async-start(bf16[32,48,128]{2,1,0:T(8,128)(2,1)} %bitcast.9), calls=%async_computation | async-start | bytes 786432 | tf_op jit(solution)/shard_map/all_to_all | solution.py:33
  35.4 25.8 %collective-permute-start.4 = (bf16[2,4,160,128]{3,2,1,0:T(8,128)(2,1)}, bf16[2,4,160,128]{3,2,1,0:T(8,128)(2,1)S(1)}, u32[]{:S(2)}, u32[]{:S(2)}) collective-permute-start(bf16[2,4,160,128]{3,2,1,0:T(8,128)(2,1)} %get-tuple-element.32), channel_id=1, source_target_pairs={{8,16},{16,8},{24,32},{32,24},{40,48},{48,40},{56,64},{64,56},{72,... | collective-permute-start | bytes 983048 | tf_op jit(solution)/shard_map/ppermute | solution.py:41
  36.1 25.1 %collective-permute-start.5 = (bf16[2,4,160,128]{3,2,1,0:T(8,128)(2,1)}, bf16[2,4,160,128]{3,2,1,0:T(8,128)(2,1)}, u32[]{:S(2)}, u32[]{:S(2)}) collective-permute-start(bf16[2,4,160,128]{3,2,1,0:T(8,128)(2,1)} %get-tuple-element.33), channel_id=1, source_target_pairs={{0,8},{8,0},{16,24},{24,16},{32,40},{40,32},{48,56},{56,48},{64,72... | collective-permute-start | bytes 983048 | tf_op jit(solution)/shard_map/ppermute | solution.py:41
  46.0 15.2 %copy-start.5 = (bf16[3,128,128]{2,1,0:T(8,128)(2,1)S(1)}, bf16[3,128,128]{2,1,0:T(8,128)(2,1)}, u32[]{:S(2)}) copy-start(bf16[3,128,128]{2,1,0:T(8,128)(2,1)} %param.9) | copy-start | bytes 294916
  46.0 27.6 %all-to-all-start.1 = ((bf16[16,48,128]{2,1,0:T(8,128)(2,1)}), bf16[16,48,128]{2,1,0:T(8,128)(2,1)S(1)}, u32[]{:S(2)}, u32[]{:S(2)}) async-start(bf16[16,48,128]{2,1,0:T(8,128)(2,1)} %share.2), calls=%async_computation.1 | async-start | bytes 393216 | tf_op jit(solution)/shard_map/all_to_all | solution.py:33
  73.6 14.9 %copy-start.4 = (bf16[4,4,160,128]{3,2,1,0:T(8,128)(2,1)S(1)}, bf16[4,4,160,128]{3,2,1,0:T(8,128)(2,1)}, u32[]{:S(2)}) copy-start(bf16[4,4,160,128]{3,2,1,0:T(8,128)(2,1)} %get-tuple-element.38.gp) | copy-start | bytes 1966084
  74.4 5.5 %copy-start.7 = (bf16[4,160,128]{2,1,0:T(8,128)(2,1)S(1)}, bf16[4,160,128]{2,1,0:T(8,128)(2,1)}, u32[]{:S(2)}) copy-start(bf16[4,160,128]{2,1,0:T(8,128)(2,1)} %get-tuple-element.42) | copy-start | bytes 491524
  74.4 8.4 %copy-start.6 = (bf16[4,160,128]{2,1,0:T(8,128)(2,1)S(1)}, bf16[4,160,128]{2,1,0:T(8,128)(2,1)}, u32[]{:S(2)}) copy-start(bf16[4,160,128]{2,1,0:T(8,128)(2,1)} %get-tuple-element.43) | copy-start | bytes 491524
  74.4 14.1 %copy-start.3 = (bf16[3,3,128,128]{3,2,1,0:T(8,128)(2,1)S(1)}, bf16[3,3,128,128]{3,2,1,0:T(8,128)(2,1)}, u32[]{:S(2)}) copy-start(bf16[3,3,128,128]{3,2,1,0:T(8,128)(2,1)} %param.8) | copy-start | bytes 884740
  74.4 16.8 %all-to-all-start.2 = ((bf16[32,48,128]{2,1,0:T(8,128)(2,1)}), bf16[32,48,128]{2,1,0:T(8,128)(2,1)S(1)}, u32[]{:S(2)}, u32[]{:S(2)}) async-start(bf16[32,48,128]{2,1,0:T(8,128)(2,1)} %share.3), calls=%async_computation.2 | async-start | bytes 786432 | tf_op jit(solution)/shard_map/all_to_all | solution.py:33
  79.9 8.6 %collective-permute-start.6 = (bf16[4,160,128]{2,1,0:T(8,128)(2,1)S(1)}, bf16[4,160,128]{2,1,0:T(8,128)(2,1)S(1)}, u32[]{:S(2)}, u32[]{:S(2)}) collective-permute-start(bf16[4,160,128]{2,1,0:T(8,128)(2,1)S(1)} %copy-done.7), channel_id=1, source_target_pairs={{1,2},{2,1},{3,4},{4,3},{5,6},{6,5},{9,10},{10,9},{11,12},{12,11},... | collective-permute-start | bytes 491528 | tf_op jit(solution)/shard_map/ppermute | solution.py:41
  82.7 5.7 %collective-permute-start.7 = (bf16[4,160,128]{2,1,0:T(8,128)(2,1)S(1)}, bf16[4,160,128]{2,1,0:T(8,128)(2,1)S(1)}, u32[]{:S(2)}, u32[]{:S(2)}) collective-permute-start(bf16[4,160,128]{2,1,0:T(8,128)(2,1)S(1)} %copy-done.6), channel_id=1, source_target_pairs={{0,1},{1,0},{2,3},{3,2},{4,5},{5,4},{6,7},{7,6},{8,9},{9,8},{10,11... | collective-permute-start | bytes 491528 | tf_op jit(solution)/shard_map/ppermute | solution.py:41

commit v6 on v4

--- a/solution.py
+++ b/solution.py
@@ -45,21 +45,22 @@
     return lax.rem(lax.axis_index(axis), 2) == 0
 
 
-def vmem_call(kernel, outs, scratch=(), name=None, in_hbm=0, outs_hbm=()):
+def vmem_call(kernel, outs, scratch=(), name=None, in_hbm=0, outs_hbm=(), pin=False, cost=None):
     space = pl.BlockSpec(memory_space=pltpu.VMEM)
 
     def call(*args):
         return pl.pallas_call(
             kernel,
-            out_shape=tuple(jax.ShapeDtypeStruct(s, t) for s, t in outs)
+            out_shape=tuple((pltpu.VMEM if pin else jax.ShapeDtypeStruct)(s, t) for s, t in outs)
             + tuple(pltpu.HBM(s, t) for s, t in outs_hbm),
             in_specs=[space] * (len(args) - in_hbm)
             + [pl.BlockSpec(memory_space=pltpu.HBM)] * in_hbm,
             out_specs=tuple(space for _ in outs)
             + tuple(pl.BlockSpec(memory_space=pltpu.HBM) for _ in outs_hbm),
             scratch_shapes=list(scratch),
-            compiler_params=pltpu.CompilerParams(vmem_limit_bytes=48 << 20),
+            compiler_params=pltpu.CompilerParams(vmem_limit_bytes=20 << 20),
             name=name,
+            cost_estimate=cost,
         )(*args[: len(args) - in_hbm], *(held(a) for a in args[len(args) - in_hbm :]))
 
     return call
@@ -107,39 +108,33 @@
     )(held(lat), held(fwd), held(rev))
 
 
-def spread_columns(row, out, frame, at):
+def beside(row):
     width = row.shape[0]
     wide = row.astype(F32)
     place = lax.broadcasted_iota(jnp.int32, wide.shape, 0)
     left = jnp.where(place == 0, 0.0, pltpu.roll(wide, 1, 0))
     right = jnp.where(place == width - 1, 0.0, pltpu.roll(wide, width - 1, 0))
-    out[frame, at, :, 0:128] = left.astype(BF16)
-    out[frame, at, :, 128:256] = row
-    out[frame, at, :, 256:384] = right.astype(BF16)
+    return jnp.concatenate([left.astype(BF16), row, right.astype(BF16)], axis=1)
+
+
+def windows(rows):
+    return jnp.concatenate([rows[i : i + 4].reshape(640, 384) for i in range(3)], axis=1)
 
 
 def spread_frame(own, got_a, got_b, even, out, frame):
     one, two = got_a[frame], got_b[frame]
-    spread_columns(jnp.where(even, two, one), out, frame, 0)
+    out[frame, 0] = beside(jnp.where(even, two, one))
     for r in range(4):
-        spread_columns(own[frame, r], out, frame, r + 1)
-    spread_columns(jnp.where(even, one, two), out, frame, 5)
-
-
-def patch_rows(spread, frame):
-    return jnp.concatenate(
-        [spread[frame, i : i + 4].reshape(640, 384) for i in range(3)], axis=1
-    )
+        out[frame, r + 1] = beside(own[frame, r])
+    out[frame, 5] = beside(jnp.where(even, one, two))
 
 
 def transposed(block):
     return jnp.transpose(block.astype(F32))
 
 
-def front_kernel(
-    lat, row_b, row_a, fwd, rev, cots_b, cots_a, w_space_at, w_time_at,
-    act_out, gp_out, act_a, act_b, gp_a, gp_b, partial,
-    spread, gp, w_space, w_time, back, acc_space, acc_time, summed, sems,
+def prep_kernel(
+    lat, fwd, rev, w_space_at, w_time_at, spread, pre, grad_act, w_space, back, w_time, sems
 ):
     loads = [
         pltpu.make_async_copy(w_time_at, w_time, sems.at[0]),
@@ -147,37 +142,76 @@
     ]
     for c in loads:
         c.start()
-    even_tm, even_tile = is_even("tm"), is_even("tile")
-    spread_frame(lat, row_a, row_b, even_tile, spread, 0)
+    for f in range(4):
+        for r in range(4):
+            spread[f, r] = beside(lat[f, r])
     for c in loads:
         c.wait()
     for k in range(3):
         turned = transposed(w_time[k * 128 : (k + 1) * 128, :]).astype(BF16)
         back[k * 128 : (k + 1) * 128, :] = turned
         back[384 + k * 128 : 384 + (k + 1) * 128, :] = turned
+    outside = jnp.zeros((1, 160, 384), BF16)
+    for f in range(4):
+        patches = windows(jnp.concatenate([outside, spread[f], outside], axis=0))
+        rows = slice(f * 640, f * 640 + 640)
+        pre[rows, :] = jnp.dot(patches, w_space[...], preferred_element_type=F32)
+        ahead, behind = min(3, 4 - f), min(3, f + 1)
+        cots = [fwd[f + k] for k in range(ahead)] + [rev[f - k] for k in range(behind)]
+        cots = jnp.concatenate([c.reshape(640, 128) for c in cots], axis=1)
+        weights = jnp.concatenate([back[: ahead * 128, :], back[384 : 384 + behind * 128, :]], axis=0)
+        grad_act[rows, :] = jnp.dot(cots, weights, preferred_element_type=F32)
+
+
+def front_kernel(
+    spread, pre_own, grad_own, w_space, back, cots_b, cots_a, row_b, row_a, fwd, rev,
+    act_out, gp_out, act_a, act_b, gp_a, gp_b, partial,
+    gp, acc_space, acc_time, summed, sems,
+):
+    even_tm, even_tile = is_even("tm"), is_even("tile")
     stores = []
     for f in range(4):
-        if f > 0:
-            spread_frame(lat, row_a, row_b, even_tile, spread, f)
-        patches = patch_rows(spread, f)
-        pre = jnp.dot(patches, w_space[...], preferred_element_type=F32)
+        top = beside(jnp.where(even_tile, row_b[f], row_a[f]))
+        bottom = beside(jnp.where(even_tile, row_a[f], row_b[f]))
+        patches = windows(jnp.concatenate([top[None], spread[f], bottom[None]], axis=0))
+        at = f * 640
+        pre = jnp.concatenate(
+            [
+                pre_own[at : at + 160, :]
+                + jnp.dot(top, w_space[:384, :], preferred_element_type=F32),
+                pre_own[at + 160 : at + 480, :],
+                pre_own[at + 480 : at + 640, :]
+                + jnp.dot(bottom, w_space[768:, :], preferred_element_type=F32),
+            ],
+            axis=0,
+        )
         sig = 0.5 + 0.5 * jnp.tanh(0.5 * pre)
         act32 = pre * sig
         act = act32.astype(BF16)
         act_out[f] = act.reshape(4, 160, 128)
-        cots = []
+        cots, sent, weights = [], [], []
         for k in range(3):
             if f + k < 4:
-                cots.append(fwd[f + k])
+                cots.append(fwd[f + k].reshape(640, 128))
             else:
-                cots.append(jnp.where(even_tm, cots_a[f + k - 4], cots_b[f + k - 4]))
+                at = f + k - 4
+                sent.append(jnp.where(even_tm, cots_a[at], cots_b[at]).reshape(640, 128))
+                weights.append(back[k * 128 : (k + 1) * 128, :])
+                cots.append(sent[-1])
         for k in range(3):
             if f >= k:
-                cots.append(rev[f - k])
+                cots.append(rev[f - k].reshape(640, 128))
             else:
-                cots.append(jnp.where(even_tm, cots_b[f - k + 2], cots_a[f - k + 2]))
-        cots = jnp.concatenate([c.reshape(640, 128) for c in cots], axis=1)
-        grad_act = jnp.dot(cots, back[...], preferred_element_type=F32)
+                at = f - k + 2
+                sent.append(jnp.where(even_tm, cots_b[at], cots_a[at]).reshape(640, 128))
+                weights.append(back[k * 128 : (k + 1) * 128, :])
+                cots.append(sent[-1])
+        cots = jnp.concatenate(cots, axis=1)
+        grad_act = grad_own[f * 640 : f * 640 + 640, :] + jnp.dot(
+            jnp.concatenate(sent, axis=1),
+            jnp.concatenate(weights, axis=0),
+            preferred_element_type=F32,
+        )
         grad = (grad_act * (sig + act32 * (1.0 - sig))).astype(BF16)
         gp[f] = grad.reshape(4, 160, 128)
         gp_copy = pltpu.make_async_copy(gp.at[f], gp_out.at[f], sems.at[7 + f])
@@ -274,7 +308,7 @@
             ).astype(BF16)
     for f in range(4):
         spread_frame(gp, got_a, got_b, even, spread, f)
-        patches = patch_rows(spread, f)
+        patches = windows(spread[f])
         total = fwd[f].astype(F32) + rev[f].astype(F32)
         total = total.reshape(640, 128) + jnp.dot(patches, back[...], preferred_element_type=F32)
         out[f] = total.astype(BF16).reshape(4, 160, 128)
@@ -294,24 +328,33 @@
     cots_a = swapped(cots_a, "tm", 0)
     row_b = swapped(row_b, "tile", 1)
     row_a = swapped(row_a, "tile", 0)
+    flat = (frame_count * height * width_cells, channels)
+    weights = (9 * channels, channels)
+    own = vmem_call(
+        prep_kernel,
+        [
+            ((frame_count, height, width_cells, 3 * channels), BF16),
+            (flat, F32), (flat, F32), (weights, BF16), ((6 * channels, channels), BF16),
+        ],
+        [pltpu.VMEM((3 * channels, channels), BF16), pltpu.SemaphoreType.DMA((2,))],
+        "prep",
+        in_hbm=2,
+        pin=True,
+
+    )(latent, cot_forward, cot_reverse, w_space, w_time)
     act, gp, act_a, act_b, gp_a, gp_b, partial = vmem_call(
         front_kernel,
         [(cells, BF16)],
         [
-            spread,
             pltpu.VMEM(cells, BF16),
-            pltpu.VMEM((9 * channels, channels), BF16),
-            pltpu.VMEM((3 * channels, channels), BF16),
-            pltpu.VMEM((6 * channels, channels), BF16),
             pltpu.VMEM((channels, 9 * channels), F32),
             pltpu.VMEM((channels, 3 * channels), F32),
             pltpu.VMEM((12 * channels, channels), BF16),
             pltpu.SemaphoreType.DMA((15,)),
         ],
         "front",
-        in_hbm=2,
         outs_hbm=[(cells, BF16)] + [(pair, BF16)] * 2 + [(line, BF16)] * 2 + [((12 * channels, channels), BF16)],
-    )(latent, row_b, row_a, cot_forward, cot_reverse, cots_b, cots_a, w_space, w_time)
+    )(*(pltpu.with_memory_space_constraint(o, pltpu.VMEM) for o in own), cots_b, cots_a, row_b, row_a, cot_forward, cot_reverse)
 
     near, far = len(NEAR[0]), len(FAR[0])
     positions = frame_count * height * width_cells * lax.axis_size("tm") * lax.axis_size("tile")

time: 91.3 us -> 88.4 us (0.968)
  starting transfers between devices: 56.1 us -> 53.9 us
  waiting for transfers between devices: 16.1 us -> 14.4 us
    all_to_all x3, starting transfers between devices: 26.8 us -> 24.7 us  [exchange(): lax.all_to_all(pieces, BOTH, 0, 0, tiled=True, axis_index_groups=members)]
    ppermute x8, waiting for transfers between devices: 5.55 us -> 3.98 us  [swapped(): return lax.ppermute(value, axis, pairs)]
    pallas_call x6 -> x7, Pallas kernels: 15.4 us -> 16.2 us  [call(): pl.pallas_call(kernel, out_shape=tuple(((pltpu.VMEM if pin else jax.Shape...]
  transfers between devices with their start and end apart: 11 -> 11, of which waited for: 5 -> 3; matrix products, arithmetic and copies ran while one was open for 0% -> 0% of each run, Pallas kernels for 7% -> 12%
where the time goes in v6:
time: 88.4 us; the launch traced here: 87.8 us
  starting transfers between devices  53.9 us (61%)
  Pallas kernels  18.5 us (21%)
  waiting for transfers between devices  14.4 us (16%)
  between operations  0.91 us (1%)
    ppermute x8, starting transfers between devices, swapped(): return lax.ppermute(value, axis, pairs)  29.2 us
    all_to_all x3, starting transfers between devices, exchange(): lax.all_to_all(pieces, BOTH, 0, 0, tiled=True, axis_index_groups=members)  24.7 us
    pallas_call x7, Pallas kernels, call(): pl.pallas_call(kernel, out_shape=tuple(((pltpu.VMEM if pin else jax.Shape...  16.2 us
    all_to_all x3, waiting for transfers between devices, exchange(): lax.all_to_all(pieces, BOTH, 0, 0, tiled=True, axis_index_groups=members)  10.5 us
    ppermute x8, waiting for transfers between devices, swapped(): return lax.ppermute(value, axis, pairs)  3.98 us
    pallas_call x1, Pallas kernels, edges(): pl.pallas_call(edges_kernel, out_shape=tuple((jax.ShapeDtypeStruct(s, BF1...  2.28 us
  transfers between devices with their start and end apart: 11, of which 3 were waited for; matrix products, arithmetic and copies ran while one was open for 0% of the time, Pallas kernels for 12%

profile of v6, /device:TPU:1, one launch (start us, length us, event | category | flops | bytes accessed | tf_op | source)
XLA Modules:
  0.0 87.8 jit_solution(4706762625255301065)
XLA Ops:
  0.6 0.0 copy-start.1
  0.6 0.0 copy-start
  0.7 0.0 copy-start.2
  0.7 2.3 %edges.1 = (bf16[2,4,160,128]{3,2,1,0:T(8,128)(2,1)}, bf16[2,4,160,128]{3,2,1,0:T(8,128)(2,1)}, bf16[4,160,128]{2,1,0:T(8,128)(2,1)}, bf16[4,160,128]{2,1,0:T(8,128)(2,1)}) custom-call(bf16[4,4,160,128]{3,2,1,0:T(8,128)(2,1)} %lat.5, bf16[4,4,160,128]{3,2,1,0:T(8,128)(2,1)} %fwd.7, bf16[4,4,160,128]{3,2,1,0:T(8,128)(2,1)} %rev.7), custom_call_target="tpu_custom_call" | custom-call | tf_op jit(solution)/shard_map/edges/pallas_call | solution.py:101
  2.9 0.7 collective-permute-start
  3.6 6.4 %collective-permute-start.1 = (bf16[2,4,160,128]{3,2,1,0:T(8,128)(2,1)}, bf16[2,4,160,128]{3,2,1,0:T(8,128)(2,1)S(1)}, u32[]{:S(2)}, u32[]{:S(2)}) collective-permute-start(bf16[2,4,160,128]{3,2,1,0:T(8,128)(2,1)} %get-tuple-element.38), channel_id=1, source_target_pairs={{0,8},{8,0},{16,24},{24,16},{32,40},{40,32},{48,56},{56,48},{64,72... | collective-permute-start | bytes 983048 | tf_op jit(solution)/shard_map/ppermute | solution.py:41
  10.0 6.9 %collective-permute-start.2 = (bf16[4,160,128]{2,1,0:T(8,128)(2,1)}, bf16[4,160,128]{2,1,0:T(8,128)(2,1)S(1)}, u32[]{:S(2)}, u32[]{:S(2)}) collective-permute-start(bf16[4,160,128]{2,1,0:T(8,128)(2,1)} %get-tuple-element.39), channel_id=1, source_target_pairs={{1,2},{2,1},{3,4},{4,3},{5,6},{6,5},{9,10},{10,9},{11,12},{12,11},... | collective-permute-start | bytes 491528 | tf_op jit(solution)/shard_map/ppermute | solution.py:41
  17.0 1.9 %collective-permute-start.3 = (bf16[4,160,128]{2,1,0:T(8,128)(2,1)}, bf16[4,160,128]{2,1,0:T(8,128)(2,1)S(1)}, u32[]{:S(2)}, u32[]{:S(2)}) collective-permute-start(bf16[4,160,128]{2,1,0:T(8,128)(2,1)} %get-tuple-element.40), channel_id=1, source_target_pairs={{0,1},{1,0},{2,3},{3,2},{4,5},{5,4},{6,7},{7,6},{8,9},{9,8},{10,11... | collective-permute-start | bytes 491528 | tf_op jit(solution)/shard_map/ppermute | solution.py:41
  18.9 0.0 copy-done.1
  18.9 0.0 copy-done
  18.9 0.0 copy-done.2
  18.9 3.5 %prep.1 = (bf16[4,4,160,384]{3,2,1,0:T(8,128)(2,1)S(1)}, f32[2560,128]{1,0:T(8,128)S(1)}, f32[2560,128]{1,0:T(8,128)S(1)}, bf16[1152,128]{1,0:T(8,128)(2,1)S(1)}, bf16[768,128]{1,0:T(8,128)(2,1)S(1)}) custom-call(bf16[4,4,160,128]{3,2,1,0:T(8,128)(2,1)S(1)} %copy-done.2, bf16[4,4,160,128]{3,2,1,0:T(8,128)(2,1)S(1)} %copy-done, ...), custom_call_target="tpu_custom_call" | custom-call | tf_op jit(solution)/shard_map/prep/pallas_call | solution.py:52
  22.5 0.0 collective-permute-done.2.row_b
  22.5 0.0 collective-permute-done.3.row_a
  22.5 0.0 collective-permute-done.cots_b
  22.5 0.0 collective-permute-done.1.cots_a
  22.5 4.3 %front.1 = (bf16[4,4,160,128]{3,2,1,0:T(8,128)(2,1)S(1)}, bf16[4,4,160,128]{3,2,1,0:T(8,128)(2,1)}, bf16[2,4,160,128]{3,2,1,0:T(8,128)(2,1)}, bf16[2,4,160,128]{...) custom-call(bf16[4,4,160,384]{3,2,1,0:T(8,128)(2,1)S(1)} %get-tuple-ele, ...), custom_call_target="tpu_custom_call" | custom-call | tf_op jit(solution)/shard_map/front/pallas_call | solution.py:52
  26.8 0.0 copy-start.5
  26.8 7.7 %all-to-all-start = ((bf16[32,48,128]{2,1,0:T(8,128)(2,1)}), bf16[32,48,128]{2,1,0:T(8,128)(2,1)S(1)}, u32[]{:S(2)}, u32[]{:S(2)}) async-start(bf16[32,48,128]{2,1,0:T(8,128)(2,1)} %bitcast.9), calls=%async_computation | async-start | bytes 786432 | tf_op jit(solution)/shard_map/all_to_all | solution.py:33
  34.5 0.7 collective-permute-start.4
  35.2 5.7 %collective-permute-start.5 = (bf16[2,4,160,128]{3,2,1,0:T(8,128)(2,1)}, bf16[2,4,160,128]{3,2,1,0:T(8,128)(2,1)}, u32[]{:S(2)}, u32[]{:S(2)}) collective-permute-start(bf16[2,4,160,128]{3,2,1,0:T(8,128)(2,1)} %get-tuple-element.45), channel_id=1, source_target_pairs={{0,8},{8,0},{16,24},{24,16},{32,40},{40,32},{48,56},{56,48},{64,72... | collective-permute-start | bytes 983048 | tf_op jit(solution)/shard_map/ppermute | solution.py:41
  40.9 3.4 %all-to-all-done.pieces = bf16[32,48,128]{2,1,0:T(8,128)(2,1)S(1)} async-done(((bf16[32,48,128]{2,1,0:T(8,128)(2,1)}), bf16[32,48,128]{2,1,0:T(8,128)(2,1)S(1)}, u32[]{:S(2)}, u32[]{:S(2)}) %all-to-all-start) | async-done | bytes 393248 | tf_op jit(solution)/shard_map/all_to_all | solution.py:33
  44.4 0.7 share.2
  45.1 13.3 %all-to-all-start.1 = ((bf16[16,48,128]{2,1,0:T(8,128)(2,1)}), bf16[16,48,128]{2,1,0:T(8,128)(2,1)S(1)}, u32[]{:S(2)}, u32[]{:S(2)}) async-start(bf16[16,48,128]{2,1,0:T(8,128)(2,1)} %share.2), calls=%async_computation.1 | async-start | bytes 393216 | tf_op jit(solution)/shard_map/all_to_all | solution.py:33
  58.4 0.0 copy-start.7
  58.4 0.0 copy-start.6
  58.4 0.0 collective-permute-done.4.got_b
  58.4 0.0 collective-permute-done.5.got_a
  58.5 0.0 copy-done.5
  58.5 0.0 copy-start.3
  58.5 3.2 %outs.1 = (bf16[4,4,160,128]{3,2,1,0:T(8,128)(2,1)}, bf16[4,4,160,128]{3,2,1,0:T(8,128)(2,1)}) custom-call(bf16[4,4,160,128]{3,2,1,0:T(8,128)(2,1)S(1)} %copy-done.2, bf16[4,4,160,128]{3,2,1,0:T(8,128)(2,1)S(1)} %get-tuple-element.43.act, bf16[2,4,160,128]{3,2,1,0:T(8,128)(2,1)S(1)} %collective-permute-done.4.got_b, ...), custom_call_target="tpu_custom_call" | custom-call | tf_op jit(solution)/shard_map/outs/pallas_call | solution.py:52
  61.7 0.0 copy-start.4
  61.7 0.0 copy-done.7
  61.7 5.0 %collective-permute-start.6 = (bf16[4,160,128]{2,1,0:T(8,128)(2,1)S(1)}, bf16[4,160,128]{2,1,0:T(8,128)(2,1)S(1)}, u32[]{:S(2)}, u32[]{:S(2)}) collective-permute-start(bf16[4,160,128]{2,1,0:T(8,128)(2,1)S(1)} %copy-done.7), channel_id=1, source_target_pairs={{1,2},{2,1},{3,4},{4,3},{5,6},{6,5},{9,10},{10,9},{11,12},{12,11},... | collective-permute-start | bytes 491528 | tf_op jit(solution)/shard_map/ppermute | solution.py:41
  66.7 0.0 copy-done.6
  66.7 1.9 %collective-permute-start.7 = (bf16[4,160,128]{2,1,0:T(8,128)(2,1)S(1)}, bf16[4,160,128]{2,1,0:T(8,128)(2,1)S(1)}, u32[]{:S(2)}, u32[]{:S(2)}) collective-permute-start(bf16[4,160,128]{2,1,0:T(8,128)(2,1)S(1)} %copy-done.6), channel_id=1, source_target_pairs={{0,1},{1,0},{2,3},{3,2},{4,5},{5,4},{6,7},{7,6},{8,9},{9,8},{10,11... | collective-permute-start | bytes 491528 | tf_op jit(solution)/shard_map/ppermute | solution.py:41
  68.6 4.0 %collective-permute-done.6.got_b = bf16[4,160,128]{2,1,0:T(8,128)(2,1)S(1)} collective-permute-done((bf16[4,160,128]{2,1,0:T(8,128)(2,1)S(1)}, bf16[4,160,128]{2,1,0:T(8,128)(2,1)S(1)}, u32[]{:S(2)}, u32[]{:S(2)}) %collective-permute-start.6) | collective-permute-done | bytes 163872 | tf_op jit(solution)/shard_map/ppermute | solution.py:41
  72.6 0.0 collective-permute-done.7.got_a
  72.6 0.0 all-to-all-done.1.pieces
  72.6 0.8 share.3
  73.4 3.7 %all-to-all-start.2 = ((bf16[32,48,128]{2,1,0:T(8,128)(2,1)}), bf16[32,48,128]{2,1,0:T(8,128)(2,1)S(1)}, u32[]{:S(2)}, u32[]{:S(2)}) async-start(bf16[32,48,128]{2,1,0:T(8,128)(2,1)} %share.3), calls=%async_computation.2 | async-start | bytes 786432 | tf_op jit(solution)/shard_map/all_to_all | solution.py:33
  77.1 0.0 copy-done.3
  77.1 0.0 copy-done.4
  77.1 2.7 %grad_input.1 = bf16[4,4,160,128]{3,2,1,0:T(8,128)(2,1)} custom-call(bf16[4,4,160,128]{3,2,1,0:T(8,128)(2,1)S(1)} %copy-done.4, bf16[4,160,128]{2,1,0:T(8,128)(2,1)S(1)} %collective-permute-done.6.got_b, bf16[4,160,128]{2,1,0:T(8,128)(2,1)S(1)} %collective-permute-done.7.got_a, bf16[4,4,160,128]{3,2,1,0:T(8,128)(2,1)S(1)} %copy-done, ...), custom_call_target="tpu_custom_call" | custom-call | tf_op jit(solution)/shard_map/grad_input/pallas_call | solution.py:52
  79.8 7.0 %all-to-all-done.2.pieces = bf16[32,48,128]{2,1,0:T(8,128)(2,1)S(1)} async-done(((bf16[32,48,128]{2,1,0:T(8,128)(2,1)}), bf16[32,48,128]{2,1,0:T(8,128)(2,1)S(1)}, u32[]{:S(2)}, u32[]{:S(2)}) %all-to-all-start.2) | async-done | bytes 393248 | tf_op jit(solution)/shard_map/all_to_all | solution.py:33
  86.8 0.9 %widen.1 = (f32[1152,128]{1,0:T(8,128)}, f32[384,128]{1,0:T(8,128)}) custom-call(bf16[32,48,128]{2,1,0:T(8,128)(2,1)S(1)} %all-to-all-done.2.pieces), custom_call_target="tpu_custom_call" | custom-call | tf_op jit(solution)/shard_map/widen/pallas_call | solution.py:52
Async XLA Ops:
  0.6 18.3 %copy-start.1 = (bf16[4,4,160,128]{3,2,1,0:T(8,128)(2,1)S(1)}, bf16[4,4,160,128]{3,2,1,0:T(8,128)(2,1)}, u32[]{:S(2)}) copy-start(bf16[4,4,160,128]{3,2,1,0:T(8,128)(2,1)} %rev.7) | copy-start | bytes 1966084
  0.6 18.3 %copy-start = (bf16[4,4,160,128]{3,2,1,0:T(8,128)(2,1)S(1)}, bf16[4,4,160,128]{3,2,1,0:T(8,128)(2,1)}, u32[]{:S(2)}) copy-start(bf16[4,4,160,128]{3,2,1,0:T(8,128)(2,1)} %fwd.7) | copy-start | bytes 1966084
  0.7 18.3 %copy-start.2 = (bf16[4,4,160,128]{3,2,1,0:T(8,128)(2,1)S(1)}, bf16[4,4,160,128]{3,2,1,0:T(8,128)(2,1)}, u32[]{:S(2)}) copy-start(bf16[4,4,160,128]{3,2,1,0:T(8,128)(2,1)} %lat.5) | copy-start | bytes 1966084
  2.9 19.5 %collective-permute-start = (bf16[2,4,160,128]{3,2,1,0:T(8,128)(2,1)}, bf16[2,4,160,128]{3,2,1,0:T(8,128)(2,1)S(1)}, u32[]{:S(2)}, u32[]{:S(2)}) collective-permute-start(bf16[2,4,160,128]{3,2,1,0:T(8,128)(2,1)} %get-tuple-element.37), channel_id=1, source_target_pairs={{8,16},{16,8},{24,32},{32,24},{40,48},{48,40},{56,64},{64,56},{72,... | collective-permute-start | bytes 983048 | tf_op jit(solution)/shard_map/ppermute | solution.py:41
  3.6 18.9 %collective-permute-start.1 = (bf16[2,4,160,128]{3,2,1,0:T(8,128)(2,1)}, bf16[2,4,160,128]{3,2,1,0:T(8,128)(2,1)S(1)}, u32[]{:S(2)}, u32[]{:S(2)}) collective-permute-start(bf16[2,4,160,128]{3,2,1,0:T(8,128)(2,1)} %get-tuple-element.38), channel_id=1, source_target_pairs={{0,8},{8,0},{16,24},{24,16},{32,40},{40,32},{48,56},{56,48},{64,72... | collective-permute-start | bytes 983048 | tf_op jit(solution)/shard_map/ppermute | solution.py:41
  10.0 12.4 %collective-permute-start.2 = (bf16[4,160,128]{2,1,0:T(8,128)(2,1)}, bf16[4,160,128]{2,1,0:T(8,128)(2,1)S(1)}, u32[]{:S(2)}, u32[]{:S(2)}) collective-permute-start(bf16[4,160,128]{2,1,0:T(8,128)(2,1)} %get-tuple-element.39), channel_id=1, source_target_pairs={{1,2},{2,1},{3,4},{4,3},{5,6},{6,5},{9,10},{10,9},{11,12},{12,11},... | collective-permute-start | bytes 491528 | tf_op jit(solution)/shard_map/ppermute | solution.py:41
  17.0 5.5 %collective-permute-start.3 = (bf16[4,160,128]{2,1,0:T(8,128)(2,1)}, bf16[4,160,128]{2,1,0:T(8,128)(2,1)S(1)}, u32[]{:S(2)}, u32[]{:S(2)}) collective-permute-start(bf16[4,160,128]{2,1,0:T(8,128)(2,1)} %get-tuple-element.40), channel_id=1, source_target_pairs={{0,1},{1,0},{2,3},{3,2},{4,5},{5,4},{6,7},{7,6},{8,9},{9,8},{10,11... | collective-permute-start | bytes 491528 | tf_op jit(solution)/shard_map/ppermute | solution.py:41
  26.8 31.6 %copy-start.5 = (bf16[3,128,128]{2,1,0:T(8,128)(2,1)S(1)}, bf16[3,128,128]{2,1,0:T(8,128)(2,1)}, u32[]{:S(2)}) copy-start(bf16[3,128,128]{2,1,0:T(8,128)(2,1)} %param.9) | copy-start | bytes 294916
  26.8 17.5 %all-to-all-start = ((bf16[32,48,128]{2,1,0:T(8,128)(2,1)}), bf16[32,48,128]{2,1,0:T(8,128)(2,1)S(1)}, u32[]{:S(2)}, u32[]{:S(2)}) async-start(bf16[32,48,128]{2,1,0:T(8,128)(2,1)} %bitcast.9), calls=%async_computation | async-start | bytes 786432 | tf_op jit(solution)/shard_map/all_to_all | solution.py:33
  34.5 23.9 %collective-permute-start.4 = (bf16[2,4,160,128]{3,2,1,0:T(8,128)(2,1)}, bf16[2,4,160,128]{3,2,1,0:T(8,128)(2,1)S(1)}, u32[]{:S(2)}, u32[]{:S(2)}) collective-permute-start(bf16[2,4,160,128]{3,2,1,0:T(8,128)(2,1)} %get-tuple-element.44), channel_id=1, source_target_pairs={{8,16},{16,8},{24,32},{32,24},{40,48},{48,40},{56,64},{64,56},{72,... | collective-permute-start | bytes 983048 | tf_op jit(solution)/shard_map/ppermute | solution.py:41
  35.2 23.2 %collective-permute-start.5 = (bf16[2,4,160,128]{3,2,1,0:T(8,128)(2,1)}, bf16[2,4,160,128]{3,2,1,0:T(8,128)(2,1)}, u32[]{:S(2)}, u32[]{:S(2)}) collective-permute-start(bf16[2,4,160,128]{3,2,1,0:T(8,128)(2,1)} %get-tuple-element.45), channel_id=1, source_target_pairs={{0,8},{8,0},{16,24},{24,16},{32,40},{40,32},{48,56},{56,48},{64,72... | collective-permute-start | bytes 983048 | tf_op jit(solution)/shard_map/ppermute | solution.py:41
  45.1 27.5 %all-to-all-start.1 = ((bf16[16,48,128]{2,1,0:T(8,128)(2,1)}), bf16[16,48,128]{2,1,0:T(8,128)(2,1)S(1)}, u32[]{:S(2)}, u32[]{:S(2)}) async-start(bf16[16,48,128]{2,1,0:T(8,128)(2,1)} %share.2), calls=%async_computation.1 | async-start | bytes 393216 | tf_op jit(solution)/shard_map/all_to_all | solution.py:33
  58.4 3.3 %copy-start.7 = (bf16[4,160,128]{2,1,0:T(8,128)(2,1)S(1)}, bf16[4,160,128]{2,1,0:T(8,128)(2,1)}, u32[]{:S(2)}) copy-start(bf16[4,160,128]{2,1,0:T(8,128)(2,1)} %get-tuple-element.52) | copy-start | bytes 491524
  58.4 8.3 %copy-start.6 = (bf16[4,160,128]{2,1,0:T(8,128)(2,1)S(1)}, bf16[4,160,128]{2,1,0:T(8,128)(2,1)}, u32[]{:S(2)}) copy-start(bf16[4,160,128]{2,1,0:T(8,128)(2,1)} %get-tuple-element.53) | copy-start | bytes 491524
  58.5 18.6 %copy-start.3 = (bf16[3,3,128,128]{3,2,1,0:T(8,128)(2,1)S(1)}, bf16[3,3,128,128]{3,2,1,0:T(8,128)(2,1)}, u32[]{:S(2)}) copy-start(bf16[3,3,128,128]{3,2,1,0:T(8,128)(2,1)} %param.8) | copy-start | bytes 884740
  61.7 15.4 %copy-start.4 = (bf16[4,4,160,128]{3,2,1,0:T(8,128)(2,1)S(1)}, bf16[4,4,160,128]{3,2,1,0:T(8,128)(2,1)}, u32[]{:S(2)}) copy-start(bf16[4,4,160,128]{3,2,1,0:T(8,128)(2,1)} %get-tuple-element.50.gp) | copy-start | bytes 1966084
  61.7 10.9 %collective-permute-start.6 = (bf16[4,160,128]{2,1,0:T(8,128)(2,1)S(1)}, bf16[4,160,128]{2,1,0:T(8,128)(2,1)S(1)}, u32[]{:S(2)}, u32[]{:S(2)}) collective-permute-start(bf16[4,160,128]{2,1,0:T(8,128)(2,1)S(1)} %copy-done.7), channel_id=1, source_target_pairs={{1,2},{2,1},{3,4},{4,3},{5,6},{6,5},{9,10},{10,9},{11,12},{12,11},... | collective-permute-start | bytes 491528 | tf_op jit(solution)/shard_map/ppermute | solution.py:41
  66.7 5.9 %collective-permute-start.7 = (bf16[4,160,128]{2,1,0:T(8,128)(2,1)S(1)}, bf16[4,160,128]{2,1,0:T(8,128)(2,1)S(1)}, u32[]{:S(2)}, u32[]{:S(2)}) collective-permute-start(bf16[4,160,128]{2,1,0:T(8,128)(2,1)S(1)} %copy-done.6), channel_id=1, source_target_pairs={{0,1},{1,0},{2,3},{3,2},{4,5},{5,4},{6,7},{7,6},{8,9},{9,8},{10,11... | collective-permute-start | bytes 491528 | tf_op jit(solution)/shard_map/ppermute | solution.py:41
  73.4 13.5 %all-to-all-start.2 = ((bf16[32,48,128]{2,1,0:T(8,128)(2,1)}), bf16[32,48,128]{2,1,0:T(8,128)(2,1)S(1)}, u32[]{:S(2)}, u32[]{:S(2)}) async-start(bf16[32,48,128]{2,1,0:T(8,128)(2,1)} %share.3), calls=%async_computation.2 | async-start | bytes 786432 | tf_op jit(solution)/shard_map/all_to_all | solution.py:33

commit v7 on v6

--- a/solution.py
+++ b/solution.py
@@ -97,15 +97,14 @@
     frames, rows, width, channels = lat.shape
     line = (frames, width, channels)
     pair = (2, rows, width, channels)
-    anywhere = pl.BlockSpec(memory_space=pl.ANY)
-    return pl.pallas_call(
+    return vmem_call(
         edges_kernel,
-        out_shape=tuple(jax.ShapeDtypeStruct(s, BF16) for s in (pair, pair, line, line)),
-        in_specs=[anywhere] * 3,
-        out_specs=(pl.BlockSpec(memory_space=pltpu.VMEM),) * 4,
-        scratch_shapes=[pltpu.SemaphoreType.DMA((4,))],
-        name="edges",
-    )(held(lat), held(fwd), held(rev))
+        [(pair, BF16), (pair, BF16), (line, BF16), (line, BF16)],
+        [pltpu.SemaphoreType.DMA((4,))],
+        "edges",
+        in_hbm=3,
+        pin=True,
+    )(lat, fwd, rev)
 
 
 def beside(row):

time: 88.4 us -> 87.3 us (0.988)
  Pallas kernels: 18.5 us -> 17.5 us
    pallas_call x1 -> x0, Pallas kernels: 2.28 us -> none  [edges(): pl.pallas_call(edges_kernel, out_shape=tuple((jax.ShapeDtypeStruct(s, BF1...]
    pallas_call x7 -> x8, Pallas kernels: 16.2 us -> 17.5 us  [call(): pl.pallas_call(kernel, out_shape=tuple(((pltpu.VMEM if pin else jax.Shape...]
where the time goes in v7:
time: 87.3 us; the launch traced here: 86.6 us
  starting transfers between devices  53.7 us (62%)
  Pallas kernels  17.5 us (20%)
  waiting for transfers between devices  14.4 us (16%)
  between operations  0.91 us (1%)
    ppermute x8, starting transfers between devices, swapped(): return lax.ppermute(value, axis, pairs)  29.2 us
    all_to_all x3, starting transfers between devices, exchange(): lax.all_to_all(pieces, BOTH, 0, 0, tiled=True, axis_index_groups=members)  24.4 us
    pallas_call x8, Pallas kernels, call(): pl.pallas_call(kernel, out_shape=tuple(((pltpu.VMEM if pin else jax.Shape...  17.5 us
    all_to_all x3, waiting for transfers between devices, exchange(): lax.all_to_all(pieces, BOTH, 0, 0, tiled=True, axis_index_groups=members)  10.5 us
    ppermute x8, waiting for transfers between devices, swapped(): return lax.ppermute(value, axis, pairs)  3.98 us
  transfers between devices with their start and end apart: 11, of which 3 were waited for; matrix products, arithmetic and copies ran while one was open for 0% of the time, Pallas kernels for 12%

profile of v7, /device:TPU:1, one launch (start us, length us, event | category | flops | bytes accessed | tf_op | source)
XLA Modules:
  0.0 86.6 jit_solution(9379729131648260593)
XLA Ops:
  0.6 0.0 copy-start.1
  0.6 0.0 copy-start
  0.7 0.0 copy-start.2
  0.7 1.3 %edges.1 = (bf16[2,4,160,128]{3,2,1,0:T(8,128)(2,1)S(1)}, bf16[2,4,160,128]{3,2,1,0:T(8,128)(2,1)S(1)}, bf16[4,160,128]{2,1,0:T(8,128)(2,1)S(1)}, bf16[4,160,128]{2,1,0:T(8,128)(2,1)S(1)}) custom-call(bf16[4,4,160,128]{3,2,1,0:T(8,128)(2,1)} %lat.5, bf16[4,4,160,128]{3,2,1,0:T(8,128)(2,1)} %fwd.7, bf16[4,4,160,128]{3,2,1,0:T(8,128)(2,1)} %rev.7), custom_call_target="tpu_custom_call" | custom-call | tf_op jit(solution)/shard_map/edges/pallas_call | solution.py:52
  2.0 0.7 collective-permute-start
  2.7 6.4 %collective-permute-start.1 = (bf16[2,4,160,128]{3,2,1,0:T(8,128)(2,1)S(1)}, bf16[2,4,160,128]{3,2,1,0:T(8,128)(2,1)S(1)}, u32[]{:S(2)}, u32[]{:S(2)}) collective-permute-start(bf16[2,4,160,128]{3,2,1,0:T(8,128)(2,1)S(1)} %get-tuple-element.38), channel_id=1, source_target_pairs={{0,8},{8,0},{16,24},{24,16},{32,40},{40,32},{48,56},{56,48},{64,72... | collective-permute-start | bytes 983048 | tf_op jit(solution)/shard_map/ppermute | solution.py:41
  9.1 6.9 %collective-permute-start.2 = (bf16[4,160,128]{2,1,0:T(8,128)(2,1)S(1)}, bf16[4,160,128]{2,1,0:T(8,128)(2,1)S(1)}, u32[]{:S(2)}, u32[]{:S(2)}) collective-permute-start(bf16[4,160,128]{2,1,0:T(8,128)(2,1)S(1)} %get-tuple-element.39), channel_id=1, source_target_pairs={{1,2},{2,1},{3,4},{4,3},{5,6},{6,5},{9,10},{10,9},{11,12},{12,11},... | collective-permute-start | bytes 491528 | tf_op jit(solution)/shard_map/ppermute | solution.py:41
  16.0 1.9 %collective-permute-start.3 = (bf16[4,160,128]{2,1,0:T(8,128)(2,1)S(1)}, bf16[4,160,128]{2,1,0:T(8,128)(2,1)S(1)}, u32[]{:S(2)}, u32[]{:S(2)}) collective-permute-start(bf16[4,160,128]{2,1,0:T(8,128)(2,1)S(1)} %get-tuple-element.40), channel_id=1, source_target_pairs={{0,1},{1,0},{2,3},{3,2},{4,5},{5,4},{6,7},{7,6},{8,9},{9,8},{10,11... | collective-permute-start | bytes 491528 | tf_op jit(solution)/shard_map/ppermute | solution.py:41
  18.0 0.0 copy-done.1
  18.0 0.0 copy-done
  18.0 0.0 copy-done.2
  18.0 3.5 %prep.1 = (bf16[4,4,160,384]{3,2,1,0:T(8,128)(2,1)S(1)}, f32[2560,128]{1,0:T(8,128)S(1)}, f32[2560,128]{1,0:T(8,128)S(1)}, bf16[1152,128]{1,0:T(8,128)(2,1)S(1)}, bf16[768,128]{1,0:T(8,128)(2,1)S(1)}) custom-call(bf16[4,4,160,128]{3,2,1,0:T(8,128)(2,1)S(1)} %copy-done.2, bf16[4,4,160,128]{3,2,1,0:T(8,128)(2,1)S(1)} %copy-done, ...), custom_call_target="tpu_custom_call" | custom-call | tf_op jit(solution)/shard_map/prep/pallas_call | solution.py:52
  21.5 0.0 collective-permute-done.2.row_b
  21.5 0.0 collective-permute-done.3.row_a
  21.6 0.0 collective-permute-done.cots_b
  21.6 0.0 collective-permute-done.1.cots_a
  21.6 4.3 %front.1 = (bf16[4,4,160,128]{3,2,1,0:T(8,128)(2,1)S(1)}, bf16[4,4,160,128]{3,2,1,0:T(8,128)(2,1)}, bf16[2,4,160,128]{3,2,1,0:T(8,128)(2,1)}, bf16[2,4,160,128]{...) custom-call(bf16[4,4,160,384]{3,2,1,0:T(8,128)(2,1)S(1)} %get-tuple-ele, ...), custom_call_target="tpu_custom_call" | custom-call | tf_op jit(solution)/shard_map/front/pallas_call | solution.py:52
  25.9 0.0 copy-start.5
  25.9 7.7 %all-to-all-start = ((bf16[32,48,128]{2,1,0:T(8,128)(2,1)}), bf16[32,48,128]{2,1,0:T(8,128)(2,1)S(1)}, u32[]{:S(2)}, u32[]{:S(2)}) async-start(bf16[32,48,128]{2,1,0:T(8,128)(2,1)} %bitcast.9), calls=%async_computation | async-start | bytes 786432 | tf_op jit(solution)/shard_map/all_to_all | solution.py:33
  33.6 0.7 collective-permute-start.4
  34.3 5.7 %collective-permute-start.5 = (bf16[2,4,160,128]{3,2,1,0:T(8,128)(2,1)}, bf16[2,4,160,128]{3,2,1,0:T(8,128)(2,1)}, u32[]{:S(2)}, u32[]{:S(2)}) collective-permute-start(bf16[2,4,160,128]{3,2,1,0:T(8,128)(2,1)} %get-tuple-element.45), channel_id=1, source_target_pairs={{0,8},{8,0},{16,24},{24,16},{32,40},{40,32},{48,56},{56,48},{64,72... | collective-permute-start | bytes 983048 | tf_op jit(solution)/shard_map/ppermute | solution.py:41
  40.0 3.4 %all-to-all-done.pieces = bf16[32,48,128]{2,1,0:T(8,128)(2,1)S(1)} async-done(((bf16[32,48,128]{2,1,0:T(8,128)(2,1)}), bf16[32,48,128]{2,1,0:T(8,128)(2,1)S(1)}, u32[]{:S(2)}, u32[]{:S(2)}) %all-to-all-start) | async-done | bytes 393248 | tf_op jit(solution)/shard_map/all_to_all | solution.py:33
  43.4 0.7 share.2
  44.2 13.1 %all-to-all-start.1 = ((bf16[16,48,128]{2,1,0:T(8,128)(2,1)}), bf16[16,48,128]{2,1,0:T(8,128)(2,1)S(1)}, u32[]{:S(2)}, u32[]{:S(2)}) async-start(bf16[16,48,128]{2,1,0:T(8,128)(2,1)} %share.2), calls=%async_computation.1 | async-start | bytes 393216 | tf_op jit(solution)/shard_map/all_to_all | solution.py:33
  57.3 0.0 copy-start.7
  57.3 0.0 copy-start.6
  57.3 0.0 collective-permute-done.4.got_b
  57.3 0.0 collective-permute-done.5.got_a
  57.3 0.0 copy-done.5
  57.3 0.0 copy-start.3
  57.3 3.2 %outs.1 = (bf16[4,4,160,128]{3,2,1,0:T(8,128)(2,1)}, bf16[4,4,160,128]{3,2,1,0:T(8,128)(2,1)}) custom-call(bf16[4,4,160,128]{3,2,1,0:T(8,128)(2,1)S(1)} %copy-done.2, bf16[4,4,160,128]{3,2,1,0:T(8,128)(2,1)S(1)} %get-tuple-element.43.act, bf16[2,4,160,128]{3,2,1,0:T(8,128)(2,1)S(1)} %collective-permute-done.4.got_b, ...), custom_call_target="tpu_custom_call" | custom-call | tf_op jit(solution)/shard_map/outs/pallas_call | solution.py:52
  60.5 0.0 copy-start.4
  60.5 0.0 copy-done.7
  60.5 5.0 %collective-permute-start.6 = (bf16[4,160,128]{2,1,0:T(8,128)(2,1)S(1)}, bf16[4,160,128]{2,1,0:T(8,128)(2,1)S(1)}, u32[]{:S(2)}, u32[]{:S(2)}) collective-permute-start(bf16[4,160,128]{2,1,0:T(8,128)(2,1)S(1)} %copy-done.7), channel_id=1, source_target_pairs={{1,2},{2,1},{3,4},{4,3},{5,6},{6,5},{9,10},{10,9},{11,12},{12,11},... | collective-permute-start | bytes 491528 | tf_op jit(solution)/shard_map/ppermute | solution.py:41
  65.5 0.0 copy-done.6
  65.6 1.9 %collective-permute-start.7 = (bf16[4,160,128]{2,1,0:T(8,128)(2,1)S(1)}, bf16[4,160,128]{2,1,0:T(8,128)(2,1)S(1)}, u32[]{:S(2)}, u32[]{:S(2)}) collective-permute-start(bf16[4,160,128]{2,1,0:T(8,128)(2,1)S(1)} %copy-done.6), channel_id=1, source_target_pairs={{0,1},{1,0},{2,3},{3,2},{4,5},{5,4},{6,7},{7,6},{8,9},{9,8},{10,11... | collective-permute-start | bytes 491528 | tf_op jit(solution)/shard_map/ppermute | solution.py:41
  67.5 4.0 %collective-permute-done.6.got_b = bf16[4,160,128]{2,1,0:T(8,128)(2,1)S(1)} collective-permute-done((bf16[4,160,128]{2,1,0:T(8,128)(2,1)S(1)}, bf16[4,160,128]{2,1,0:T(8,128)(2,1)S(1)}, u32[]{:S(2)}, u32[]{:S(2)}) %collective-permute-start.6) | collective-permute-done | bytes 163872 | tf_op jit(solution)/shard_map/ppermute | solution.py:41
  71.4 0.0 collective-permute-done.7.got_a
  71.4 0.0 all-to-all-done.1.pieces
  71.5 0.8 share.3
  72.2 3.7 %all-to-all-start.2 = ((bf16[32,48,128]{2,1,0:T(8,128)(2,1)}), bf16[32,48,128]{2,1,0:T(8,128)(2,1)S(1)}, u32[]{:S(2)}, u32[]{:S(2)}) async-start(bf16[32,48,128]{2,1,0:T(8,128)(2,1)} %share.3), calls=%async_computation.2 | async-start | bytes 786432 | tf_op jit(solution)/shard_map/all_to_all | solution.py:33
  75.9 0.0 copy-done.3
  75.9 0.0 copy-done.4
  75.9 2.7 %grad_input.1 = bf16[4,4,160,128]{3,2,1,0:T(8,128)(2,1)} custom-call(bf16[4,4,160,128]{3,2,1,0:T(8,128)(2,1)S(1)} %copy-done.4, bf16[4,160,128]{2,1,0:T(8,128)(2,1)S(1)} %collective-permute-done.6.got_b, bf16[4,160,128]{2,1,0:T(8,128)(2,1)S(1)} %collective-permute-done.7.got_a, bf16[4,4,160,128]{3,2,1,0:T(8,128)(2,1)S(1)} %copy-done, ...), custom_call_target="tpu_custom_call" | custom-call | tf_op jit(solution)/shard_map/grad_input/pallas_call | solution.py:52
  78.7 7.0 %all-to-all-done.2.pieces = bf16[32,48,128]{2,1,0:T(8,128)(2,1)S(1)} async-done(((bf16[32,48,128]{2,1,0:T(8,128)(2,1)}), bf16[32,48,128]{2,1,0:T(8,128)(2,1)S(1)}, u32[]{:S(2)}, u32[]{:S(2)}) %all-to-all-start.2) | async-done | bytes 393248 | tf_op jit(solution)/shard_map/all_to_all | solution.py:33
  85.7 0.9 %widen.1 = (f32[1152,128]{1,0:T(8,128)}, f32[384,128]{1,0:T(8,128)}) custom-call(bf16[32,48,128]{2,1,0:T(8,128)(2,1)S(1)} %all-to-all-done.2.pieces), custom_call_target="tpu_custom_call" | custom-call | tf_op jit(solution)/shard_map/widen/pallas_call | solution.py:52
Async XLA Ops:
  0.6 17.3 %copy-start.1 = (bf16[4,4,160,128]{3,2,1,0:T(8,128)(2,1)S(1)}, bf16[4,4,160,128]{3,2,1,0:T(8,128)(2,1)}, u32[]{:S(2)}) copy-start(bf16[4,4,160,128]{3,2,1,0:T(8,128)(2,1)} %rev.7) | copy-start | bytes 1966084
  0.6 17.3 %copy-start = (bf16[4,4,160,128]{3,2,1,0:T(8,128)(2,1)S(1)}, bf16[4,4,160,128]{3,2,1,0:T(8,128)(2,1)}, u32[]{:S(2)}) copy-start(bf16[4,4,160,128]{3,2,1,0:T(8,128)(2,1)} %fwd.7) | copy-start | bytes 1966084
  0.7 17.3 %copy-start.2 = (bf16[4,4,160,128]{3,2,1,0:T(8,128)(2,1)S(1)}, bf16[4,4,160,128]{3,2,1,0:T(8,128)(2,1)}, u32[]{:S(2)}) copy-start(bf16[4,4,160,128]{3,2,1,0:T(8,128)(2,1)} %lat.5) | copy-start | bytes 1966084
  2.0 19.5 %collective-permute-start = (bf16[2,4,160,128]{3,2,1,0:T(8,128)(2,1)S(1)}, bf16[2,4,160,128]{3,2,1,0:T(8,128)(2,1)S(1)}, u32[]{:S(2)}, u32[]{:S(2)}) collective-permute-start(bf16[2,4,160,128]{3,2,1,0:T(8,128)(2,1)S(1)} %get-tuple-element.37), channel_id=1, source_target_pairs={{8,16},{16,8},{24,32},{32,24},{40,48},{48,40},{56,64},{64,56},{72,... | collective-permute-start | bytes 983048 | tf_op jit(solution)/shard_map/ppermute | solution.py:41
  2.7 18.9 %collective-permute-start.1 = (bf16[2,4,160,128]{3,2,1,0:T(8,128)(2,1)S(1)}, bf16[2,4,160,128]{3,2,1,0:T(8,128)(2,1)S(1)}, u32[]{:S(2)}, u32[]{:S(2)}) collective-permute-start(bf16[2,4,160,128]{3,2,1,0:T(8,128)(2,1)S(1)} %get-tuple-element.38), channel_id=1, source_target_pairs={{0,8},{8,0},{16,24},{24,16},{32,40},{40,32},{48,56},{56,48},{64,72... | collective-permute-start | bytes 983048 | tf_op jit(solution)/shard_map/ppermute | solution.py:41
  9.1 12.4 %collective-permute-start.2 = (bf16[4,160,128]{2,1,0:T(8,128)(2,1)S(1)}, bf16[4,160,128]{2,1,0:T(8,128)(2,1)S(1)}, u32[]{:S(2)}, u32[]{:S(2)}) collective-permute-start(bf16[4,160,128]{2,1,0:T(8,128)(2,1)S(1)} %get-tuple-element.39), channel_id=1, source_target_pairs={{1,2},{2,1},{3,4},{4,3},{5,6},{6,5},{9,10},{10,9},{11,12},{12,11},... | collective-permute-start | bytes 491528 | tf_op jit(solution)/shard_map/ppermute | solution.py:41
  16.0 5.5 %collective-permute-start.3 = (bf16[4,160,128]{2,1,0:T(8,128)(2,1)S(1)}, bf16[4,160,128]{2,1,0:T(8,128)(2,1)S(1)}, u32[]{:S(2)}, u32[]{:S(2)}) collective-permute-start(bf16[4,160,128]{2,1,0:T(8,128)(2,1)S(1)} %get-tuple-element.40), channel_id=1, source_target_pairs={{0,1},{1,0},{2,3},{3,2},{4,5},{5,4},{6,7},{7,6},{8,9},{9,8},{10,11... | collective-permute-start | bytes 491528 | tf_op jit(solution)/shard_map/ppermute | solution.py:41
  25.9 31.4 %copy-start.5 = (bf16[3,128,128]{2,1,0:T(8,128)(2,1)S(1)}, bf16[3,128,128]{2,1,0:T(8,128)(2,1)}, u32[]{:S(2)}) copy-start(bf16[3,128,128]{2,1,0:T(8,128)(2,1)} %param.9) | copy-start | bytes 294916
  25.9 17.5 %all-to-all-start = ((bf16[32,48,128]{2,1,0:T(8,128)(2,1)}), bf16[32,48,128]{2,1,0:T(8,128)(2,1)S(1)}, u32[]{:S(2)}, u32[]{:S(2)}) async-start(bf16[32,48,128]{2,1,0:T(8,128)(2,1)} %bitcast.9), calls=%async_computation | async-start | bytes 786432 | tf_op jit(solution)/shard_map/all_to_all | solution.py:33
  33.6 23.7 %collective-permute-start.4 = (bf16[2,4,160,128]{3,2,1,0:T(8,128)(2,1)}, bf16[2,4,160,128]{3,2,1,0:T(8,128)(2,1)S(1)}, u32[]{:S(2)}, u32[]{:S(2)}) collective-permute-start(bf16[2,4,160,128]{3,2,1,0:T(8,128)(2,1)} %get-tuple-element.44), channel_id=1, source_target_pairs={{8,16},{16,8},{24,32},{32,24},{40,48},{48,40},{56,64},{64,56},{72,... | collective-permute-start | bytes 983048 | tf_op jit(solution)/shard_map/ppermute | solution.py:41
  34.3 23.0 %collective-permute-start.5 = (bf16[2,4,160,128]{3,2,1,0:T(8,128)(2,1)}, bf16[2,4,160,128]{3,2,1,0:T(8,128)(2,1)}, u32[]{:S(2)}, u32[]{:S(2)}) collective-permute-start(bf16[2,4,160,128]{3,2,1,0:T(8,128)(2,1)} %get-tuple-element.45), channel_id=1, source_target_pairs={{0,8},{8,0},{16,24},{24,16},{32,40},{40,32},{48,56},{56,48},{64,72... | collective-permute-start | bytes 983048 | tf_op jit(solution)/shard_map/ppermute | solution.py:41
  44.2 27.3 %all-to-all-start.1 = ((bf16[16,48,128]{2,1,0:T(8,128)(2,1)}), bf16[16,48,128]{2,1,0:T(8,128)(2,1)S(1)}, u32[]{:S(2)}, u32[]{:S(2)}) async-start(bf16[16,48,128]{2,1,0:T(8,128)(2,1)} %share.2), calls=%async_computation.1 | async-start | bytes 393216 | tf_op jit(solution)/shard_map/all_to_all | solution.py:33
  57.3 3.3 %copy-start.7 = (bf16[4,160,128]{2,1,0:T(8,128)(2,1)S(1)}, bf16[4,160,128]{2,1,0:T(8,128)(2,1)}, u32[]{:S(2)}) copy-start(bf16[4,160,128]{2,1,0:T(8,128)(2,1)} %get-tuple-element.52) | copy-start | bytes 491524
  57.3 8.3 %copy-start.6 = (bf16[4,160,128]{2,1,0:T(8,128)(2,1)S(1)}, bf16[4,160,128]{2,1,0:T(8,128)(2,1)}, u32[]{:S(2)}) copy-start(bf16[4,160,128]{2,1,0:T(8,128)(2,1)} %get-tuple-element.53) | copy-start | bytes 491524
  57.3 18.6 %copy-start.3 = (bf16[3,3,128,128]{3,2,1,0:T(8,128)(2,1)S(1)}, bf16[3,3,128,128]{3,2,1,0:T(8,128)(2,1)}, u32[]{:S(2)}) copy-start(bf16[3,3,128,128]{3,2,1,0:T(8,128)(2,1)} %param.8) | copy-start | bytes 884740
  60.5 15.4 %copy-start.4 = (bf16[4,4,160,128]{3,2,1,0:T(8,128)(2,1)S(1)}, bf16[4,4,160,128]{3,2,1,0:T(8,128)(2,1)}, u32[]{:S(2)}) copy-start(bf16[4,4,160,128]{3,2,1,0:T(8,128)(2,1)} %get-tuple-element.50.gp) | copy-start | bytes 1966084
  60.5 10.9 %collective-permute-start.6 = (bf16[4,160,128]{2,1,0:T(8,128)(2,1)S(1)}, bf16[4,160,128]{2,1,0:T(8,128)(2,1)S(1)}, u32[]{:S(2)}, u32[]{:S(2)}) collective-permute-start(bf16[4,160,128]{2,1,0:T(8,128)(2,1)S(1)} %copy-done.7), channel_id=1, source_target_pairs={{1,2},{2,1},{3,4},{4,3},{5,6},{6,5},{9,10},{10,9},{11,12},{12,11},... | collective-permute-start | bytes 491528 | tf_op jit(solution)/shard_map/ppermute | solution.py:41
  65.6 5.9 %collective-permute-start.7 = (bf16[4,160,128]{2,1,0:T(8,128)(2,1)S(1)}, bf16[4,160,128]{2,1,0:T(8,128)(2,1)S(1)}, u32[]{:S(2)}, u32[]{:S(2)}) collective-permute-start(bf16[4,160,128]{2,1,0:T(8,128)(2,1)S(1)} %copy-done.6), channel_id=1, source_target_pairs={{0,1},{1,0},{2,3},{3,2},{4,5},{5,4},{6,7},{7,6},{8,9},{9,8},{10,11... | collective-permute-start | bytes 491528 | tf_op jit(solution)/shard_map/ppermute | solution.py:41
  72.2 13.5 %all-to-all-start.2 = ((bf16[32,48,128]{2,1,0:T(8,128)(2,1)}), bf16[32,48,128]{2,1,0:T(8,128)(2,1)S(1)}, u32[]{:S(2)}, u32[]{:S(2)}) async-start(bf16[32,48,128]{2,1,0:T(8,128)(2,1)} %share.3), calls=%async_computation.2 | async-start | bytes 786432 | tf_op jit(solution)/shard_map/all_to_all | solution.py:33
